TPU v7x, 32 devices: a whole 2x2x4 slice. The times are simulated.
32 devices in a mesh: rows: 8 (over z, y), feat: 4 (over x, core).
Axes of the slice: x: 2, y: 2, z: 4, core: 2. Of those that a mesh axis runs over, the one named last changes fastest.
Arguments:
- gradients: bfloat16 [4096, 128], P('rows'), may hold values from -6 to 6
- hessians: bfloat16 [4096], P('rows'), may hold values from 0.25 to 2
- bin_words: int32 [128, 4096], P('feat', 'rows'), may hold values from 0 to 4095, as said below
- children: int32 [3, 4096], P(None, 'rows'), may hold values from 0 to 1, as said below
- split_feature: int32 [14], replicated, may hold values from 0 to 255
- split_bin: int32 [14], replicated, may hold values from 0 to 62
Outputs:
- split_gain_one: float32 [128, 256], P('rows', 'feat')
- split_gain_two: float32 [256, 256], P('rows', 'feat')
- split_gain_three: float32 [512, 256], P('rows', 'feat')
- child_scores: float32 [3, 8, 2, 128], P(None, 'rows')
Inputs may be any that keep to these rules, and one draw needn't show every extreme that they name: `children`: of the 512 rows of one device, at most 3 / 4, 1 / 2 and 1 / 4 of 512 lie in one node at depths 1, 2 and 3; every device reaches each of these bounds in some node. `bin_words`: word w of panel p, six bits a feature with the lowest bits first, holds the bins of the panel's features 2 w and 2 w + 1, numbered within the panel of 64 features; slots past the panel's last feature are zero. Every bin is below 64.
All inputs are finite; a program needn't handle non-finite values.
Results may differ from a plain program's by a relative error of at most 0.0003.
Values may be sent and summed in bfloat16 or wider, within the bound.
No kernel may reach another device: no remote copies, remote signals or barrier semaphores. Data moves between devices by JAX's collectives and lax.ppermute only.
A program may use at most 64 MiB of HBM per device.

v0:
```python
import jax
import jax.numpy as jnp
from jax import lax
from jax.sharding import PartitionSpec as P

FEATURES = 256
BINS = 64
OUT = 128
LEVELS = 3


penalty = 1.0


def as_sent(array):
    return jax.tree.map(lambda a: a.astype(jnp.bfloat16) if a.dtype == jnp.float32 else a, array)


def swapped(block, axis, stride):
    count = lax.axis_size(axis)
    route = []
    for low in range(count):
        high = low | 1 << stride
        if high != low and high < count:
            route += [(low, high), (high, low)]
    return lax.ppermute(block, axis, route)


def unpack_codes(packed):
    shifts = 6 * jnp.arange(2, dtype=jnp.int32)
    pieces = jnp.bitwise_and(jnp.right_shift(packed[:, None, :], shifts[None, :, None]), 63)
    return pieces.reshape(-1, packed.shape[-1])


def split_terms(cumulative, hess_cum):
    total_sum = cumulative[..., -1:, :]
    hess_total = hess_cum[..., -1:]
    right_sum = total_sum - cumulative
    hess_right = hess_total - hess_cum
    split_score = (
        jnp.sum(cumulative * cumulative, -1) / (hess_cum + penalty)
        + jnp.sum(right_sum * right_sum, -1) / (hess_right + penalty)
        - jnp.sum(total_sum * total_sum, -1) / (hess_total + penalty)
    ) / OUT
    return (split_score, right_sum, hess_right)


def front_index(marked, slot_total):
    running = jnp.cumsum(marked.astype(jnp.int32))
    wanted = jnp.arange(slot_total, dtype=jnp.int32) + 1
    source = jnp.searchsorted(running, wanted, side="left")
    filled = wanted <= running[-1]
    return (jnp.minimum(source, marked.shape[0] - 1), filled)


def pick_rows(values, source, filled):
    taken = jnp.take(values, source, axis=0)
    return jnp.where(filled[:, None], taken, jnp.zeros_like(taken))


def pick_slots(values, source, filled):
    taken = jnp.take(values, source, axis=0)
    return jnp.where(filled, taken, jnp.zeros_like(taken))


def pick_columns(values, source, filled):
    taken = jnp.take(values, source, axis=1)
    return jnp.where(filled[None, :], taken, jnp.zeros_like(taken))


def build_hist(bin_codes, grad_rows, hess_rows, block_rows):
    feat_count = bin_codes.shape[0]
    bin_levels = jnp.arange(BINS, dtype=jnp.int32)

    def add_block(step_index, running):
        start_row = step_index * block_rows
        code_block = lax.dynamic_slice_in_dim(bin_codes, start_row, block_rows, 1)
        grad_block = lax.dynamic_slice_in_dim(grad_rows, start_row, block_rows, 0)
        hess_block = lax.dynamic_slice_in_dim(hess_rows, start_row, block_rows, 0)
        one_hot = (code_block[:, None, :] == bin_levels[None, :, None]).astype(jnp.bfloat16)
        one_hot = one_hot.reshape(feat_count * BINS, block_rows)
        return (
            running[0] + jnp.dot(one_hot, grad_block, preferred_element_type=jnp.float32),
            running[1] + jnp.dot(one_hot, hess_block, preferred_element_type=jnp.float32),
        )

    initial = (
        jnp.zeros((feat_count * BINS, OUT), jnp.float32),
        jnp.zeros((feat_count * BINS,), jnp.float32),
    )
    return lax.fori_loop(0, grad_rows.shape[0] // block_rows, add_block, initial)


def on_device(gradients, hessians, bin_words, children, split_feature, split_bin):
    row_count = lax.axis_size("rows")
    top_bit = row_count.bit_length() - 1
    row_index = lax.axis_index("rows")
    panel_index = lax.axis_index("feat")
    feat_dev = FEATURES // lax.axis_size("feat")
    row_dev = gradients.shape[0]
    slot_count = 2 * row_dev
    block_rows = min(256, slot_count)
    pad_rows = slot_count - row_dev
    grad_rows = jnp.concatenate([gradients, jnp.zeros((pad_rows, OUT), jnp.bfloat16)], 0)
    hess_rows = jnp.concatenate([hessians, jnp.zeros((pad_rows,), jnp.bfloat16)], 0)
    word_rows = jnp.concatenate(
        [bin_words, jnp.zeros((bin_words.shape[0], pad_rows), jnp.int32)], 1
    )
    child_rows = jnp.concatenate([children, jnp.zeros((children.shape[0], pad_rows), jnp.int32)], 1)
    splits_total = split_feature.shape[0]
    collected = jnp.zeros((splits_total, 2, OUT), jnp.float32)
    gain_list = []
    slot_list = []
    for level_index in range(LEVELS):
        cross_bit = top_bit - 1 - level_index
        half_bit = jnp.bitwise_and(jnp.right_shift(row_index, cross_bit), 1)
        living = hess_rows > 0
        staying = living & (child_rows[level_index] == half_bit)
        leaving = living & (child_rows[level_index] != half_bit)
        sent_hess = jnp.where(leaving, hess_rows, jnp.zeros_like(hess_rows))
        got_grad, got_hess, got_words, got_child = (
            swapped(grad_rows, "rows", cross_bit),
            swapped(sent_hess, "rows", cross_bit),
            swapped(as_sent(word_rows), "rows", cross_bit).astype(word_rows.dtype),
            swapped(as_sent(child_rows), "rows", cross_bit).astype(child_rows.dtype),
        )
        accepted = jnp.concatenate([staying, got_hess > 0])
        source, filled = front_index(accepted, slot_count)
        grad_rows = pick_rows(jnp.concatenate([grad_rows, got_grad], 0), source, filled)
        hess_rows = pick_slots(jnp.concatenate([hess_rows, got_hess], 0), source, filled)
        word_rows = pick_columns(jnp.concatenate([word_rows, got_words], 1), source, filled)
        child_rows = pick_columns(jnp.concatenate([child_rows, got_child], 1), source, filled)
        bin_codes = unpack_codes(word_rows)
        hist_grad, hist_hess = build_hist(bin_codes, grad_rows, hess_rows, block_rows)
        group_size = row_count >> level_index + 1
        node_count = 2 ** (level_index + 1)
        node_here = jnp.right_shift(row_index, top_bit - level_index - 1)
        share_grad = hist_grad.reshape(feat_dev, BINS * OUT)
        share_hess = hist_hess.reshape(feat_dev, BINS)
        for step_bit in reversed(range(top_bit - level_index - 1)):
            half_rows = share_grad.shape[0] // 2
            upper_half = jnp.bitwise_and(jnp.right_shift(row_index, step_bit), 1) == 1
            keep_grad = jnp.where(upper_half, share_grad[half_rows:], share_grad[:half_rows])
            give_grad = jnp.where(upper_half, share_grad[:half_rows], share_grad[half_rows:])
            keep_hess = jnp.where(upper_half, share_hess[half_rows:], share_hess[:half_rows])
            give_hess = jnp.where(upper_half, share_hess[:half_rows], share_hess[half_rows:])
            got_partial, got_curv = swapped((give_grad, give_hess), "rows", step_bit)
            share_grad = keep_grad + got_partial
            share_hess = keep_hess + got_curv
        share_count = share_grad.shape[0]
        cumulative = jnp.cumsum(share_grad.reshape(share_count, BINS, OUT), axis=1)
        hess_cum = jnp.cumsum(share_hess, axis=1)
        split_score, right_sum, hess_right = split_terms(cumulative, hess_cum)
        gain_list.append(split_score)
        position = jnp.bitwise_and(row_index, group_size - 1)
        split_slot = node_count - 2 + node_here
        feature_id = split_feature[split_slot]
        bin_id = split_bin[split_slot]
        inner_feature = feature_id % feat_dev
        is_owner = (feature_id // feat_dev == panel_index) & (
            inner_feature // share_count == position
        )
        chosen = (
            (jnp.arange(share_count)[:, None] == inner_feature % share_count)
            & (jnp.arange(BINS)[None, :] == bin_id)
            & is_owner
        )
        left_grad = jnp.sum(jnp.where(chosen[..., None], cumulative, 0.0), axis=(0, 1))
        left_hess = jnp.sum(jnp.where(chosen, hess_cum, 0.0))
        right_grad = jnp.sum(jnp.where(chosen[..., None], right_sum, 0.0), axis=(0, 1))
        right_hess = jnp.sum(jnp.where(chosen, hess_right, 0.0))
        child_pair = jnp.stack(
            [
                -left_grad / jnp.sqrt(left_hess + penalty),
                -right_grad / jnp.sqrt(right_hess + penalty),
            ],
            0,
        )
        slot_match = jnp.arange(splits_total) == split_slot
        collected = collected + jnp.where(slot_match[:, None, None], child_pair[None], 0.0)
        slot_list.append(split_slot)
    totals = lax.psum(collected, ("rows", "feat"))
    child_scores = jnp.stack([totals[slot_index] for slot_index in slot_list], 0)[:, None]
    return (gain_list[0], gain_list[1], gain_list[2], child_scores)


def solution(mesh):
    placed = (P("rows", None), P("rows"), P("feat", "rows"), P(None, "rows"), P(), P())
    return jax.shard_map(
        on_device,
        mesh=mesh,
        in_specs=placed,
        out_specs=(
            P("rows", "feat"),
            P("rows", "feat"),
            P("rows", "feat"),
            P(None, "rows", None, None),
        ),
        check_vma=False,
    )
```

profile of v0, /device:TPU:0, one launch (start us, length us, event | category | flops | bytes accessed | tf_op | source)
XLA Modules:
  0.0 483.5 jit_solution(8364313952394002553)
XLA Ops:
  25.9 74.8 %while.98 = (s32[]{:T(128)}, u32[1024]{0:T(1024)S(1)}, u32[1024]{0:T(1024)S(1)}, s32[2048]{0:T(1024)S(1)}, s32[]{:T(128)}, /*index=5*/s32[]{:T(128)}, s32[]{}) while((s32[]{:T(128)}, u32[1024]{0:T(1024)S(1)}, u32[1024]{0:T(1024)S(1)}, s32[2048]{0:T(1024)S(1)}, s32[]{:T(128)}, /*index=5*/s32[]{:T(128)}, s32[]{}) %tuple.221), condition=%wide.region_3.4_spmd.clone, body=%wide.region_2.3_spmd.clone.sunk | while | flops 20484 | bytes 63597 | solution.py:51
  25.9 6.2 %gather_fusion = s32[1024]{0:T(1024)S(1)} fusion(s32[2048]{0:T(1024)S(1)} %get-tuple-element.1042, u32[1024]{0:T(1024)S(1)} %broadcast_clamp_fusion.6), kind=kCustom, calls=%fused_computation.clone.clone.1 | custom fusion | bytes 12288 | tf_op jit(solution)/shard_map/jit(searchsorted)/jit(_searchsorted_scan_impl)/vmap(jit(_searchsorted_scan_impl))/while/body/eval_jaxpr/gather | solution.py:51
  32.1 6.2 %gather_fusion = s32[1024]{0:T(1024)S(1)} fusion(s32[2048]{0:T(1024)S(1)} %get-tuple-element.1042, u32[1024]{0:T(1024)S(1)} %broadcast_clamp_fusion.6), kind=kCustom, calls=%fused_computation.clone.clone.1 | custom fusion | bytes 12288 | tf_op jit(solution)/shard_map/jit(searchsorted)/jit(_searchsorted_scan_impl)/vmap(jit(_searchsorted_scan_impl))/while/body/eval_jaxpr/gather | solution.py:51
  38.3 6.2 %gather_fusion = s32[1024]{0:T(1024)S(1)} fusion(s32[2048]{0:T(1024)S(1)} %get-tuple-element.1042, u32[1024]{0:T(1024)S(1)} %broadcast_clamp_fusion.6), kind=kCustom, calls=%fused_computation.clone.clone.1 | custom fusion | bytes 12288 | tf_op jit(solution)/shard_map/jit(searchsorted)/jit(_searchsorted_scan_impl)/vmap(jit(_searchsorted_scan_impl))/while/body/eval_jaxpr/gather | solution.py:51
  44.6 6.2 %gather_fusion = s32[1024]{0:T(1024)S(1)} fusion(s32[2048]{0:T(1024)S(1)} %get-tuple-element.1042, u32[1024]{0:T(1024)S(1)} %broadcast_clamp_fusion.6), kind=kCustom, calls=%fused_computation.clone.clone.1 | custom fusion | bytes 12288 | tf_op jit(solution)/shard_map/jit(searchsorted)/jit(_searchsorted_scan_impl)/vmap(jit(_searchsorted_scan_impl))/while/body/eval_jaxpr/gather | solution.py:51
  50.8 6.2 %gather_fusion = s32[1024]{0:T(1024)S(1)} fusion(s32[2048]{0:T(1024)S(1)} %get-tuple-element.1042, u32[1024]{0:T(1024)S(1)} %broadcast_clamp_fusion.6), kind=kCustom, calls=%fused_computation.clone.clone.1 | custom fusion | bytes 12288 | tf_op jit(solution)/shard_map/jit(searchsorted)/jit(_searchsorted_scan_impl)/vmap(jit(_searchsorted_scan_impl))/while/body/eval_jaxpr/gather | solution.py:51
  57.0 6.2 %gather_fusion = s32[1024]{0:T(1024)S(1)} fusion(s32[2048]{0:T(1024)S(1)} %get-tuple-element.1042, u32[1024]{0:T(1024)S(1)} %broadcast_clamp_fusion.6), kind=kCustom, calls=%fused_computation.clone.clone.1 | custom fusion | bytes 12288 | tf_op jit(solution)/shard_map/jit(searchsorted)/jit(_searchsorted_scan_impl)/vmap(jit(_searchsorted_scan_impl))/while/body/eval_jaxpr/gather | solution.py:51
  63.3 6.2 %gather_fusion = s32[1024]{0:T(1024)S(1)} fusion(s32[2048]{0:T(1024)S(1)} %get-tuple-element.1042, u32[1024]{0:T(1024)S(1)} %broadcast_clamp_fusion.6), kind=kCustom, calls=%fused_computation.clone.clone.1 | custom fusion | bytes 12288 | tf_op jit(solution)/shard_map/jit(searchsorted)/jit(_searchsorted_scan_impl)/vmap(jit(_searchsorted_scan_impl))/while/body/eval_jaxpr/gather | solution.py:51
  69.5 6.2 %gather_fusion = s32[1024]{0:T(1024)S(1)} fusion(s32[2048]{0:T(1024)S(1)} %get-tuple-element.1042, u32[1024]{0:T(1024)S(1)} %broadcast_clamp_fusion.6), kind=kCustom, calls=%fused_computation.clone.clone.1 | custom fusion | bytes 12288 | tf_op jit(solution)/shard_map/jit(searchsorted)/jit(_searchsorted_scan_impl)/vmap(jit(_searchsorted_scan_impl))/while/body/eval_jaxpr/gather | solution.py:51
  75.8 6.2 %gather_fusion = s32[1024]{0:T(1024)S(1)} fusion(s32[2048]{0:T(1024)S(1)} %get-tuple-element.1042, u32[1024]{0:T(1024)S(1)} %broadcast_clamp_fusion.6), kind=kCustom, calls=%fused_computation.clone.clone.1 | custom fusion | bytes 12288 | tf_op jit(solution)/shard_map/jit(searchsorted)/jit(_searchsorted_scan_impl)/vmap(jit(_searchsorted_scan_impl))/while/body/eval_jaxpr/gather | solution.py:51
  82.0 6.2 %gather_fusion = s32[1024]{0:T(1024)S(1)} fusion(s32[2048]{0:T(1024)S(1)} %get-tuple-element.1042, u32[1024]{0:T(1024)S(1)} %broadcast_clamp_fusion.6), kind=kCustom, calls=%fused_computation.clone.clone.1 | custom fusion | bytes 12288 | tf_op jit(solution)/shard_map/jit(searchsorted)/jit(_searchsorted_scan_impl)/vmap(jit(_searchsorted_scan_impl))/while/body/eval_jaxpr/gather | solution.py:51
  88.2 6.2 %gather_fusion = s32[1024]{0:T(1024)S(1)} fusion(s32[2048]{0:T(1024)S(1)} %get-tuple-element.1042, u32[1024]{0:T(1024)S(1)} %broadcast_clamp_fusion.6), kind=kCustom, calls=%fused_computation.clone.clone.1 | custom fusion | bytes 12288 | tf_op jit(solution)/shard_map/jit(searchsorted)/jit(_searchsorted_scan_impl)/vmap(jit(_searchsorted_scan_impl))/while/body/eval_jaxpr/gather | solution.py:51
  101.4 6.8 %gather_fusion.5 = bf16[1024]{0:T(1024)(128)(2,1)S(1)} fusion(bf16[2048]{0:T(1024)(128)(2,1)S(1)} %get-tuple-element.809, s32[1024]{0:T(1024)S(1)} %fusion.32), kind=kCustom, calls=%fused_computation.3.clone | custom fusion | bytes 8192 | tf_op jit(solution)/shard_map/jit(_take)/gather | solution.py:62
  117.2 74.8 %while.100 = (s32[]{:T(128)}, u32[1024]{0:T(1024)S(1)}, u32[1024]{0:T(1024)S(1)}, s32[2048]{0:T(1024)S(1)}, s32[]{:T(128)}, /*index=5*/s32[]{:T(128)}, s32[]{}) while((s32[]{:T(128)}, u32[1024]{0:T(1024)S(1)}, u32[1024]{0:T(1024)S(1)}, s32[2048]{0:T(1024)S(1)}, s32[]{:T(128)}, /*index=5*/s32[]{:T(128)}, s32[]{}) %tuple.224), condition=%wide.region_14.19_spmd.clone, body=%wide.region_13.18_spmd.clone.sunk | while | flops 20484 | bytes 63597 | solution.py:51
  123.5 6.2 %gather_fusion.1 = s32[1024]{0:T(1024)S(1)} fusion(s32[2048]{0:T(1024)S(1)} %get-tuple-element.1063, u32[1024]{0:T(1024)S(1)} %broadcast_clamp_fusion.7), kind=kCustom, calls=%fused_computation.5.clone.clone.1 | custom fusion | bytes 12288 | tf_op jit(solution)/shard_map/jit(searchsorted)/jit(_searchsorted_scan_impl)/vmap(jit(_searchsorted_scan_impl))/while/body/eval_jaxpr/gather | solution.py:51
  129.7 6.2 %gather_fusion.1 = s32[1024]{0:T(1024)S(1)} fusion(s32[2048]{0:T(1024)S(1)} %get-tuple-element.1063, u32[1024]{0:T(1024)S(1)} %broadcast_clamp_fusion.7), kind=kCustom, calls=%fused_computation.5.clone.clone.1 | custom fusion | bytes 12288 | tf_op jit(solution)/shard_map/jit(searchsorted)/jit(_searchsorted_scan_impl)/vmap(jit(_searchsorted_scan_impl))/while/body/eval_jaxpr/gather | solution.py:51
  135.9 6.2 %gather_fusion.1 = s32[1024]{0:T(1024)S(1)} fusion(s32[2048]{0:T(1024)S(1)} %get-tuple-element.1063, u32[1024]{0:T(1024)S(1)} %broadcast_clamp_fusion.7), kind=kCustom, calls=%fused_computation.5.clone.clone.1 | custom fusion | bytes 12288 | tf_op jit(solution)/shard_map/jit(searchsorted)/jit(_searchsorted_scan_impl)/vmap(jit(_searchsorted_scan_impl))/while/body/eval_jaxpr/gather | solution.py:51
  142.2 6.2 %gather_fusion.1 = s32[1024]{0:T(1024)S(1)} fusion(s32[2048]{0:T(1024)S(1)} %get-tuple-element.1063, u32[1024]{0:T(1024)S(1)} %broadcast_clamp_fusion.7), kind=kCustom, calls=%fused_computation.5.clone.clone.1 | custom fusion | bytes 12288 | tf_op jit(solution)/shard_map/jit(searchsorted)/jit(_searchsorted_scan_impl)/vmap(jit(_searchsorted_scan_impl))/while/body/eval_jaxpr/gather | solution.py:51
  148.4 6.2 %gather_fusion.1 = s32[1024]{0:T(1024)S(1)} fusion(s32[2048]{0:T(1024)S(1)} %get-tuple-element.1063, u32[1024]{0:T(1024)S(1)} %broadcast_clamp_fusion.7), kind=kCustom, calls=%fused_computation.5.clone.clone.1 | custom fusion | bytes 12288 | tf_op jit(solution)/shard_map/jit(searchsorted)/jit(_searchsorted_scan_impl)/vmap(jit(_searchsorted_scan_impl))/while/body/eval_jaxpr/gather | solution.py:51
  154.7 6.2 %gather_fusion.1 = s32[1024]{0:T(1024)S(1)} fusion(s32[2048]{0:T(1024)S(1)} %get-tuple-element.1063, u32[1024]{0:T(1024)S(1)} %broadcast_clamp_fusion.7), kind=kCustom, calls=%fused_computation.5.clone.clone.1 | custom fusion | bytes 12288 | tf_op jit(solution)/shard_map/jit(searchsorted)/jit(_searchsorted_scan_impl)/vmap(jit(_searchsorted_scan_impl))/while/body/eval_jaxpr/gather | solution.py:51
  160.9 6.2 %gather_fusion.1 = s32[1024]{0:T(1024)S(1)} fusion(s32[2048]{0:T(1024)S(1)} %get-tuple-element.1063, u32[1024]{0:T(1024)S(1)} %broadcast_clamp_fusion.7), kind=kCustom, calls=%fused_computation.5.clone.clone.1 | custom fusion | bytes 12288 | tf_op jit(solution)/shard_map/jit(searchsorted)/jit(_searchsorted_scan_impl)/vmap(jit(_searchsorted_scan_impl))/while/body/eval_jaxpr/gather | solution.py:51
  167.1 6.2 %gather_fusion.1 = s32[1024]{0:T(1024)S(1)} fusion(s32[2048]{0:T(1024)S(1)} %get-tuple-element.1063, u32[1024]{0:T(1024)S(1)} %broadcast_clamp_fusion.7), kind=kCustom, calls=%fused_computation.5.clone.clone.1 | custom fusion | bytes 12288 | tf_op jit(solution)/shard_map/jit(searchsorted)/jit(_searchsorted_scan_impl)/vmap(jit(_searchsorted_scan_impl))/while/body/eval_jaxpr/gather | solution.py:51
  173.4 6.2 %gather_fusion.1 = s32[1024]{0:T(1024)S(1)} fusion(s32[2048]{0:T(1024)S(1)} %get-tuple-element.1063, u32[1024]{0:T(1024)S(1)} %broadcast_clamp_fusion.7), kind=kCustom, calls=%fused_computation.5.clone.clone.1 | custom fusion | bytes 12288 | tf_op jit(solution)/shard_map/jit(searchsorted)/jit(_searchsorted_scan_impl)/vmap(jit(_searchsorted_scan_impl))/while/body/eval_jaxpr/gather | solution.py:51
  179.6 6.2 %gather_fusion.1 = s32[1024]{0:T(1024)S(1)} fusion(s32[2048]{0:T(1024)S(1)} %get-tuple-element.1063, u32[1024]{0:T(1024)S(1)} %broadcast_clamp_fusion.7), kind=kCustom, calls=%fused_computation.5.clone.clone.1 | custom fusion | bytes 12288 | tf_op jit(solution)/shard_map/jit(searchsorted)/jit(_searchsorted_scan_impl)/vmap(jit(_searchsorted_scan_impl))/while/body/eval_jaxpr/gather | solution.py:51
  193.3 6.8 %gather_fusion.9 = bf16[1024]{0:T(1024)(128)(2,1)S(1)} fusion(bf16[2048]{0:T(1024)(128)(2,1)S(1)} %pad_maximum_fusion.4, s32[1024]{0:T(1024)S(1)} %fusion.33), kind=kCustom, calls=%fused_computation.11.clone | custom fusion | bytes 8192 | tf_op jit(solution)/shard_map/jit(_take)/gather | solution.py:62
  208.8 74.8 %while.102 = (s32[]{:T(128)}, u32[1024]{0:T(1024)S(1)}, u32[1024]{0:T(1024)S(1)}, s32[2048]{0:T(1024)S(1)}, s32[]{:T(128)}, /*index=5*/s32[]{:T(128)}, s32[]{}) while((s32[]{:T(128)}, u32[1024]{0:T(1024)S(1)}, u32[1024]{0:T(1024)S(1)}, s32[2048]{0:T(1024)S(1)}, s32[]{:T(128)}, /*index=5*/s32[]{:T(128)}, s32[]{}) %tuple.227), condition=%wide.region_25.30_spmd.clone, body=%wide.region_24.29_spmd.clone.sunk | while | flops 20484 | bytes 63597 | solution.py:51
  284.2 6.8 %gather_fusion.13 = bf16[1024]{0:T(1024)(128)(2,1)S(1)} fusion(bf16[2048]{0:T(1024)(128)(2,1)S(1)} %pad_maximum_fusion.5, s32[1024]{0:T(1024)S(1)} %fusion.34), kind=kCustom, calls=%fused_computation.12.clone | custom fusion | bytes 8192 | tf_op jit(solution)/shard_map/jit(_take)/gather | solution.py:62
  301.3 6.2 %collective-permute-done.9 = s32[32,1024]{0,1:T(8,128)} collective-permute-done((s32[32,1024]{0,1:T(8,128)S(1)}, s32[32,1024]{0,1:T(8,128)}, u32[]{:S(2)}, u32[]{:S(2)}) %collective-permute-start.9) | collective-permute-done | bytes 131104 | tf_op jit(solution)/shard_map/ppermute | solution.py:26
  335.5 14.5 %while.99 = (s32[]{:T(128)}, f32[4096,128]{1,0:T(8,128)S(1)}, f32[4096]{0:T(1024)S(1)}, s32[64,1024]{1,0:T(8,128)}, bf16[1024,128]{1,0:T(8,128)(2,1)S(1)}, /*ind...) while((s32[]{:T(128)}, f32[4096,128]{1,0:T(8,128)S(1)}, ...), condition=%wide.region_5.9_spmd.clone, body=%wide.region_4.8_spmd.clone.sunk | while | flops 272637952 | bytes 7735986 | solution.py:91
  369.2 23.6 %while.101 = (s32[]{:T(128)}, f32[4096,128]{1,0:T(8,128)}, f32[4096]{0:T(1024)S(1)}, s32[64,1024]{1,0:T(8,128)}, bf16[1024,128]{1,0:T(8,128)(2,1)}, /*index=5*/b...) while((s32[]{:T(128)}, f32[4096,128]{1,0:T(8,128)}, ...), condition=%wide.region_16.21_spmd.clone, body=%wide.region_15.20_spmd.clone.sunk | while | flops 272637952 | bytes 7735986 | solution.py:91
  406.2 14.4 %while.103 = (s32[]{:T(128)}, f32[4096,128]{1,0:T(8,128)S(1)}, f32[4096]{0:T(1024)S(1)}, s32[64,1024]{1,0:T(8,128)}, bf16[1024,128]{1,0:T(8,128)(2,1)S(1)}, /*in...) while((s32[]{:T(128)}, f32[4096,128]{1,0:T(8,128)S(1)}, ...), condition=%wide.region_27.32_spmd.clone, body=%wide.region_26.31_spmd.clone.sunk | while | flops 272637952 | bytes 7735986 | solution.py:91
  442.4 40.6 %psum.7 = f32[14,2,128]{2,1,0:T(2,128)S(1)} all-reduce(f32[14,2,128]{2,1,0:T(2,128)S(1)} %select_add_fusion.3), channel_id=1, replica_groups=mesh['rows'=8,'feat'=4] {'rows','feat'}, use_global_device_ids=true, to_apply=%region_45.50 | all-reduce | flops 3584 | bytes 28672 | tf_op jit(solution)/shard_map/psum | solution.py:182
  (498 shorter events, 271.5 us)
Async XLA Ops:
  1.5 289.6 %collective-permute-start.1 = (s32[32,1024]{1,0:T(8,128)S(1)}, s32[32,1024]{1,0:T(8,128)S(1)}, u32[]{:S(2)}, u32[]{:S(2)}) collective-permute-start(s32[32,1024]{1,0:T(8,128)S(1)} %concatenate.78), channel_id=1, source_target_pairs={{0,16},{16,0},{4,20},{20,4},{8,24},{24,8},{12,28},{28,12},{1,17},{... | collective-permute-start | bytes 393224 | tf_op jit(solution)/shard_map/ppermute | solution.py:26
  7.1 17.6 %collective-permute-start = (bf16[1024]{0:T(1024)(128)(2,1)S(1)}, bf16[1024]{0:T(1024)(128)(2,1)S(1)}, u32[]{:S(2)}, u32[]{:S(2)}) collective-permute-start(bf16[1024]{0:T(1024)(128)(2,1)S(1)} %and_select_fusion.2), channel_id=1, source_target_pairs={{0,16},{16,0},{4,20},{20,4},{8,24},{24,8},{12,28},{28,12},{1,17},{... | collective-permute-start | bytes 6152 | tf_op jit(solution)/shard_map/ppermute | solution.py:26
  7.8 100.4 %collective-permute-start.7 = (s32[3,1024]{1,0:T(4,128)S(1)}, s32[3,1024]{1,0:T(4,128)S(1)}, u32[]{:S(2)}, u32[]{:S(2)}) collective-permute-start(s32[3,1024]{1,0:T(4,128)S(1)} %concatenate.74), channel_id=1, source_target_pairs={{0,16},{16,0},{4,20},{20,4},{8,24},{24,8},{12,28},{28,12},{1,17},{... | collective-permute-start | bytes 36872 | tf_op jit(solution)/shard_map/ppermute | solution.py:26
  12.3 304.4 %collective-permute-start.2 = (bf16[1024,128]{1,0:T(8,128)(2,1)}, bf16[1024,128]{1,0:T(8,128)(2,1)}, u32[]{:S(2)}, u32[]{:S(2)}) collective-permute-start(bf16[1024,128]{1,0:T(8,128)(2,1)} %concatenate.80), channel_id=1, source_target_pairs={{0,16},{16,0},{4,20},{20,4},{8,24},{24,8},{12,28},{28,12},{1,17},{... | collective-permute-start | bytes 786440 | tf_op jit(solution)/shard_map/ppermute | solution.py:26
  25.9 75.5 %copy-start.8 = (bf16[512]{0:T(512)(128)(2,1)S(1)}, bf16[512]{0:T(512)(128)(2,1)}, u32[]{:S(2)}) copy-start(bf16[512]{0:T(512)(128)(2,1)} %param.27) | copy-start | bytes 3076
  100.7 7.5 %copy-start.7 = (s32[3,512]{1,0:T(4,128)S(1)}, s32[3,512]{1,0:T(4,128)}, u32[]{:S(2)}) copy-start(s32[3,512]{1,0:T(4,128)} %param.29) | copy-start | bytes 18436
  113.0 3.7 collective-permute-start.8
  115.5 84.7 %collective-permute-start.13 = (s32[3,1024]{0,1:T(8,128)S(1)}, s32[3,1024]{0,1:T(8,128)S(1)}, u32[]{:S(2)}, u32[]{:S(2)}) collective-permute-start(s32[3,1024]{0,1:T(8,128)S(1)} %bitcast_select_fusion.2), channel_id=1, source_target_pairs={{0,8},{8,0},{4,12},{12,4},{16,24},{24,16},{20,28},{28,20},{1,9},{9... | collective-permute-start | bytes 36872 | tf_op jit(solution)/shard_map/ppermute | solution.py:26
  204.6 3.7 collective-permute-start.14
  283.6 7.4 %copy-start.6 = (s32[32,512]{1,0:T(8,128)S(1)}, s32[32,512]{1,0:T(8,128)}, u32[]{:S(2)}) copy-start(s32[32,512]{1,0:T(8,128)} %param.28) | copy-start | bytes 196612
  296.8 10.7 %collective-permute-start.9 = (s32[32,1024]{0,1:T(8,128)S(1)}, s32[32,1024]{0,1:T(8,128)}, u32[]{:S(2)}, u32[]{:S(2)}) collective-permute-start(s32[32,1024]{0,1:T(8,128)S(1)} %bitcast_select_fusion.3), channel_id=1, source_target_pairs={{0,8},{8,0},{4,12},{12,4},{16,24},{24,16},{20,28},{28,20},{1,9},{9... | collective-permute-start | bytes 393224 | tf_op jit(solution)/shard_map/ppermute | solution.py:26
  309.6 7.2 %copy-start.5 = (bf16[512,128]{1,0:T(8,128)(2,1)S(1)}, bf16[512,128]{1,0:T(8,128)(2,1)}, u32[]{:S(2)}) copy-start(bf16[512,128]{1,0:T(8,128)(2,1)} %param.26) | copy-start | bytes 393220
  314.0 9.8 %collective-permute-start.15 = (s32[32,1024]{0,1:T(8,128)S(1)}, s32[32,1024]{0,1:T(8,128)}, u32[]{:S(2)}, u32[]{:S(2)}) collective-permute-start(s32[32,1024]{0,1:T(8,128)S(1)} %bitcast_select_fusion.1), channel_id=1, source_target_pairs={{0,4},{4,0},{8,12},{12,8},{16,20},{20,16},{24,28},{28,24},{1,5},{5... | collective-permute-start | bytes 393224 | tf_op jit(solution)/shard_map/ppermute | solution.py:26
  325.9 8.7 %copy-start.3 = (s32[64,1024]{1,0:T(8,128)S(1)}, s32[64,1024]{1,0:T(8,128)}, u32[]{:S(2)}) copy-start(s32[64,1024]{1,0:T(8,128)} %shift_right_arithmetic.79) | copy-start | bytes 786436
  325.9 8.7 %copy-start.4 = (s32[64,1024]{1,0:T(8,128)S(1)}, s32[64,1024]{1,0:T(8,128)}, u32[]{:S(2)}) copy-start(s32[64,1024]{1,0:T(8,128)} %shift_right_arithmetic.85) | copy-start | bytes 786436
  350.1 2.1 copy-start
  350.1 3.7 collective-permute-start.5
  352.5 10.8 %collective-permute-start.10 = (bf16[1024,128]{1,0:T(8,128)(2,1)S(1)}, bf16[1024,128]{1,0:T(8,128)(2,1)}, u32[]{:S(2)}, u32[]{:S(2)}) collective-permute-start(bf16[1024,128]{1,0:T(8,128)(2,1)S(1)} %get-tuple-element.1183), channel_id=1, source_target_pairs={{0,8},{8,0},{4,12},{12,4},{16,24},{24,16},{20,28},{28,20},{1,9},{9... | collective-permute-start | bytes 786440 | tf_op jit(solution)/shard_map/ppermute | solution.py:26
  353.9 9.1 %collective-permute-start.6 = (f32[16,64]{1,0:T(8,128)S(1)}, f32[16,64]{1,0:T(8,128)S(1)}, u32[]{:S(2)}, u32[]{:S(2)}) collective-permute-start(f32[16,64]{1,0:T(8,128)S(1)} %slice_select_fusion.6), channel_id=1, source_target_pairs={{0,4},{4,0},{8,12},{12,8},{16,20},{20,16},{24,28},{28,24},{1,5},{5... | collective-permute-start | bytes 12296 | tf_op jit(solution)/shard_map/ppermute | solution.py:26
  361.5 66.0 %collective-permute-start.3 = (f32[32,8192]{1,0:T(8,128)}, f32[32,8192]{1,0:T(8,128)}, u32[]{:S(2)}, u32[]{:S(2)}) collective-permute-start(f32[32,8192]{1,0:T(8,128)} %select_n.344), channel_id=1, source_target_pairs={{0,8},{8,0},{4,12},{12,4},{16,24},{24,16},{20,28},{28,20},{1,9},{9... | collective-permute-start | bytes 3145736 | tf_op jit(solution)/shard_map/ppermute | solution.py:26
  368.5 33.1 %collective-permute-start.16 = (bf16[1024,128]{1,0:T(8,128)(2,1)}, bf16[1024,128]{1,0:T(8,128)(2,1)}, u32[]{:S(2)}, u32[]{:S(2)}) collective-permute-start(bf16[1024,128]{1,0:T(8,128)(2,1)} %select_select_fusion.7), channel_id=1, source_target_pairs={{0,4},{4,0},{8,12},{12,8},{16,20},{20,16},{24,28},{28,24},{1,5},{5... | collective-permute-start | bytes 786440 | tf_op jit(solution)/shard_map/ppermute | solution.py:26
  392.9 8.4 %collective-permute-start.12 = (f32[32,64]{1,0:T(8,128)S(1)}, f32[32,64]{1,0:T(8,128)S(1)}, u32[]{:S(2)}, u32[]{:S(2)}) collective-permute-start(f32[32,64]{1,0:T(8,128)S(1)} %select_n.369), channel_id=1, source_target_pairs={{0,4},{4,0},{8,12},{12,8},{16,20},{20,16},{24,28},{28,24},{1,5},{5... | collective-permute-start | bytes 24584 | tf_op jit(solution)/shard_map/ppermute | solution.py:26
  400.6 29.8 %collective-permute-start.11 = (f32[32,8192]{1,0:T(8,128)}, f32[32,8192]{1,0:T(8,128)}, u32[]{:S(2)}, u32[]{:S(2)}) collective-permute-start(f32[32,8192]{1,0:T(8,128)} %select_n.364), channel_id=1, source_target_pairs={{0,4},{4,0},{8,12},{12,8},{16,20},{20,16},{24,28},{28,24},{1,5},{5... | collective-permute-start | bytes 3145736 | tf_op jit(solution)/shard_map/ppermute | solution.py:26
  421.8 5.7 %copy-start.1 = (f32[32,8192]{1,0:T(8,128)S(1)}, f32[32,8192]{1,0:T(8,128)}, u32[]{:S(2)}) copy-start(f32[32,8192]{1,0:T(8,128)} %select_n.342) | copy-start | bytes 3145732
  427.5 2.9 copy-start.2
  429.0 9.2 %collective-permute-start.4 = (f32[16,8192]{1,0:T(8,128)S(1)}, f32[16,8192]{1,0:T(8,128)S(1)}, u32[]{:S(2)}, u32[]{:S(2)}) collective-permute-start(f32[16,8192]{1,0:T(8,128)S(1)} %slice_select_fusion.5), channel_id=1, source_target_pairs={{0,4},{4,0},{8,12},{12,8},{16,20},{20,16},{24,28},{28,24},{1,5},{5... | collective-permute-start | bytes 1572872 | tf_op jit(solution)/shard_map/ppermute | solution.py:26
  432.0 10.2 %copy-start.9 = (pred[14]{0:T(512)(128)(4,1)S(1)}, pred[14]{0:T(512)(128)(4,1)}, u32[]{:S(2)}) copy-start(pred[14]{0:T(512)(128)(4,1)} %get-tuple-element.825) | copy-start | bytes 46
  432.0 10.2 %copy-start.10 = (pred[14]{0:T(512)(128)(4,1)S(1)}, pred[14]{0:T(512)(128)(4,1)}, u32[]{:S(2)}) copy-start(pred[14]{0:T(512)(128)(4,1)} %get-tuple-element.826) | copy-start | bytes 46
  432.0 10.2 %copy-start.11 = (pred[14]{0:T(512)(128)(4,1)S(1)}, pred[14]{0:T(512)(128)(4,1)}, u32[]{:S(2)}) copy-start(pred[14]{0:T(512)(128)(4,1)} %iota_compare_fusion.2) | copy-start | bytes 46
where the time goes:
time: 485 us; the launch traced here: 484 us
  local copies, waits for them, and re-layouts  304 us (63%)
  other arithmetic  56 us (12%)
  blocking collectives  40.6 us (8%)
  matrix products  31.3 us (6%)
  starting transfers between devices  23.8 us (5%)
  between operations  13.5 us (3%)
  waiting for transfers between devices  11.8 us (2%)
    gather x36, local copies, waits for them, and re-layouts, front_index(): source = jnp.searchsorted(running, wanted, side='left')  222 us
    psum x1, blocking collectives, on_device(): totals = lax.psum(collected, ('rows', 'feat'))  40.6 us
    ppermute x17, starting transfers between devices, swapped(): return lax.ppermute(block, axis, route)  23.8 us
    dot_general x12, matrix products, add_block(): jnp.dot(one_hot, grad_block, preferred_element_type=jnp.float32)  23.5 us
    gather x3, local copies, waits for them, and re-layouts, pick_slots(): taken = jnp.take(values, source, axis=0)  20.4 us
    gather x5, local copies, waits for them, and re-layouts, pick_columns(): taken = jnp.take(values, source, axis=1)  19 us
    ppermute x17, waiting for transfers between devices, swapped(): return lax.ppermute(block, axis, route)  11.8 us
    gather x3, local copies, waits for them, and re-layouts, pick_rows(): taken = jnp.take(values, source, axis=0)  10.7 us
  transfers between devices with their start and end apart: 17, of which 6 were waited for; matrix products, arithmetic and copies ran while one was open for 75% of the time, Pallas kernels for 0%

commit v1 on v0

v1 whole, which is shorter than its diff:
```python
import functools

import jax
import jax.numpy as jnp
from jax import lax
from jax.experimental import pallas as pl
from jax.experimental.pallas import tpu as pltpu
from jax.sharding import PartitionSpec as P

BINS = 64
LANES = 128
TILE = 16
OUT_SPLIT = 2
penalty = 1.0
VMEM_BYTES = 32 * 2**20

bf16 = jnp.bfloat16
f32 = jnp.float32
NT = (((1,), (1,)), ((), ()))


def round_up(value, unit):
    return -(-value // unit) * unit


def whole(*_):
    return pl.BlockSpec(memory_space=pltpu.VMEM)


class Plan:
    def __init__(self, rows_axis, feat_axis, gradients, bin_words, children):
        self.devices = rows_axis
        self.row_dev, self.outs = gradients.shape
        self.words = bin_words.shape[0]
        self.feats = 2 * self.words
        self.levels = children.shape[0]
        self.leaves = 2**self.levels
        self.shares = rows_axis // OUT_SPLIT
        self.share = self.feats // self.shares
        self.outs_dev = self.outs // OUT_SPLIT
        self.pair = 2 if feat_axis % 2 == 0 else 1
        self.outs_sent = self.outs_dev // self.pair
        self.code_at = self.outs_sent
        self.misc_at = self.outs_sent + self.share
        self.sent_rows = round_up(self.misc_at + 2, 8)
        self.groups = self.share // 2
        self.gain_rows = self.levels * self.groups
        self.score_at = round_up(self.gain_rows, 8)
        self.message = self.score_at + 8
        self.top_bit = rows_axis.bit_length() - 1

    def leaf_of(self, device):
        return device >> (self.top_bit - self.levels)

    def code_row(self, feature):
        return self.code_at + feature // 2 + (feature % 2) * (self.share // 2)


def prep_kernel(plan, place, feature_ref, bin_ref, grad_ref, hess_ref, word_ref, child_ref, send_ref, score_ref, masks, turned):
    rows = plan.row_dev
    grads = grad_ref[...]
    hess = hess_ref[...].astype(f32)
    words = word_ref[...]
    low = jnp.bitwise_and(words, 63)
    high = jnp.bitwise_and(jnp.right_shift(words, 6), 63)
    codes = (low.astype(f32), high.astype(f32))
    nodes = [child_ref[0:1, :]]
    for level in range(1, plan.levels):
        nodes.append(nodes[-1] * 2 + child_ref[level : level + 1, :])

    unit = jnp.where(
        lax.broadcasted_iota(jnp.int32, (plan.outs, plan.outs), 0)
        == lax.broadcasted_iota(jnp.int32, (plan.outs, plan.outs), 1),
        1.0,
        0.0,
    ).astype(bf16)
    turned[...] = lax.dot_general(unit, grads, NT, preferred_element_type=f32)

    half = lax.rem(place[1], plan.pair)
    word_share = plan.share // 2
    misc_rows = plan.sent_rows - plan.misc_at
    at = lax.broadcasted_iota(jnp.int32, (misc_rows, rows), 0)
    misc = jnp.where(at == 0, hess, jnp.where(at == 1, nodes[-1].astype(f32), 0.0))
    for split in range(OUT_SPLIT):
        start = pl.multiple_of(split * plan.outs_dev + half * plan.outs_sent, plan.outs_sent)
        part = turned[pl.ds(start, plan.outs_sent), :]
        for share in range(plan.shares):
            span = slice(share * word_share, (share + 1) * word_share)
            send_ref[share * OUT_SPLIT + split] = jnp.concatenate(
                [part, codes[0][span], codes[1][span], misc], axis=0
            ).astype(bf16)

    masks[...] = jnp.zeros_like(masks)
    panel = place[1]
    for level in range(plan.levels):
        for node in range(2 ** (level + 1)):
            slot = 2 ** (level + 1) - 2 + node
            feature = feature_ref[slot]
            inner = feature - panel * plan.feats
            owned = jnp.logical_and(inner >= 0, inner < plan.feats)
            inner = jnp.clip(inner, 0, plan.feats - 1)
            word = word_ref[pl.ds(inner // 2, 1), :]
            code = jnp.bitwise_and(jnp.right_shift(word, 6 * lax.rem(inner, 2)), 63)
            here = jnp.where(nodes[level] == node, jnp.where(owned, 1.0, 0.0), 0.0)
            left = jnp.where(code <= bin_ref[slot], here, 0.0)
            right = here - left
            under = 2 ** (plan.levels - level - 1)
            for leaf in range(node * under, (node + 1) * under):
                masks[leaf * 8 + level : leaf * 8 + level + 1, :] = left
                at_right = leaf * 8 + plan.levels + level
                masks[at_right : at_right + 1, :] = right
    mask = masks[...]
    sums = jnp.dot(mask.astype(bf16), grads, preferred_element_type=f32)
    curv = jnp.sum(mask * hess, axis=1, keepdims=True)
    shape = (plan.leaves * 8, plan.outs)
    line = jnp.bitwise_and(lax.broadcasted_iota(jnp.int32, shape, 0), 7)
    lane = lax.broadcasted_iota(jnp.int32, shape, 1)
    spread = jnp.where(lane == line, curv, 0.0).reshape(plan.leaves, 8, plan.outs)
    spread = jnp.broadcast_to(jnp.sum(spread, axis=1, keepdims=True), spread.shape)
    score_ref[...] = jnp.where(line == 2 * plan.levels, spread.reshape(shape), sums)


def main_kernel(plan, chunk, got_ref, *refs):
    others, (score_ref, out_ref, weighted, marks, left_sums) = refs[:-5], refs[-5:]
    rows = plan.row_dev
    leaves, outs_dev = plan.leaves, plan.outs_dev
    hess_at = leaves * outs_dev
    step = min(4, plan.share)
    order = [feature for k in range(plan.groups) for feature in (k, k + plan.groups)]
    level_bins = lax.broadcasted_iota(jnp.int32, (BINS, rows), 0).astype(f32).astype(bf16)
    leaf_ids = lax.broadcasted_iota(jnp.int32, (TILE, rows), 0).astype(f32)
    zero = jnp.zeros((), bf16)
    one = jnp.ones((), bf16)

    def add_chunk(first, fresh):
        for k in range(chunk):
            source = first + k
            columns = slice(k * rows, (k + 1) * rows)
            misc = got_ref[source, plan.misc_at : plan.misc_at + 2, :].astype(f32)
            hess, node = misc[0:1], misc[1:2]
            weighted[hess_at : hess_at + TILE, columns] = jnp.where(leaf_ids == node, hess, 0.0).astype(bf16)
            node_wide = jnp.broadcast_to(node, (plan.outs_sent, rows)).astype(bf16)
            for place, ref in enumerate((got_ref, *others)):
                grads = ref[source, 0 : plan.outs_sent, :]
                for leaf in range(leaves):
                    at = leaf * outs_dev + place * plan.outs_sent
                    weighted[at : at + plan.outs_sent, columns] = jnp.where(
                        node_wide == jnp.asarray(leaf, bf16), grads, zero
                    )
        for group in range(plan.share // step):
            for k in range(chunk):
                for place, feature in enumerate(order[group * step : (group + 1) * step]):
                    row = plan.code_row(feature)
                    code = got_ref[first + k, row : row + 1, :]
                    marks[place * BINS : (place + 1) * BINS, k * rows : (k + 1) * rows] = jnp.where(
                        jnp.broadcast_to(code, (BINS, rows)) <= level_bins, one, zero
                    )
            part = lax.dot_general(weighted[...], marks[...], NT, preferred_element_type=f32)
            span = slice(group * step * BINS, (group + 1) * step * BINS)
            if fresh:
                left_sums[:, span] = part
            else:
                left_sums[:, span] += part

    add_chunk(0, True)
    count = plan.devices // chunk
    if count > 1:
        lax.fori_loop(1, count, lambda c, _: (add_chunk(c * chunk, False), 0)[1], 0)

    for group in range(plan.share // step):
        span = slice(group * step * BINS, (group + 1) * step * BINS)
        left = [left_sums[leaf * outs_dev : (leaf + 1) * outs_dev, span] for leaf in range(leaves)]
        hess = [left_sums[hess_at + leaf : hess_at + leaf + 1, span] for leaf in range(leaves)]
        for level in reversed(range(plan.levels)):
            nodes = 2 ** (level + 1)
            if level < plan.levels - 1:
                left = [left[2 * n] + left[2 * n + 1] for n in range(nodes)]
                hess = [hess[2 * n] + hess[2 * n + 1] for n in range(nodes)]
            for n in range(nodes):
                total = left[n][:, BINS - 1 : BINS]
                hess_total = hess[n][:, BINS - 1 : BINS]
                right = total - left[n]
                gain = (
                    jnp.sum(left[n] * left[n], axis=0, keepdims=True) / (hess[n] + penalty)
                    + jnp.sum(right * right, axis=0, keepdims=True) / (hess_total - hess[n] + penalty)
                    - jnp.sum(total * total, axis=0, keepdims=True) / (hess_total + penalty)
                ) / plan.outs
                under = plan.devices // nodes
                for tile in range(step // 2):
                    piece = gain[:, tile * LANES : (tile + 1) * LANES]
                    row = level * plan.groups + group * (step // 2) + tile
                    for device in range(n * under, (n + 1) * under):
                        out_ref[device, row : row + 1, :] = piece
    if plan.score_at > plan.gain_rows:
        filler = jnp.zeros((plan.score_at - plan.gain_rows, LANES), f32)
        for device in range(plan.devices):
            out_ref[device, plan.gain_rows : plan.score_at, :] = filler
    for device in range(plan.devices):
        leaf = plan.leaf_of(device)
        out_ref[device, plan.score_at : plan.score_at + 8, :] = score_ref[leaf * 8 : leaf * 8 + 8, :]


def final_kernel(plan, place, got_ref, *outs):
    *gain_refs, child_ref = outs
    half = plan.groups
    for level, gain_ref in enumerate(gain_refs):
        size = plan.devices >> (level + 1)
        position = lax.rem(place[0], size)
        count = plan.feats // size // plan.share
        for t in range(count):
            share = position * count + t
            rows = slice(level * half, (level + 1) * half)
            total = got_ref[share * OUT_SPLIT, rows, :]
            for split in range(1, OUT_SPLIT):
                total = total + got_ref[share * OUT_SPLIT + split, rows, :]
            for side in range(2):
                at = t * plan.share + side * half
                gain_ref[at : at + half, :] = total[:, side * BINS : (side + 1) * BINS]
    sums = got_ref[0, plan.score_at : plan.score_at + 8, :]
    for device in range(1, plan.devices):
        sums = sums + got_ref[device, plan.score_at : plan.score_at + 8, :]
    curv = sums[2 * plan.levels : 2 * plan.levels + 1, :]
    for level in range(plan.levels):
        for side in range(2):
            line = side * plan.levels + level
            scale = jnp.sqrt(curv[:, line : line + 1] + penalty)
            child_ref[level, 0, side : side + 1, :] = -sums[line : line + 1, :] / scale


def on_device(gradients, hessians, bin_words, children, split_feature, split_bin):
    plan = Plan(lax.axis_size("rows"), lax.axis_size("feat"), gradients, bin_words, children)
    rows = plan.row_dev
    place = jnp.stack([lax.axis_index("rows"), lax.axis_index("feat")]).astype(jnp.int32)
    params = pltpu.CompilerParams(vmem_limit_bytes=VMEM_BYTES)
    smem = pl.BlockSpec(memory_space=pltpu.SMEM)

    send, scores = pl.pallas_call(
        functools.partial(prep_kernel, plan),
        out_shape=(
            jax.ShapeDtypeStruct((plan.devices, plan.sent_rows, rows), bf16),
            jax.ShapeDtypeStruct((plan.leaves * 8, plan.outs), f32),
        ),
        in_specs=[smem, smem, smem] + [whole()] * 4,
        out_specs=(whole(), whole()),
        scratch_shapes=[
            pltpu.VMEM((plan.leaves * 8, rows), f32),
            pltpu.VMEM((plan.outs, rows), f32),
        ],
        compiler_params=params,
        name="prep",
    )(place, split_feature, split_bin, gradients, hessians.reshape(1, rows), bin_words, children)

    scores = lax.psum(scores, "feat")
    got = lax.all_to_all(send, "rows", 0, 0)
    arrays = [got]
    if plan.pair > 1:
        route = [(p, p ^ 1) for p in range(lax.axis_size("feat"))]
        arrays.append(lax.ppermute(got, "feat", route))

    chunk = max(1, min(plan.devices, 4096 // rows))
    while plan.devices % chunk:
        chunk -= 1
    sums_rows = plan.leaves * plan.outs_dev + TILE
    message = pl.pallas_call(
        functools.partial(main_kernel, plan, chunk),
        out_shape=jax.ShapeDtypeStruct((plan.devices, plan.message, LANES), f32),
        in_specs=[whole()] * (len(arrays) + 1),
        out_specs=whole(),
        scratch_shapes=[
            pltpu.VMEM((sums_rows, chunk * rows), bf16),
            pltpu.VMEM((min(4, plan.share) * BINS, chunk * rows), bf16),
            pltpu.VMEM((sums_rows, plan.share * BINS), f32),
        ],
        compiler_params=params,
        name="gains",
    )(*arrays, scores)

    answer = lax.all_to_all(message, "rows", 0, 0)
    shapes = [
        jax.ShapeDtypeStruct((plan.feats // (plan.devices >> (level + 1)), BINS), f32)
        for level in range(plan.levels)
    ]
    shapes.append(jax.ShapeDtypeStruct((plan.levels, 1, 2, plan.outs), f32))
    return pl.pallas_call(
        functools.partial(final_kernel, plan),
        out_shape=tuple(shapes),
        in_specs=[smem, whole()],
        out_specs=tuple(whole() for _ in shapes),
        compiler_params=params,
        name="finish",
    )(place, answer)


def solution(mesh):
    placed = (P("rows", None), P("rows"), P("feat", "rows"), P(None, "rows"), P(), P())
    return jax.shard_map(
        on_device,
        mesh=mesh,
        in_specs=placed,
        out_specs=(
            P("rows", "feat"),
            P("rows", "feat"),
            P("rows", "feat"),
            P(None, "rows", None, None),
        ),
        check_vma=False,
    )
```

time: 485 us -> 54.3 us (0.11)
  local copies, waits for them, and re-layouts: 304 us -> 3 us
  other arithmetic: 56 us -> 0.07 us
  matrix products: 31.3 us -> 0 us
  starting transfers between devices: 23.8 us -> 0.01 us
  between operations: 13.5 us -> 0.68 us
  waiting for transfers between devices: 11.8 us -> 0.01 us
  Pallas kernels: 0 us -> 7.58 us
    gather x47 -> x0, local copies, waits for them, and re-layouts: 272 us -> none  [the longest x36 222 us: front_index(): source = jnp.searchsorted(running, wanted, side='left')]
    dot_general x24 -> x0, matrix products: 31.3 us -> none  [the longest x12 23.5 us: add_block(): jnp.dot(one_hot, grad_block, preferred_element_type=jnp.float32)]
    all_to_all x0 -> x2, blocking collectives: none -> 30.9 us  [the longest x1 20.3 us: on_device(): got = lax.all_to_all(send, 'rows', 0, 0)]
    psum x1, blocking collectives: 40.6 us -> 11.7 us  [on_device(): scores = lax.psum(scores, 'feat')]
    ppermute x17 -> x1, starting transfers between devices: 23.8 us -> 0.01 us  [on_device(): arrays.append(lax.ppermute(got, 'feat', route))]
    select_n x90 -> x0, other arithmetic: 13.8 us -> none  [the longest x3 5.4 us: on_device(): jnp.where(upper_half, share_grad[:half_rows], share_grad[half_rows:])]
    eq x23 -> x0, other arithmetic: 13.5 us -> none  [the longest x12 8.54 us: add_block(): code_block[:, None, :] == bin_levels[None, :, None]]
    dynamic_slice x38 -> x0, local copies, waits for them, and re-layouts: 12.6 us -> none  [the longest x12 10.2 us: add_block(): code_block = lax.dynamic_slice_in_dim(bin_codes, start_row, block_rows, 1)]
  transfers between devices with their start and end apart: 17 -> 1, of which waited for: 6 -> 0; matrix products, arithmetic and copies ran while one was open for 75% -> 0% of each run, Pallas kernels for 0% -> 0%
where the time goes in v1:
time: 54.3 us; the launch traced here: 54 us
  blocking collectives  42.7 us (79%)
  Pallas kernels  7.58 us (14%)
  local copies, waits for them, and re-layouts  3 us (6%)
  between operations  0.68 us (1%)
    all_to_all x1, blocking collectives, on_device(): got = lax.all_to_all(send, 'rows', 0, 0)  20.3 us
    psum x1, blocking collectives, on_device(): scores = lax.psum(scores, 'feat')  11.7 us
    all_to_all x1, blocking collectives, on_device(): answer = lax.all_to_all(message, 'rows', 0, 0)  10.6 us
    pallas_call x1, Pallas kernels, on_device(): pl.pallas_call(functools.partial(main_kernel, plan, chunk), out_shape=jax...  5.47 us
    unnamed x12, local copies, waits for them, and re-layouts  3 us
    pallas_call x1, Pallas kernels, on_device(): pl.pallas_call(functools.partial(final_kernel, plan), out_shape=tuple(sha...  1.26 us
  transfers between devices with their start and end apart: 1, of which 0 were waited for; matrix products, arithmetic and copies ran while one was open for 0% of the time, Pallas kernels for 0%

profile of v1, /device:TPU:0, one launch (start us, length us, event | category | flops | bytes accessed | tf_op | source)
XLA Modules:
  0.0 54.0 jit_solution(11331681936845857125)
XLA Ops:
  0.6 0.0 copy-start.5
  0.6 0.0 copy-start.2
  0.7 0.7 %copy-done.5 = bf16[512]{0:T(512)(128)(2,1)S(1)} copy-done((bf16[512]{0:T(512)(128)(2,1)S(1)}, bf16[512]{0:T(512)(128)(2,1)}, u32[]{:S(2)}) %copy-start.5) | copy-done | bytes 1048
  1.3 0.0 copy-start.3
  1.3 0.0 copy-start.4
  1.3 0.1 pad_add_fusion.place
  1.4 0.0 copy-done.2
  1.4 0.6 %copy-done.3 = s32[14]{0:T(128)S(1)} copy-done((s32[14]{0:T(128)S(1)}, s32[14]{0:T(128)}, u32[]{:S(2)}) %copy-start.3) | copy-done | bytes 80
  2.0 0.0 copy-done.4
  2.0 0.0 copy-start
  2.0 0.9 %copy-done = bf16[512,128]{1,0:T(8,128)(2,1)S(1)} copy-done((bf16[512,128]{1,0:T(8,128)(2,1)S(1)}, bf16[512,128]{1,0:T(8,128)(2,1)}, u32[]{:S(2)}) %copy-start) | copy-done | bytes 131096
  2.9 0.0 copy-start.1
  2.9 0.8 %copy-done.1 = s32[32,512]{1,0:T(8,128)S(1)} copy-done((s32[32,512]{1,0:T(8,128)S(1)}, s32[32,512]{1,0:T(8,128)}, u32[]{:S(2)}) %copy-start.1) | copy-done | bytes 65560
  3.7 0.9 %prep.1 = (bf16[8,56,512]{2,1,0:T(8,128)(2,1)S(1)}, f32[64,128]{1,0:T(8,128)S(1)}) custom-call(s32[2]{0:T(128)S(1)} %pad_add_fusion.place, s32[14]{0:T(128)S(1)} %copy-done.3, s32[14]{0:T(128)S(1)} %copy-done.4, bf16[512,128]{1,0:T(8,128)(2,1)S(1)} %copy-done, bf16[1,512]{1,0:T(2,128)(2,1)S(1)} %reshape.11.hess_ref, s32[32,512]{1,0:T(8,128)S(1)} %copy-done.1, ...), custom_call_target="tpu_custom_call" | custom-call | tf_op jit(solution)/shard_map/prep/pallas_call | solution.py:237
  4.6 20.3 %all_to_all.10.got_ref = bf16[8,56,512]{2,1,0:T(8,128)(2,1)S(1)} all-to-all(bf16[8,56,512]{2,1,0:T(8,128)(2,1)S(1)} %get-tuple-element.6), channel_id=1, replica_groups=mesh['rows'=8,'feat'=4] {'rows'}, dimensions={0} | all-to-all | bytes 917504 | tf_op jit(solution)/shard_map/all_to_all | solution.py:254
  24.9 0.0 collective-permute-start
  24.9 11.7 %psum.7.refs_1_ = f32[64,128]{1,0:T(8,128)S(1)} all-reduce(f32[64,128]{1,0:T(8,128)S(1)} %get-tuple-element.7), channel_id=1, replica_groups=mesh['rows'=8,'feat'=4] {'feat'}, use_global_device_ids=true, to_apply=%region_0.0 | all-reduce | flops 8192 | bytes 65536 | tf_op jit(solution)/shard_map/psum | solution.py:253
  36.6 0.0 collective-permute-done.refs_0_
  36.7 5.5 %gains.1 = f32[8,32,128]{2,1,0:T(8,128)S(1)} custom-call(bf16[8,56,512]{2,1,0:T(8,128)(2,1)S(1)} %all_to_all.10.got_ref, bf16[8,56,512]{2,1,0:T(8,128)(2,1)S(1)} %collective-permute-done.refs_0_, f32[64,128]{1,0:T(8,128)S(1)} %psum.7.refs_1_), custom_call_target="tpu_custom_call" | custom-call | tf_op jit(solution)/shard_map/gains/pallas_call | solution.py:264
  42.1 10.6 %all_to_all.11.got_ref = f32[8,32,128]{2,1,0:T(8,128)S(1)} all-to-all(f32[8,32,128]{2,1,0:T(8,128)S(1)} %gains.1), channel_id=1, replica_groups=mesh['rows'=8,'feat'=4] {'rows'}, dimensions={0} | all-to-all | bytes 262144 | tf_op jit(solution)/shard_map/all_to_all | solution.py:278
  52.8 1.3 %finish.1 = (f32[16,64]{1,0:T(8,128)}, f32[32,64]{1,0:T(8,128)}, f32[64,64]{1,0:T(8,128)}, f32[3,1,2,128]{3,2,1,0:T(2,128)}) custom-call(s32[2]{0:T(128)S(1)} %pad_add_fusion.place, f32[8,32,128]{2,1,0:T(8,128)S(1)} %all_to_all.11.got_ref), custom_call_target="tpu_custom_call" | custom-call | tf_op jit(solution)/shard_map/finish/pallas_call | solution.py:284
  (1 shorter events, 0.0 us)
Async XLA Ops:
  0.6 0.7 %copy-start.5 = (bf16[512]{0:T(512)(128)(2,1)S(1)}, bf16[512]{0:T(512)(128)(2,1)}, u32[]{:S(2)}) copy-start(bf16[512]{0:T(512)(128)(2,1)} %param.7) | copy-start | bytes 3076
  0.6 0.8 %copy-start.2 = (s32[3,512]{1,0:T(4,128)S(1)}, s32[3,512]{1,0:T(4,128)}, u32[]{:S(2)}) copy-start(s32[3,512]{1,0:T(4,128)} %child_ref.1) | copy-start | bytes 18436
  1.3 0.7 %copy-start.3 = (s32[14]{0:T(128)S(1)}, s32[14]{0:T(128)}, u32[]{:S(2)}) copy-start(s32[14]{0:T(128)} %feature_ref.1) | copy-start | bytes 172
  1.3 0.7 %copy-start.4 = (s32[14]{0:T(128)S(1)}, s32[14]{0:T(128)}, u32[]{:S(2)}) copy-start(s32[14]{0:T(128)} %bin_ref.1) | copy-start | bytes 172
  2.0 0.9 %copy-start = (bf16[512,128]{1,0:T(8,128)(2,1)S(1)}, bf16[512,128]{1,0:T(8,128)(2,1)}, u32[]{:S(2)}) copy-start(bf16[512,128]{1,0:T(8,128)(2,1)} %grad_ref.1) | copy-start | bytes 393220
  2.9 0.8 %copy-start.1 = (s32[32,512]{1,0:T(8,128)S(1)}, s32[32,512]{1,0:T(8,128)}, u32[]{:S(2)}) copy-start(s32[32,512]{1,0:T(8,128)} %word_ref.1) | copy-start | bytes 196612
  24.9 11.8 %collective-permute-start = (bf16[8,56,512]{2,1,0:T(8,128)(2,1)S(1)}, bf16[8,56,512]{2,1,0:T(8,128)(2,1)S(1)}, u32[]{:S(2)}, u32[]{:S(2)}) collective-permute-start(bf16[8,56,512]{2,1,0:T(8,128)(2,1)S(1)} %all_to_all.10.got_ref), channel_id=1, source_target_pairs={{0,1},{1,0},{2,3},{3,2},{4,5},{5,4},{6,7},{7,6},{8,9},{9,8},{10,11... | collective-permute-start | bytes 1376264 | tf_op jit(solution)/shard_map/ppermute | solution.py:258

commit v2 on v1

--- a/solution.py
+++ b/solution.py
@@ -11,6 +11,7 @@
 LANES = 128
 TILE = 16
 OUT_SPLIT = 2
+PIECES = 3
 penalty = 1.0
 VMEM_BYTES = 32 * 2**20
 
@@ -42,11 +43,13 @@
         self.outs_sent = self.outs_dev // self.pair
         self.code_at = self.outs_sent
         self.misc_at = self.outs_sent + self.share
-        self.sent_rows = round_up(self.misc_at + 2, 8)
+        self.score_rows = 2 * self.levels + 1
+        self.spans = self.row_dev // LANES
+        self.misc_rows = 2 + -(-self.score_rows * PIECES // self.spans)
+        self.sent_rows = round_up(self.misc_at + self.misc_rows, 8)
         self.groups = self.share // 2
         self.gain_rows = self.levels * self.groups
-        self.score_at = round_up(self.gain_rows, 8)
-        self.message = self.score_at + 8
+        self.message = round_up(self.gain_rows, 8)
         self.top_bit = rows_axis.bit_length() - 1
 
     def leaf_of(self, device):
@@ -56,10 +59,22 @@
         return self.code_at + feature // 2 + (feature % 2) * (self.share // 2)
 
 
-def prep_kernel(plan, place, feature_ref, bin_ref, grad_ref, hess_ref, word_ref, child_ref, send_ref, score_ref, masks, turned):
+def prep_kernel(plan, *refs):
+    inputs, send_ref, refs = refs[:6], refs[6], refs[7:]
+    fetched, (masks, turned, sems) = refs[:6], refs[6:]
+    copies = [
+        pltpu.make_async_copy(source, target, sems.at[i])
+        for i, (source, target) in enumerate(zip(inputs, fetched, strict=True))
+    ]
+    for copy in copies:
+        copy.start()
+    for copy in copies:
+        copy.wait()
+    grad_ref, hess_ref, word_ref, child_ref, feature_ref, bin_ref = fetched
     rows = plan.row_dev
     grads = grad_ref[...]
-    hess = hess_ref[...].astype(f32)
+    hess = hess_ref[...].astype(f32).reshape(1, rows)
+    panel = lax.axis_index("feat")
     words = word_ref[...]
     low = jnp.bitwise_and(words, 63)
     high = jnp.bitwise_and(jnp.right_shift(words, 6), 63)
@@ -76,22 +91,7 @@
     ).astype(bf16)
     turned[...] = lax.dot_general(unit, grads, NT, preferred_element_type=f32)
 
-    half = lax.rem(place[1], plan.pair)
-    word_share = plan.share // 2
-    misc_rows = plan.sent_rows - plan.misc_at
-    at = lax.broadcasted_iota(jnp.int32, (misc_rows, rows), 0)
-    misc = jnp.where(at == 0, hess, jnp.where(at == 1, nodes[-1].astype(f32), 0.0))
-    for split in range(OUT_SPLIT):
-        start = pl.multiple_of(split * plan.outs_dev + half * plan.outs_sent, plan.outs_sent)
-        part = turned[pl.ds(start, plan.outs_sent), :]
-        for share in range(plan.shares):
-            span = slice(share * word_share, (share + 1) * word_share)
-            send_ref[share * OUT_SPLIT + split] = jnp.concatenate(
-                [part, codes[0][span], codes[1][span], misc], axis=0
-            ).astype(bf16)
-
     masks[...] = jnp.zeros_like(masks)
-    panel = place[1]
     for level in range(plan.levels):
         for node in range(2 ** (level + 1)):
             slot = 2 ** (level + 1) - 2 + node
@@ -117,11 +117,38 @@
     lane = lax.broadcasted_iota(jnp.int32, shape, 1)
     spread = jnp.where(lane == line, curv, 0.0).reshape(plan.leaves, 8, plan.outs)
     spread = jnp.broadcast_to(jnp.sum(spread, axis=1, keepdims=True), spread.shape)
-    score_ref[...] = jnp.where(line == 2 * plan.levels, spread.reshape(shape), sums)
+    sums = jnp.where(line == 2 * plan.levels, spread.reshape(shape), sums)
+    pieces = []
+    for _ in range(PIECES):
+        pieces.append(sums.astype(bf16).astype(f32))
+        sums = sums - pieces[-1]
+
+    half = lax.rem(panel, plan.pair)
+    word_share = plan.share // 2
+    own = [hess, nodes[-1].astype(f32)]
+    blank = jnp.zeros((1, LANES), f32)
+    filler = jnp.zeros((plan.sent_rows - plan.misc_at - plan.misc_rows, rows), f32)
+    misc = []
+    for leaf in range(plan.leaves):
+        parts = [piece[leaf * 8 + i : leaf * 8 + i + 1] for i in range(plan.score_rows) for piece in pieces]
+        parts += [blank] * (-len(parts) % plan.spans)
+        lines = [jnp.concatenate(parts[i : i + plan.spans], axis=1) for i in range(0, len(parts), plan.spans)]
+        lines += [filler] if filler.shape[0] else []
+        misc.append(jnp.concatenate(own + lines, axis=0))
+    for split in range(OUT_SPLIT):
+        start = pl.multiple_of(split * plan.outs_dev + half * plan.outs_sent, plan.outs_sent)
+        part = turned[pl.ds(start, plan.outs_sent), :]
+        for share in range(plan.shares):
+            span = slice(share * word_share, (share + 1) * word_share)
+            device = share * OUT_SPLIT + split
+            send_ref[device] = jnp.concatenate(
+                [part, codes[0][span], codes[1][span], misc[plan.leaf_of(device)]], axis=0
+            ).astype(bf16)
 
 
 def main_kernel(plan, chunk, got_ref, *refs):
-    others, (score_ref, out_ref, weighted, marks, left_sums) = refs[:-5], refs[-5:]
+    others, refs = refs[: plan.pair - 1], refs[plan.pair - 1 :]
+    out_ref, score_ref, weighted, marks, left_sums = refs
     rows = plan.row_dev
     leaves, outs_dev = plan.leaves, plan.outs_dev
     hess_at = leaves * outs_dev
@@ -191,21 +218,33 @@
                     row = level * plan.groups + group * (step // 2) + tile
                     for device in range(n * under, (n + 1) * under):
                         out_ref[device, row : row + 1, :] = piece
-    if plan.score_at > plan.gain_rows:
-        filler = jnp.zeros((plan.score_at - plan.gain_rows, LANES), f32)
+    if plan.message > plan.gain_rows:
+        filler = jnp.zeros((plan.message - plan.gain_rows, LANES), f32)
         for device in range(plan.devices):
-            out_ref[device, plan.gain_rows : plan.score_at, :] = filler
-    for device in range(plan.devices):
-        leaf = plan.leaf_of(device)
-        out_ref[device, plan.score_at : plan.score_at + 8, :] = score_ref[leaf * 8 : leaf * 8 + 8, :]
-
-
-def final_kernel(plan, place, got_ref, *outs):
-    *gain_refs, child_ref = outs
+            out_ref[device, plan.gain_rows : plan.message, :] = filler
+
+    def add_scores(source, total):
+        for ref in (got_ref, *others):
+            total = total + ref[source, plan.misc_at + 2 : plan.misc_at + plan.misc_rows, :].astype(f32)
+        return total
+
+    total = lax.fori_loop(0, plan.devices, add_scores, jnp.zeros((plan.misc_rows - 2, rows), f32))
+    score_ref[...] = jnp.zeros_like(score_ref)
+    for i in range(plan.score_rows):
+        value = 0.0
+        for piece in reversed(range(PIECES)):
+            line, span = divmod(i * PIECES + piece, plan.spans)
+            value = value + total[line : line + 1, span * LANES : (span + 1) * LANES]
+        score_ref[i : i + 1, :] = value
+
+
+def final_kernel(plan, got_ref, *refs):
+    score_refs, refs = refs[: -plan.levels - 1], refs[-plan.levels - 1 :]
+    *gain_refs, child_ref = refs
     half = plan.groups
     for level, gain_ref in enumerate(gain_refs):
         size = plan.devices >> (level + 1)
-        position = lax.rem(place[0], size)
+        position = lax.rem(lax.axis_index("rows"), size)
         count = plan.feats // size // plan.share
         for t in range(count):
             share = position * count + t
@@ -216,9 +255,9 @@
             for side in range(2):
                 at = t * plan.share + side * half
                 gain_ref[at : at + half, :] = total[:, side * BINS : (side + 1) * BINS]
-    sums = got_ref[0, plan.score_at : plan.score_at + 8, :]
-    for device in range(1, plan.devices):
-        sums = sums + got_ref[device, plan.score_at : plan.score_at + 8, :]
+    sums = score_refs[0][...]
+    for score_ref in score_refs[1:]:
+        sums = sums + score_ref[...]
     curv = sums[2 * plan.levels : 2 * plan.levels + 1, :]
     for level in range(plan.levels):
         for side in range(2):
@@ -227,45 +266,49 @@
             child_ref[level, 0, side : side + 1, :] = -sums[line : line + 1, :] / scale
 
 
+def flipped(block, bit):
+    count = lax.axis_size("feat")
+    return lax.ppermute(block, "feat", [(p, p ^ bit) for p in range(count)])
+
+
 def on_device(gradients, hessians, bin_words, children, split_feature, split_bin):
     plan = Plan(lax.axis_size("rows"), lax.axis_size("feat"), gradients, bin_words, children)
     rows = plan.row_dev
-    place = jnp.stack([lax.axis_index("rows"), lax.axis_index("feat")]).astype(jnp.int32)
     params = pltpu.CompilerParams(vmem_limit_bytes=VMEM_BYTES)
-    smem = pl.BlockSpec(memory_space=pltpu.SMEM)
-
-    send, scores = pl.pallas_call(
+
+    inputs = (gradients, hessians, bin_words, children, split_feature, split_bin)
+    inputs = tuple(pltpu.with_memory_space_constraint(a, pltpu.HBM) for a in inputs)
+    send = pl.pallas_call(
         functools.partial(prep_kernel, plan),
-        out_shape=(
-            jax.ShapeDtypeStruct((plan.devices, plan.sent_rows, rows), bf16),
-            jax.ShapeDtypeStruct((plan.leaves * 8, plan.outs), f32),
-        ),
-        in_specs=[smem, smem, smem] + [whole()] * 4,
-        out_specs=(whole(), whole()),
+        out_shape=jax.ShapeDtypeStruct((plan.devices, plan.sent_rows, rows), bf16),
+        in_specs=[pl.BlockSpec(memory_space=pltpu.HBM)] * len(inputs),
+        out_specs=whole(),
         scratch_shapes=[
+            *(pltpu.VMEM(a.shape, a.dtype) for a in inputs[:4]),
+            *(pltpu.SMEM(a.shape, a.dtype) for a in inputs[4:]),
             pltpu.VMEM((plan.leaves * 8, rows), f32),
             pltpu.VMEM((plan.outs, rows), f32),
+            pltpu.SemaphoreType.DMA((len(inputs),)),
         ],
         compiler_params=params,
         name="prep",
-    )(place, split_feature, split_bin, gradients, hessians.reshape(1, rows), bin_words, children)
-
-    scores = lax.psum(scores, "feat")
+    )(*inputs)
+
     got = lax.all_to_all(send, "rows", 0, 0)
-    arrays = [got]
-    if plan.pair > 1:
-        route = [(p, p ^ 1) for p in range(lax.axis_size("feat"))]
-        arrays.append(lax.ppermute(got, "feat", route))
+    arrays = [got] + ([flipped(got, 1)] if plan.pair > 1 else [])
 
     chunk = max(1, min(plan.devices, 4096 // rows))
     while plan.devices % chunk:
         chunk -= 1
     sums_rows = plan.leaves * plan.outs_dev + TILE
-    message = pl.pallas_call(
+    message, scores = pl.pallas_call(
         functools.partial(main_kernel, plan, chunk),
-        out_shape=jax.ShapeDtypeStruct((plan.devices, plan.message, LANES), f32),
-        in_specs=[whole()] * (len(arrays) + 1),
-        out_specs=whole(),
+        out_shape=(
+            jax.ShapeDtypeStruct((plan.devices, plan.message, LANES), f32),
+            jax.ShapeDtypeStruct((8, plan.outs), f32),
+        ),
+        in_specs=[whole()] * len(arrays),
+        out_specs=(whole(), whole()),
         scratch_shapes=[
             pltpu.VMEM((sums_rows, chunk * rows), bf16),
             pltpu.VMEM((min(4, plan.share) * BINS, chunk * rows), bf16),
@@ -273,8 +316,11 @@
         ],
         compiler_params=params,
         name="gains",
-    )(*arrays, scores)
-
+    )(*arrays)
+
+    score_parts = [scores]
+    for away in range(1, lax.axis_size("feat") // plan.pair):
+        score_parts.append(flipped(scores, away * plan.pair))
     answer = lax.all_to_all(message, "rows", 0, 0)
     shapes = [
         jax.ShapeDtypeStruct((plan.feats // (plan.devices >> (level + 1)), BINS), f32)
@@ -284,11 +330,11 @@
     return pl.pallas_call(
         functools.partial(final_kernel, plan),
         out_shape=tuple(shapes),
-        in_specs=[smem, whole()],
+        in_specs=[whole()] * (1 + len(score_parts)),
         out_specs=tuple(whole() for _ in shapes),
         compiler_params=params,
         name="finish",
-    )(place, answer)
+    )(answer, *score_parts)
 
 
 def solution(mesh):

time: 54.3 us -> 41.8 us (0.77)
  blocking collectives: 42.7 us -> 20.3 us
  waiting for transfers between devices: 0.01 us -> 7.44 us
  starting transfers between devices: 0.01 us -> 4.99 us
  local copies, waits for them, and re-layouts: 3 us -> 0 us
  Pallas kernels: 7.58 us -> 8.17 us
    psum x1 -> x0, blocking collectives: 11.7 us -> none  [on_device(): scores = lax.psum(scores, 'feat')]
    all_to_all x1 -> x0, blocking collectives: 10.6 us -> none  [on_device(): answer = lax.all_to_all(message, 'rows', 0, 0)]
    ppermute x1 -> x2, waiting for transfers between devices: 0.01 us -> 3.93 us  [flipped(): return lax.ppermute(block, 'feat', [(p, p ^ bit) for p in range(count)])]
    all_to_all x0 -> x1, waiting for transfers between devices: none -> 3.52 us  [on_device(): answer = lax.all_to_all(message, 'rows', 0, 0)]
    all_to_all x0 -> x1, starting transfers between devices: none -> 3.49 us  [on_device(): answer = lax.all_to_all(message, 'rows', 0, 0)]
    unnamed x12 -> x0, local copies, waits for them, and re-layouts: 3 us -> none
    ppermute x1 -> x2, starting transfers between devices: 0.01 us -> 1.5 us  [flipped(): return lax.ppermute(block, 'feat', [(p, p ^ bit) for p in range(count)])]
    pallas_call x2, Pallas kernels: 6.32 us -> 7.45 us  [the longest x1 6.14 us: on_device(): pl.pallas_call(functools.partial(main_kernel, plan, chunk), out_shape=(ja...]
  transfers between devices with their start and end apart: 1 -> 3, of which waited for: 0 -> 3; matrix products, arithmetic and copies ran while one was open for 0% -> 0% of each run, Pallas kernels for 0% -> 0%
where the time goes in v2:
time: 41.8 us; the launch traced here: 41.6 us
  blocking collectives  20.3 us (49%)
  Pallas kernels  8.17 us (20%)
  waiting for transfers between devices  7.44 us (18%)
  starting transfers between devices  4.99 us (12%)
  between operations  0.64 us (2%)
    all_to_all x1, blocking collectives, on_device(): got = lax.all_to_all(send, 'rows', 0, 0)  20.3 us
    pallas_call x1, Pallas kernels, on_device(): pl.pallas_call(functools.partial(main_kernel, plan, chunk), out_shape=(ja...  6.14 us
    ppermute x2, waiting for transfers between devices, flipped(): return lax.ppermute(block, 'feat', [(p, p ^ bit) for p in range(count)])  3.93 us
    all_to_all x1, waiting for transfers between devices, on_device(): answer = lax.all_to_all(message, 'rows', 0, 0)  3.52 us
    all_to_all x1, starting transfers between devices, on_device(): answer = lax.all_to_all(message, 'rows', 0, 0)  3.49 us
    ppermute x2, starting transfers between devices, flipped(): return lax.ppermute(block, 'feat', [(p, p ^ bit) for p in range(count)])  1.5 us
    pallas_call x1, Pallas kernels, on_device(): pl.pallas_call(functools.partial(prep_kernel, plan), out_shape=jax.ShapeD...  1.31 us
  transfers between devices with their start and end apart: 3, of which 3 were waited for; matrix products, arithmetic and copies ran while one was open for 0% of the time, Pallas kernels for 0%

profile of v2, /device:TPU:0, one launch (start us, length us, event | category | flops | bytes accessed | tf_op | source)
XLA Modules:
  0.0 41.6 jit_solution(13690910241953268612)
XLA Ops:
  0.6 1.3 %prep.1 = bf16[8,56,512]{2,1,0:T(8,128)(2,1)S(1)} custom-call(bf16[512,128]{1,0:T(8,128)(2,1)} %refs_0_.1, bf16[512]{0:T(512)(128)(2,1)} %refs_1_.1, s32[32,512]{1,0:T(8,128)} %refs_2_.1, s32[3,512]{1,0:T(4,128)} %refs_3_.1, s32[14]{0:T(128)} %refs_4_.1, s32[14]{0:T(128)} %refs_5_.1), custom_call_target="tpu_custom_call" | custom-call | tf_op jit(solution)/shard_map/prep/pallas_call | solution.py:281
  2.0 20.3 %all_to_all.10.got_ref = bf16[8,56,512]{2,1,0:T(8,128)(2,1)S(1)} all-to-all(bf16[8,56,512]{2,1,0:T(8,128)(2,1)S(1)} %prep.1), channel_id=1, replica_groups=mesh['rows'=8,'feat'=4] {'rows'}, dimensions={0} | all-to-all | bytes 917504 | tf_op jit(solution)/shard_map/all_to_all | solution.py:297
  22.3 0.0 collective-permute-start
  22.3 1.8 %collective-permute-done.refs_0_ = bf16[8,56,512]{2,1,0:T(8,128)(2,1)S(1)} collective-permute-done((bf16[8,56,512]{2,1,0:T(8,128)(2,1)S(1)}, bf16[8,56,512]{2,1,0:T(8,128)(2,1)S(1)}, u32[]{:S(2)}, u32[]{:S(2)}) %collective-permute-start) | collective-permute-done | bytes 458784 | tf_op jit(solution)/shard_map/ppermute | solution.py:271
  24.1 6.1 %gains.1 = (f32[8,24,128]{2,1,0:T(8,128)}, f32[8,128]{1,0:T(8,128)S(1)}) custom-call(bf16[8,56,512]{2,1,0:T(8,128)(2,1)S(1)} %all_to_all.10.got_ref, bf16[8,56,512]{2,1,0:T(8,128)(2,1)S(1)} %collective-permute-done.refs_0_), custom_call_target="tpu_custom_call" | custom-call | tf_op jit(solution)/shard_map/gains/pallas_call | solution.py:304
  30.2 3.5 %all-to-all-start.1 = ((f32[8,24,128]{2,1,0:T(8,128)}), f32[8,24,128]{2,1,0:T(8,128)S(1)}, u32[]{:S(2)}, u32[]{:S(2)}) async-start(f32[8,24,128]{2,1,0:T(8,128)} %get-tuple-element.6), calls=%async_computation.1 | async-start | bytes 196608 | tf_op jit(solution)/shard_map/all_to_all | solution.py:324
  33.7 1.5 %collective-permute-start.1 = (f32[8,128]{1,0:T(8,128)S(1)}, f32[8,128]{1,0:T(8,128)S(1)}, u32[]{:S(2)}, u32[]{:S(2)}) collective-permute-start(f32[8,128]{1,0:T(8,128)S(1)} %get-tuple-element.7.refs_0_), channel_id=1, source_target_pairs={{0,2},{1,3},{2,0},{3,1},{4,6},{5,7},{6,4},{7,5},{8,10},{9,11},{10,... | collective-permute-start | bytes 12296 | tf_op jit(solution)/shard_map/ppermute | solution.py:271
  35.2 2.1 %collective-permute-done.1.refs_1_ = f32[8,128]{1,0:T(8,128)S(1)} collective-permute-done((f32[8,128]{1,0:T(8,128)S(1)}, f32[8,128]{1,0:T(8,128)S(1)}, u32[]{:S(2)}, u32[]{:S(2)}) %collective-permute-start.1) | collective-permute-done | bytes 4128 | tf_op jit(solution)/shard_map/ppermute | solution.py:271
  37.3 3.5 %all-to-all-done.1.got_ref = f32[8,24,128]{2,1,0:T(8,128)S(1)} async-done(((f32[8,24,128]{2,1,0:T(8,128)}), f32[8,24,128]{2,1,0:T(8,128)S(1)}, u32[]{:S(2)}, u32[]{:S(2)}) %all-to-all-start.1) | async-done | bytes 98336 | tf_op jit(solution)/shard_map/all_to_all | solution.py:324
  40.8 0.7 %finish.1 = (f32[16,64]{1,0:T(8,128)}, f32[32,64]{1,0:T(8,128)}, f32[64,64]{1,0:T(8,128)}, f32[3,1,2,128]{3,2,1,0:T(2,128)}) custom-call(f32[8,24,128]{2,1,0:T(8,128)S(1)} %all-to-all-done.1.got_ref, f32[8,128]{1,0:T(8,128)S(1)} %get-tuple-element.7.refs_0_, f32[8,128]{1,0:T(8,128)S(1)} %collective-permute-done.1.refs_1_), custom_call_target="tpu_custom_call" | custom-call | tf_op jit(solution)/shard_map/finish/pallas_call | solution.py:330
Async XLA Ops:
  22.3 1.8 %collective-permute-start = (bf16[8,56,512]{2,1,0:T(8,128)(2,1)S(1)}, bf16[8,56,512]{2,1,0:T(8,128)(2,1)S(1)}, u32[]{:S(2)}, u32[]{:S(2)}) collective-permute-start(bf16[8,56,512]{2,1,0:T(8,128)(2,1)S(1)} %all_to_all.10.got_ref), channel_id=1, source_target_pairs={{0,1},{1,0},{2,3},{3,2},{4,5},{5,4},{6,7},{7,6},{8,9},{9,8},{10,11... | collective-permute-start | bytes 1376264 | tf_op jit(solution)/shard_map/ppermute | solution.py:271
  30.2 10.6 %all-to-all-start.1 = ((f32[8,24,128]{2,1,0:T(8,128)}), f32[8,24,128]{2,1,0:T(8,128)S(1)}, u32[]{:S(2)}, u32[]{:S(2)}) async-start(f32[8,24,128]{2,1,0:T(8,128)} %get-tuple-element.6), calls=%async_computation.1 | async-start | bytes 196608 | tf_op jit(solution)/shard_map/all_to_all | solution.py:324
  33.7 3.6 %collective-permute-start.1 = (f32[8,128]{1,0:T(8,128)S(1)}, f32[8,128]{1,0:T(8,128)S(1)}, u32[]{:S(2)}, u32[]{:S(2)}) collective-permute-start(f32[8,128]{1,0:T(8,128)S(1)} %get-tuple-element.7.refs_0_), channel_id=1, source_target_pairs={{0,2},{1,3},{2,0},{3,1},{4,6},{5,7},{6,4},{7,5},{8,10},{9,11},{10,... | collective-permute-start | bytes 12296 | tf_op jit(solution)/shard_map/ppermute | solution.py:271

commit v3 on v2

--- a/solution.py
+++ b/solution.py
@@ -11,7 +11,7 @@
 LANES = 128
 TILE = 16
 OUT_SPLIT = 2
-PIECES = 3
+PIECES = 2
 penalty = 1.0
 VMEM_BYTES = 32 * 2**20
 
@@ -31,12 +31,14 @@
 class Plan:
     def __init__(self, rows_axis, feat_axis, gradients, bin_words, children):
         self.devices = rows_axis
+        self.half = rows_axis // 2
         self.row_dev, self.outs = gradients.shape
         self.words = bin_words.shape[0]
         self.feats = 2 * self.words
         self.levels = children.shape[0]
-        self.leaves = 2**self.levels
-        self.shares = rows_axis // OUT_SPLIT
+        self.leaves = 2 ** (self.levels - 1)
+        self.slots = round_up(self.row_dev * 3 // 4, LANES)
+        self.shares = self.half // OUT_SPLIT
         self.share = self.feats // self.shares
         self.outs_dev = self.outs // OUT_SPLIT
         self.pair = 2 if feat_axis % 2 == 0 else 1
@@ -44,16 +46,22 @@
         self.code_at = self.outs_sent
         self.misc_at = self.outs_sent + self.share
         self.score_rows = 2 * self.levels + 1
-        self.spans = self.row_dev // LANES
+        self.spans = self.slots // LANES
         self.misc_rows = 2 + -(-self.score_rows * PIECES // self.spans)
         self.sent_rows = round_up(self.misc_at + self.misc_rows, 8)
-        self.groups = self.share // 2
-        self.gain_rows = self.levels * self.groups
+        self.sizes = [self.devices >> (level + 1) for level in range(self.levels)]
+        self.returned = [self.feats // size for size in self.sizes]
+        self.needed = [min(self.share, count) for count in self.returned]
+        self.block = min(self.needed)
+        self.step = min(4, self.share)
+        self.tiles = [
+            (start + k, start + k + self.block // 2)
+            for start in range(0, self.share, self.block)
+            for k in range(self.block // 2)
+        ]
+        self.level_at = [sum(self.needed[:level]) // 2 for level in range(self.levels)]
+        self.gain_rows = sum(self.needed) // 2
         self.message = round_up(self.gain_rows, 8)
-        self.top_bit = rows_axis.bit_length() - 1
-
-    def leaf_of(self, device):
-        return device >> (self.top_bit - self.levels)
 
     def code_row(self, feature):
         return self.code_at + feature // 2 + (feature % 2) * (self.share // 2)
@@ -61,7 +69,7 @@
 
 def prep_kernel(plan, *refs):
     inputs, send_ref, refs = refs[:6], refs[6], refs[7:]
-    fetched, (masks, turned, sems) = refs[:6], refs[6:]
+    fetched, (masks, table, packed, sems) = refs[:6], refs[6:]
     copies = [
         pltpu.make_async_copy(source, target, sems.at[i])
         for i, (source, target) in enumerate(zip(inputs, fetched, strict=True))
@@ -89,9 +97,26 @@
         1.0,
         0.0,
     ).astype(bf16)
-    turned[...] = lax.dot_general(unit, grads, NT, preferred_element_type=f32)
+    low_at, high_at, own_at = plan.outs, plan.outs + plan.words, plan.outs + plan.feats
+    table[0:low_at] = lax.dot_general(unit, grads, NT, preferred_element_type=f32).astype(bf16)
+    table[low_at:high_at] = low.astype(f32).astype(bf16)
+    table[high_at:own_at] = high.astype(f32).astype(bf16)
+    at = lax.broadcasted_iota(jnp.int32, (TILE, rows), 0)
+    leaf = jnp.bitwise_and(nodes[-1], plan.leaves - 1).astype(f32)
+    table[own_at:] = jnp.where(at == 0, hess, jnp.where(at == 1, leaf, 0.0)).astype(bf16)
+    side = jnp.where(at == nodes[0], 1.0, 0.0)
+    ahead = jnp.where(
+        lax.broadcasted_iota(jnp.int32, (rows, rows), 0) <= lax.broadcasted_iota(jnp.int32, (rows, rows), 1), 1.0, 0.0
+    )
+    rank = jnp.dot(side.astype(bf16), ahead.astype(bf16), preferred_element_type=f32)
+    slot = jnp.where(side > 0.0, rank - 1.0, -1.0)
+    slot_ids = lax.broadcasted_iota(jnp.int32, (plan.slots, rows), 0).astype(f32)
+    for half in range(2):
+        chosen = jnp.where(slot_ids == slot[half : half + 1], 1.0, 0.0).astype(bf16)
+        packed[half] = lax.dot_general(table[...], chosen, NT, preferred_element_type=f32)
 
     masks[...] = jnp.zeros_like(masks)
+    leaf_count = 2 * plan.leaves
     for level in range(plan.levels):
         for node in range(2 ** (level + 1)):
             slot = 2 ** (level + 1) - 2 + node
@@ -112,10 +137,10 @@
     mask = masks[...]
     sums = jnp.dot(mask.astype(bf16), grads, preferred_element_type=f32)
     curv = jnp.sum(mask * hess, axis=1, keepdims=True)
-    shape = (plan.leaves * 8, plan.outs)
+    shape = (leaf_count * 8, plan.outs)
     line = jnp.bitwise_and(lax.broadcasted_iota(jnp.int32, shape, 0), 7)
     lane = lax.broadcasted_iota(jnp.int32, shape, 1)
-    spread = jnp.where(lane == line, curv, 0.0).reshape(plan.leaves, 8, plan.outs)
+    spread = jnp.where(lane == line, curv, 0.0).reshape(leaf_count, 8, plan.outs)
     spread = jnp.broadcast_to(jnp.sum(spread, axis=1, keepdims=True), spread.shape)
     sums = jnp.where(line == 2 * plan.levels, spread.reshape(shape), sums)
     pieces = []
@@ -123,37 +148,40 @@
         pieces.append(sums.astype(bf16).astype(f32))
         sums = sums - pieces[-1]
 
-    half = lax.rem(panel, plan.pair)
+    parity = lax.rem(panel, plan.pair)
     word_share = plan.share // 2
-    own = [hess, nodes[-1].astype(f32)]
     blank = jnp.zeros((1, LANES), f32)
-    filler = jnp.zeros((plan.sent_rows - plan.misc_at - plan.misc_rows, rows), f32)
-    misc = []
-    for leaf in range(plan.leaves):
+    filler = jnp.zeros((plan.sent_rows - plan.misc_at - plan.misc_rows, plan.slots), f32)
+    lines = []
+    for leaf in range(leaf_count):
         parts = [piece[leaf * 8 + i : leaf * 8 + i + 1] for i in range(plan.score_rows) for piece in pieces]
         parts += [blank] * (-len(parts) % plan.spans)
-        lines = [jnp.concatenate(parts[i : i + plan.spans], axis=1) for i in range(0, len(parts), plan.spans)]
-        lines += [filler] if filler.shape[0] else []
-        misc.append(jnp.concatenate(own + lines, axis=0))
-    for split in range(OUT_SPLIT):
-        start = pl.multiple_of(split * plan.outs_dev + half * plan.outs_sent, plan.outs_sent)
-        part = turned[pl.ds(start, plan.outs_sent), :]
-        for share in range(plan.shares):
-            span = slice(share * word_share, (share + 1) * word_share)
-            device = share * OUT_SPLIT + split
-            send_ref[device] = jnp.concatenate(
-                [part, codes[0][span], codes[1][span], misc[plan.leaf_of(device)]], axis=0
-            ).astype(bf16)
+        parts = [jnp.concatenate(parts[i : i + plan.spans], axis=1) for i in range(0, len(parts), plan.spans)]
+        lines.append(jnp.concatenate(parts + ([filler] if filler.shape[0] else []), axis=0))
+    for device in range(plan.devices):
+        half, place = divmod(device, plan.half)
+        share, split = divmod(place, OUT_SPLIT)
+        start = pl.multiple_of(split * plan.outs_dev + parity * plan.outs_sent, plan.outs_sent)
+        low_from, high_from = low_at + share * word_share, high_at + share * word_share
+        send_ref[device] = jnp.concatenate(
+            [
+                packed[half, pl.ds(start, plan.outs_sent), :],
+                packed[half, low_from : low_from + word_share, :],
+                packed[half, high_from : high_from + word_share, :],
+                packed[half, own_at : own_at + 2, :],
+                lines[device * leaf_count // plan.devices],
+            ],
+            axis=0,
+        ).astype(bf16)
 
 
 def main_kernel(plan, chunk, got_ref, *refs):
     others, refs = refs[: plan.pair - 1], refs[plan.pair - 1 :]
     out_ref, score_ref, weighted, marks, left_sums = refs
-    rows = plan.row_dev
-    leaves, outs_dev = plan.leaves, plan.outs_dev
+    rows = plan.slots
+    leaves, outs_dev, step = plan.leaves, plan.outs_dev, plan.step
     hess_at = leaves * outs_dev
-    step = min(4, plan.share)
-    order = [feature for k in range(plan.groups) for feature in (k, k + plan.groups)]
+    order = [feature for tile in plan.tiles for feature in tile]
     level_bins = lax.broadcasted_iota(jnp.int32, (BINS, rows), 0).astype(f32).astype(bf16)
     leaf_ids = lax.broadcasted_iota(jnp.int32, (TILE, rows), 0).astype(f32)
     zero = jnp.zeros((), bf16)
@@ -184,22 +212,18 @@
                     )
             part = lax.dot_general(weighted[...], marks[...], NT, preferred_element_type=f32)
             span = slice(group * step * BINS, (group + 1) * step * BINS)
-            if fresh:
+            if count == 1:
+                add_gains(group, part)
+            elif fresh:
                 left_sums[:, span] = part
             else:
                 left_sums[:, span] += part
 
-    add_chunk(0, True)
-    count = plan.devices // chunk
-    if count > 1:
-        lax.fori_loop(1, count, lambda c, _: (add_chunk(c * chunk, False), 0)[1], 0)
-
-    for group in range(plan.share // step):
-        span = slice(group * step * BINS, (group + 1) * step * BINS)
-        left = [left_sums[leaf * outs_dev : (leaf + 1) * outs_dev, span] for leaf in range(leaves)]
-        hess = [left_sums[hess_at + leaf : hess_at + leaf + 1, span] for leaf in range(leaves)]
+    def add_gains(group, sums):
+        left = [sums[leaf * outs_dev : (leaf + 1) * outs_dev] for leaf in range(leaves)]
+        hess = [sums[hess_at + leaf : hess_at + leaf + 1] for leaf in range(leaves)]
         for level in reversed(range(plan.levels)):
-            nodes = 2 ** (level + 1)
+            nodes = 2**level
             if level < plan.levels - 1:
                 left = [left[2 * n] + left[2 * n + 1] for n in range(nodes)]
                 hess = [hess[2 * n] + hess[2 * n + 1] for n in range(nodes)]
@@ -212,15 +236,25 @@
                     + jnp.sum(right * right, axis=0, keepdims=True) / (hess_total - hess[n] + penalty)
                     - jnp.sum(total * total, axis=0, keepdims=True) / (hess_total + penalty)
                 ) / plan.outs
-                under = plan.devices // nodes
+                size = plan.sizes[level]
                 for tile in range(step // 2):
                     piece = gain[:, tile * LANES : (tile + 1) * LANES]
-                    row = level * plan.groups + group * (step // 2) + tile
-                    for device in range(n * under, (n + 1) * under):
-                        out_ref[device, row : row + 1, :] = piece
+                    for place in range(size):
+                        first = place * plan.returned[level] % plan.share // 2
+                        line = group * (step // 2) + tile - first
+                        if 0 <= line < plan.needed[level] // 2:
+                            row = plan.level_at[level] + line
+                            out_ref[n * size + place, row : row + 1, :] = piece
+
+    count = plan.devices // chunk
+    add_chunk(0, True)
+    if count > 1:
+        lax.fori_loop(1, count, lambda c, _: (add_chunk(c * chunk, False), 0)[1], 0)
+        for group in range(plan.share // step):
+            add_gains(group, left_sums[:, group * step * BINS : (group + 1) * step * BINS])
     if plan.message > plan.gain_rows:
         filler = jnp.zeros((plan.message - plan.gain_rows, LANES), f32)
-        for device in range(plan.devices):
+        for device in range(plan.half):
             out_ref[device, plan.gain_rows : plan.message, :] = filler
 
     def add_scores(source, total):
@@ -241,20 +275,20 @@
 def final_kernel(plan, got_ref, *refs):
     score_refs, refs = refs[: -plan.levels - 1], refs[-plan.levels - 1 :]
     *gain_refs, child_ref = refs
-    half = plan.groups
+    side = plan.block // 2
     for level, gain_ref in enumerate(gain_refs):
-        size = plan.devices >> (level + 1)
-        position = lax.rem(lax.axis_index("rows"), size)
-        count = plan.feats // size // plan.share
-        for t in range(count):
-            share = position * count + t
-            rows = slice(level * half, (level + 1) * half)
+        position = lax.rem(lax.axis_index("rows"), plan.sizes[level])
+        for t in range(plan.returned[level] // plan.needed[level]):
+            share = (position * plan.returned[level] + t * plan.share) // plan.share
+            rows = slice(plan.level_at[level], plan.level_at[level] + plan.needed[level] // 2)
             total = got_ref[share * OUT_SPLIT, rows, :]
             for split in range(1, OUT_SPLIT):
                 total = total + got_ref[share * OUT_SPLIT + split, rows, :]
-            for side in range(2):
-                at = t * plan.share + side * half
-                gain_ref[at : at + half, :] = total[:, side * BINS : (side + 1) * BINS]
+            for start in range(0, plan.needed[level], plan.block):
+                part = total[start // 2 : start // 2 + side]
+                at = t * plan.share + start
+                gain_ref[at : at + side, :] = part[:, :BINS]
+                gain_ref[at + side : at + 2 * side, :] = part[:, BINS:]
     sums = score_refs[0][...]
     for score_ref in score_refs[1:]:
         sums = sums + score_ref[...]
@@ -273,21 +307,21 @@
 
 def on_device(gradients, hessians, bin_words, children, split_feature, split_bin):
     plan = Plan(lax.axis_size("rows"), lax.axis_size("feat"), gradients, bin_words, children)
-    rows = plan.row_dev
     params = pltpu.CompilerParams(vmem_limit_bytes=VMEM_BYTES)
 
     inputs = (gradients, hessians, bin_words, children, split_feature, split_bin)
     inputs = tuple(pltpu.with_memory_space_constraint(a, pltpu.HBM) for a in inputs)
     send = pl.pallas_call(
         functools.partial(prep_kernel, plan),
-        out_shape=jax.ShapeDtypeStruct((plan.devices, plan.sent_rows, rows), bf16),
+        out_shape=jax.ShapeDtypeStruct((plan.devices, plan.sent_rows, plan.slots), bf16),
         in_specs=[pl.BlockSpec(memory_space=pltpu.HBM)] * len(inputs),
         out_specs=whole(),
         scratch_shapes=[
             *(pltpu.VMEM(a.shape, a.dtype) for a in inputs[:4]),
             *(pltpu.SMEM(a.shape, a.dtype) for a in inputs[4:]),
-            pltpu.VMEM((plan.leaves * 8, rows), f32),
-            pltpu.VMEM((plan.outs, rows), f32),
+            pltpu.VMEM((2 * plan.leaves * 8, plan.row_dev), f32),
+            pltpu.VMEM((plan.outs + plan.feats + TILE, plan.row_dev), bf16),
+            pltpu.VMEM((2, plan.outs + plan.feats + TILE, plan.slots), f32),
             pltpu.SemaphoreType.DMA((len(inputs),)),
         ],
         compiler_params=params,
@@ -297,21 +331,21 @@
     got = lax.all_to_all(send, "rows", 0, 0)
     arrays = [got] + ([flipped(got, 1)] if plan.pair > 1 else [])
 
-    chunk = max(1, min(plan.devices, 4096 // rows))
+    chunk = max(1, min(plan.devices, 4096 // plan.slots))
     while plan.devices % chunk:
         chunk -= 1
     sums_rows = plan.leaves * plan.outs_dev + TILE
     message, scores = pl.pallas_call(
         functools.partial(main_kernel, plan, chunk),
         out_shape=(
-            jax.ShapeDtypeStruct((plan.devices, plan.message, LANES), f32),
+            jax.ShapeDtypeStruct((plan.half, plan.message, LANES), f32),
             jax.ShapeDtypeStruct((8, plan.outs), f32),
         ),
         in_specs=[whole()] * len(arrays),
         out_specs=(whole(), whole()),
         scratch_shapes=[
-            pltpu.VMEM((sums_rows, chunk * rows), bf16),
-            pltpu.VMEM((min(4, plan.share) * BINS, chunk * rows), bf16),
+            pltpu.VMEM((sums_rows, chunk * plan.slots), bf16),
+            pltpu.VMEM((plan.step * BINS, chunk * plan.slots), bf16),
             pltpu.VMEM((sums_rows, plan.share * BINS), f32),
         ],
         compiler_params=params,
@@ -321,10 +355,10 @@
     score_parts = [scores]
     for away in range(1, lax.axis_size("feat") // plan.pair):
         score_parts.append(flipped(scores, away * plan.pair))
-    answer = lax.all_to_all(message, "rows", 0, 0)
+    halves = [list(range(plan.half)), list(range(plan.half, plan.devices))]
+    answer = lax.all_to_all(message, "rows", 0, 0, axis_index_groups=halves)
     shapes = [
-        jax.ShapeDtypeStruct((plan.feats // (plan.devices >> (level + 1)), BINS), f32)
-        for level in range(plan.levels)
+        jax.ShapeDtypeStruct((count, BINS), f32) for count in plan.returned
     ]
     shapes.append(jax.ShapeDtypeStruct((plan.levels, 1, 2, plan.outs), f32))
     return pl.pallas_call(

time: 41.8 us -> 39.2 us (0.938)
  waiting for transfers between devices: 7.44 us -> 5.08 us
    all_to_all x1, waiting for transfers between devices: 3.52 us -> 1.18 us  [on_device(): answer = lax.all_to_all(message, 'rows', 0, 0, axis_index_groups=halves)]
where the time goes in v3:
time: 39.2 us; the launch traced here: 38.9 us
  blocking collectives  20 us (51%)
  Pallas kernels  8.29 us (21%)
  waiting for transfers between devices  5.08 us (13%)
  starting transfers between devices  4.86 us (12%)
  between operations  0.65 us (2%)
    all_to_all x1, blocking collectives, on_device(): got = lax.all_to_all(send, 'rows', 0, 0)  20 us
    pallas_call x1, Pallas kernels, on_device(): pl.pallas_call(functools.partial(main_kernel, plan, chunk), out_shape=(ja...  5.86 us
    ppermute x2, waiting for transfers between devices, flipped(): return lax.ppermute(block, 'feat', [(p, p ^ bit) for p in range(count)])  3.9 us
    all_to_all x1, starting transfers between devices, on_device(): answer = lax.all_to_all(message, 'rows', 0, 0, axis_index_groups=halves)  3.29 us
    pallas_call x1, Pallas kernels, on_device(): pl.pallas_call(functools.partial(prep_kernel, plan), out_shape=jax.ShapeD...  1.71 us
    ppermute x2, starting transfers between devices, flipped(): return lax.ppermute(block, 'feat', [(p, p ^ bit) for p in range(count)])  1.56 us
    all_to_all x1, waiting for transfers between devices, on_device(): answer = lax.all_to_all(message, 'rows', 0, 0, axis_index_groups=halves)  1.18 us
  transfers between devices with their start and end apart: 3, of which 3 were waited for; matrix products, arithmetic and copies ran while one was open for 0% of the time, Pallas kernels for 0%

profile of v3, /device:TPU:0, one launch (start us, length us, event | category | flops | bytes accessed | tf_op | source)
XLA Modules:
  0.0 38.9 jit_solution(12467020617371492227)
XLA Ops:
  0.6 1.7 %prep.1 = bf16[8,72,384]{2,1,0:T(8,128)(2,1)S(1)} custom-call(bf16[512,128]{1,0:T(8,128)(2,1)} %refs_0_.1, bf16[512]{0:T(512)(128)(2,1)} %refs_1_.1, s32[32,512]{1,0:T(8,128)} %refs_2_.1, s32[3,512]{1,0:T(4,128)} %refs_3_.1, s32[14]{0:T(128)} %refs_4_.1, s32[14]{0:T(128)} %refs_5_.1), custom_call_target="tpu_custom_call" | custom-call | tf_op jit(solution)/shard_map/prep/pallas_call | solution.py:314
  2.4 20.0 %all_to_all.10.got_ref = bf16[8,72,384]{2,1,0:T(8,128)(2,1)S(1)} all-to-all(bf16[8,72,384]{2,1,0:T(8,128)(2,1)S(1)} %prep.1), channel_id=1, replica_groups=mesh['rows'=8,'feat'=4] {'rows'}, dimensions={0} | all-to-all | bytes 884736 | tf_op jit(solution)/shard_map/all_to_all | solution.py:331
  22.4 0.0 collective-permute-start
  22.4 1.8 %collective-permute-done.refs_0_ = bf16[8,72,384]{2,1,0:T(8,128)(2,1)S(1)} collective-permute-done((bf16[8,72,384]{2,1,0:T(8,128)(2,1)S(1)}, bf16[8,72,384]{2,1,0:T(8,128)(2,1)S(1)}, u32[]{:S(2)}, u32[]{:S(2)}) %collective-permute-start) | collective-permute-done | bytes 442400 | tf_op jit(solution)/shard_map/ppermute | solution.py:305
  24.2 5.9 %gains.1 = (f32[4,40,128]{2,1,0:T(8,128)}, f32[8,128]{1,0:T(8,128)S(1)}) custom-call(bf16[8,72,384]{2,1,0:T(8,128)(2,1)S(1)} %all_to_all.10.got_ref, bf16[8,72,384]{2,1,0:T(8,128)(2,1)S(1)} %collective-permute-done.refs_0_), custom_call_target="tpu_custom_call" | custom-call | tf_op jit(solution)/shard_map/gains/pallas_call | solution.py:338
  30.0 3.3 %all-to-all-start.1 = ((f32[4,40,128]{2,1,0:T(8,128)}), f32[4,40,128]{2,1,0:T(8,128)S(1)}, u32[]{:S(2)}, u32[]{:S(2)}) async-start(f32[4,40,128]{2,1,0:T(8,128)} %get-tuple-element.6), calls=%async_computation.1 | async-start | bytes 163840 | tf_op jit(solution)/shard_map/all_to_all | solution.py:359
  33.3 1.6 %collective-permute-start.1 = (f32[8,128]{1,0:T(8,128)S(1)}, f32[8,128]{1,0:T(8,128)S(1)}, u32[]{:S(2)}, u32[]{:S(2)}) collective-permute-start(f32[8,128]{1,0:T(8,128)S(1)} %get-tuple-element.7.refs_0_), channel_id=1, source_target_pairs={{0,2},{1,3},{2,0},{3,1},{4,6},{5,7},{6,4},{7,5},{8,10},{9,11},{10,... | collective-permute-start | bytes 12296 | tf_op jit(solution)/shard_map/ppermute | solution.py:305
  34.9 2.1 %collective-permute-done.1.refs_1_ = f32[8,128]{1,0:T(8,128)S(1)} collective-permute-done((f32[8,128]{1,0:T(8,128)S(1)}, f32[8,128]{1,0:T(8,128)S(1)}, u32[]{:S(2)}, u32[]{:S(2)}) %collective-permute-start.1) | collective-permute-done | bytes 4128 | tf_op jit(solution)/shard_map/ppermute | solution.py:305
  37.0 1.2 %all-to-all-done.1.got_ref = f32[4,40,128]{2,1,0:T(8,128)S(1)} async-done(((f32[4,40,128]{2,1,0:T(8,128)}), f32[4,40,128]{2,1,0:T(8,128)S(1)}, u32[]{:S(2)}, u32[]{:S(2)}) %all-to-all-start.1) | async-done | bytes 81952 | tf_op jit(solution)/shard_map/all_to_all | solution.py:359
  38.2 0.7 %finish.1 = (f32[16,64]{1,0:T(8,128)}, f32[32,64]{1,0:T(8,128)}, f32[64,64]{1,0:T(8,128)}, f32[3,1,2,128]{3,2,1,0:T(2,128)}) custom-call(f32[4,40,128]{2,1,0:T(8,128)S(1)} %all-to-all-done.1.got_ref, f32[8,128]{1,0:T(8,128)S(1)} %get-tuple-element.7.refs_0_, f32[8,128]{1,0:T(8,128)S(1)} %collective-permute-done.1.refs_1_), custom_call_target="tpu_custom_call" | custom-call | tf_op jit(solution)/shard_map/finish/pallas_call | solution.py:364
Async XLA Ops:
  22.4 1.8 %collective-permute-start = (bf16[8,72,384]{2,1,0:T(8,128)(2,1)S(1)}, bf16[8,72,384]{2,1,0:T(8,128)(2,1)S(1)}, u32[]{:S(2)}, u32[]{:S(2)}) collective-permute-start(bf16[8,72,384]{2,1,0:T(8,128)(2,1)S(1)} %all_to_all.10.got_ref), channel_id=1, source_target_pairs={{0,1},{1,0},{2,3},{3,2},{4,5},{5,4},{6,7},{7,6},{8,9},{9,8},{10,11... | collective-permute-start | bytes 1327112 | tf_op jit(solution)/shard_map/ppermute | solution.py:305
  30.0 8.2 %all-to-all-start.1 = ((f32[4,40,128]{2,1,0:T(8,128)}), f32[4,40,128]{2,1,0:T(8,128)S(1)}, u32[]{:S(2)}, u32[]{:S(2)}) async-start(f32[4,40,128]{2,1,0:T(8,128)} %get-tuple-element.6), calls=%async_computation.1 | async-start | bytes 163840 | tf_op jit(solution)/shard_map/all_to_all | solution.py:359
  33.3 3.7 %collective-permute-start.1 = (f32[8,128]{1,0:T(8,128)S(1)}, f32[8,128]{1,0:T(8,128)S(1)}, u32[]{:S(2)}, u32[]{:S(2)}) collective-permute-start(f32[8,128]{1,0:T(8,128)S(1)} %get-tuple-element.7.refs_0_), channel_id=1, source_target_pairs={{0,2},{1,3},{2,0},{3,1},{4,6},{5,7},{6,4},{7,5},{8,10},{9,11},{10,... | collective-permute-start | bytes 12296 | tf_op jit(solution)/shard_map/ppermute | solution.py:305

commit v4 on v3

--- a/solution.py
+++ b/solution.py
@@ -53,7 +53,7 @@
         self.returned = [self.feats // size for size in self.sizes]
         self.needed = [min(self.share, count) for count in self.returned]
         self.block = min(self.needed)
-        self.step = min(4, self.share)
+        self.step = min(8, self.share)
         self.tiles = [
             (start + k, start + k + self.block // 2)
             for start in range(0, self.share, self.block)
@@ -177,7 +177,7 @@
 
 def main_kernel(plan, chunk, got_ref, *refs):
     others, refs = refs[: plan.pair - 1], refs[plan.pair - 1 :]
-    out_ref, score_ref, weighted, marks, left_sums = refs
+    out_ref, weighted, left_sums = refs
     rows = plan.slots
     leaves, outs_dev, step = plan.leaves, plan.outs_dev, plan.step
     hess_at = leaves * outs_dev
@@ -186,6 +186,11 @@
     leaf_ids = lax.broadcasted_iota(jnp.int32, (TILE, rows), 0).astype(f32)
     zero = jnp.zeros((), bf16)
     one = jnp.ones((), bf16)
+
+    def marked(source, feature):
+        row = plan.code_row(feature)
+        code = jnp.broadcast_to(got_ref[source, row : row + 1, :], (BINS, rows))
+        return jnp.where(code <= level_bins, one, zero)
 
     def add_chunk(first, fresh):
         for k in range(chunk):
@@ -203,14 +208,15 @@
                         node_wide == jnp.asarray(leaf, bf16), grads, zero
                     )
         for group in range(plan.share // step):
-            for k in range(chunk):
-                for place, feature in enumerate(order[group * step : (group + 1) * step]):
-                    row = plan.code_row(feature)
-                    code = got_ref[first + k, row : row + 1, :]
-                    marks[place * BINS : (place + 1) * BINS, k * rows : (k + 1) * rows] = jnp.where(
-                        jnp.broadcast_to(code, (BINS, rows)) <= level_bins, one, zero
-                    )
-            part = lax.dot_general(weighted[...], marks[...], NT, preferred_element_type=f32)
+            features = order[group * step : (group + 1) * step]
+            marks = jnp.concatenate(
+                [
+                    jnp.concatenate([marked(first + k, feature) for feature in features], axis=0)
+                    for k in range(chunk)
+                ],
+                axis=1,
+            )
+            part = lax.dot_general(weighted[...], marks, NT, preferred_element_type=f32)
             span = slice(group * step * BINS, (group + 1) * step * BINS)
             if count == 1:
                 add_gains(group, part)
@@ -219,32 +225,38 @@
             else:
                 left_sums[:, span] += part
 
+    known = []
+
     def add_gains(group, sums):
         left = [sums[leaf * outs_dev : (leaf + 1) * outs_dev] for leaf in range(leaves)]
         hess = [sums[hess_at + leaf : hess_at + leaf + 1] for leaf in range(leaves)]
-        for level in reversed(range(plan.levels)):
-            nodes = 2**level
-            if level < plan.levels - 1:
-                left = [left[2 * n] + left[2 * n + 1] for n in range(nodes)]
-                hess = [hess[2 * n] + hess[2 * n + 1] for n in range(nodes)]
-            for n in range(nodes):
-                total = left[n][:, BINS - 1 : BINS]
-                hess_total = hess[n][:, BINS - 1 : BINS]
-                right = total - left[n]
-                gain = (
-                    jnp.sum(left[n] * left[n], axis=0, keepdims=True) / (hess[n] + penalty)
-                    + jnp.sum(right * right, axis=0, keepdims=True) / (hess_total - hess[n] + penalty)
-                    - jnp.sum(total * total, axis=0, keepdims=True) / (hess_total + penalty)
-                ) / plan.outs
-                size = plan.sizes[level]
-                for tile in range(step // 2):
-                    piece = gain[:, tile * LANES : (tile + 1) * LANES]
-                    for place in range(size):
-                        first = place * plan.returned[level] % plan.share // 2
-                        line = group * (step // 2) + tile - first
-                        if 0 <= line < plan.needed[level] // 2:
-                            row = plan.level_at[level] + line
-                            out_ref[n * size + place, row : row + 1, :] = piece
+        ends = [(level, n) for level in reversed(range(plan.levels)) for n in range(2**level)]
+        for level in reversed(range(plan.levels - 1)):
+            past = len(left) - 2 ** (level + 1)
+            for n in range(past, len(left), 2):
+                left.append(left[n] + left[n + 1])
+                hess.append(hess[n] + hess[n + 1])
+        hess = jnp.concatenate(hess, axis=0) + penalty
+        if not known:
+            totals = [part[:, BINS - 1 : BINS] for part in left]
+            squares = jnp.concatenate([jnp.sum(t * t, axis=0, keepdims=True) for t in totals], axis=0)
+            hess_total = hess[:, BINS - 1 : BINS] + penalty
+            known.extend([totals, hess_total, squares / (hess_total - penalty)])
+        totals, hess_total, whole_part = known
+        on_left = jnp.concatenate([jnp.sum(part * part, axis=0, keepdims=True) for part in left], axis=0)
+        rights = [t - part for t, part in zip(totals, left, strict=True)]
+        on_right = jnp.concatenate([jnp.sum(part * part, axis=0, keepdims=True) for part in rights], axis=0)
+        gains = (on_left / hess + on_right / (hess_total - hess) - whole_part) / plan.outs
+        for line_at, (level, n) in enumerate(ends):
+            size = plan.sizes[level]
+            for tile in range(step // 2):
+                piece = gains[line_at : line_at + 1, tile * LANES : (tile + 1) * LANES]
+                for place in range(size):
+                    first = place * plan.returned[level] % plan.share // 2
+                    line = group * (step // 2) + tile - first
+                    if 0 <= line < plan.needed[level] // 2:
+                        row = plan.level_at[level] + line
+                        out_ref[n * size + place, row : row + 1, :] = piece
 
     count = plan.devices // chunk
     add_chunk(0, True)
@@ -257,12 +269,12 @@
         for device in range(plan.half):
             out_ref[device, plan.gain_rows : plan.message, :] = filler
 
-    def add_scores(source, total):
-        for ref in (got_ref, *others):
-            total = total + ref[source, plan.misc_at + 2 : plan.misc_at + plan.misc_rows, :].astype(f32)
-        return total
-
-    total = lax.fori_loop(0, plan.devices, add_scores, jnp.zeros((plan.misc_rows - 2, rows), f32))
+
+def score_kernel(plan, got_ref, score_ref):
+    def add(source, total):
+        return total + got_ref[source, plan.misc_at + 2 : plan.misc_at + plan.misc_rows, :].astype(f32)
+
+    total = lax.fori_loop(0, plan.devices, add, jnp.zeros((plan.misc_rows - 2, plan.slots), f32))
     score_ref[...] = jnp.zeros_like(score_ref)
     for i in range(plan.score_rows):
         value = 0.0
@@ -330,31 +342,39 @@
 
     got = lax.all_to_all(send, "rows", 0, 0)
     arrays = [got] + ([flipped(got, 1)] if plan.pair > 1 else [])
+    scores = pl.pallas_call(
+        functools.partial(score_kernel, plan),
+        out_shape=jax.ShapeDtypeStruct((8, plan.outs), f32),
+        in_specs=[whole()],
+        out_specs=whole(),
+        compiler_params=params,
+        name="scores",
+    )(got)
+    score_parts = [scores] + [flipped(scores, away) for away in range(1, lax.axis_size("feat"))]
 
     chunk = max(1, min(plan.devices, 4096 // plan.slots))
     while plan.devices % chunk:
         chunk -= 1
     sums_rows = plan.leaves * plan.outs_dev + TILE
-    message, scores = pl.pallas_call(
+    message = pl.pallas_call(
         functools.partial(main_kernel, plan, chunk),
-        out_shape=(
-            jax.ShapeDtypeStruct((plan.half, plan.message, LANES), f32),
-            jax.ShapeDtypeStruct((8, plan.outs), f32),
-        ),
+        out_shape=jax.ShapeDtypeStruct((plan.half, plan.message, LANES), f32),
         in_specs=[whole()] * len(arrays),
-        out_specs=(whole(), whole()),
+        out_specs=whole(),
         scratch_shapes=[
             pltpu.VMEM((sums_rows, chunk * plan.slots), bf16),
-            pltpu.VMEM((plan.step * BINS, chunk * plan.slots), bf16),
             pltpu.VMEM((sums_rows, plan.share * BINS), f32),
         ],
+        cost_estimate=pl.CostEstimate(
+            flops=2 * sums_rows * plan.devices * plan.slots * plan.share * BINS,
+            bytes_accessed=4 * plan.devices * plan.sent_rows * plan.slots,
+            transcendentals=0,
+        ),
         compiler_params=params,
         name="gains",
     )(*arrays)
 
-    score_parts = [scores]
-    for away in range(1, lax.axis_size("feat") // plan.pair):
-        score_parts.append(flipped(scores, away * plan.pair))
+    message, *score_parts = lax.optimization_barrier((message, *score_parts))
     halves = [list(range(plan.half)), list(range(plan.half, plan.devices))]
     answer = lax.all_to_all(message, "rows", 0, 0, axis_index_groups=halves)
     shapes = [

time: 39.2 us -> 37.2 us (0.949)
  blocking collectives: 20 us -> 27.4 us
  waiting for transfers between devices: 5.08 us -> 0.01 us
  starting transfers between devices: 4.86 us -> 2.07 us
  Pallas kernels: 8.29 us -> 6.83 us
    all_to_all x0 -> x1, blocking collectives: none -> 7.37 us  [on_device(): answer = lax.all_to_all(message, 'rows', 0, 0, axis_index_groups=halves)]
    ppermute x2 -> x4, waiting for transfers between devices: 3.9 us -> 0.01 us  [flipped(): return lax.ppermute(block, 'feat', [(p, p ^ bit) for p in range(count)])]
    all_to_all x1 -> x0, starting transfers between devices: 3.29 us -> none  [on_device(): answer = lax.all_to_all(message, 'rows', 0, 0, axis_index_groups=halves)]
    pallas_call x1 -> x2, Pallas kernels: 5.86 us -> 4.39 us  [the longest x1 4.36 us: on_device(): pl.pallas_call(functools.partial(main_kernel, plan, chunk), out_shape=jax...]
    all_to_all x1 -> x0, waiting for transfers between devices: 1.18 us -> none  [on_device(): answer = lax.all_to_all(message, 'rows', 0, 0, axis_index_groups=halves)]
    ppermute x2 -> x4, starting transfers between devices: 1.56 us -> 2.07 us  [flipped(): return lax.ppermute(block, 'feat', [(p, p ^ bit) for p in range(count)])]
  transfers between devices with their start and end apart: 3 -> 4, of which waited for: 3 -> 0; matrix products, arithmetic and copies ran while one was open for 0% -> 0% of each run, Pallas kernels for 0% -> 12%
where the time goes in v4:
time: 37.2 us; the launch traced here: 37 us
  blocking collectives  27.4 us (74%)
  Pallas kernels  6.83 us (18%)
  starting transfers between devices  2.07 us (6%)
  between operations  0.68 us (2%)
    all_to_all x1, blocking collectives, on_device(): got = lax.all_to_all(send, 'rows', 0, 0)  20 us
    all_to_all x1, blocking collectives, on_device(): answer = lax.all_to_all(message, 'rows', 0, 0, axis_index_groups=halves)  7.37 us
    pallas_call x1, Pallas kernels, on_device(): pl.pallas_call(functools.partial(main_kernel, plan, chunk), out_shape=jax...  4.36 us
    ppermute x4, starting transfers between devices, flipped(): return lax.ppermute(block, 'feat', [(p, p ^ bit) for p in range(count)])  2.07 us
    pallas_call x1, Pallas kernels, on_device(): pl.pallas_call(functools.partial(prep_kernel, plan), out_shape=jax.ShapeD...  1.71 us
  transfers between devices with their start and end apart: 4, of which 0 were waited for; matrix products, arithmetic and copies ran while one was open for 0% of the time, Pallas kernels for 12%

profile of v4, /device:TPU:0, one launch (start us, length us, event | category | flops | bytes accessed | tf_op | source)
XLA Modules:
  0.0 37.0 jit_solution(1319514615576195165)
XLA Ops:
  0.6 1.7 %prep.1 = bf16[8,72,384]{2,1,0:T(8,128)(2,1)S(1)} custom-call(bf16[512,128]{1,0:T(8,128)(2,1)} %refs_0_.1, bf16[512]{0:T(512)(128)(2,1)} %refs_1_.1, s32[32,512]{1,0:T(8,128)} %refs_2_.1, s32[3,512]{1,0:T(4,128)} %refs_3_.1, s32[14]{0:T(128)} %refs_4_.1, s32[14]{0:T(128)} %refs_5_.1), custom_call_target="tpu_custom_call" | custom-call | tf_op jit(solution)/shard_map/prep/pallas_call | solution.py:326
  2.4 20.0 %all_to_all.10.got_ref = bf16[8,72,384]{2,1,0:T(8,128)(2,1)S(1)} all-to-all(bf16[8,72,384]{2,1,0:T(8,128)(2,1)S(1)} %prep.1), channel_id=1, replica_groups=mesh['rows'=8,'feat'=4] {'rows'}, dimensions={0} | all-to-all | bytes 884736 | tf_op jit(solution)/shard_map/all_to_all | solution.py:343
  22.4 0.0 collective-permute-start
  22.4 0.6 %collective-permute-start.1 = (f32[8,128]{1,0:T(8,128)S(1)}, f32[8,128]{1,0:T(8,128)S(1)}, u32[]{:S(2)}, u32[]{:S(2)}) collective-permute-start(f32[8,128]{1,0:T(8,128)S(1)} %scores.1.refs_0_), channel_id=1, source_target_pairs={{0,1},{1,0},{2,3},{3,2},{4,5},{5,4},{6,7},{7,6},{8,9},{9,8},{10,11... | collective-permute-start | bytes 12296 | tf_op jit(solution)/shard_map/ppermute | solution.py:317
  23.0 1.5 %collective-permute-start.2 = (f32[8,128]{1,0:T(8,128)S(1)}, f32[8,128]{1,0:T(8,128)S(1)}, u32[]{:S(2)}, u32[]{:S(2)}) collective-permute-start(f32[8,128]{1,0:T(8,128)S(1)} %scores.1.refs_0_), channel_id=1, source_target_pairs={{0,2},{1,3},{2,0},{3,1},{4,6},{5,7},{6,4},{7,5},{8,10},{9,11},{10,... | collective-permute-start | bytes 12296 | tf_op jit(solution)/shard_map/ppermute | solution.py:317
  24.5 0.0 collective-permute-start.3
  24.5 0.0 collective-permute-done.refs_0_
  24.5 4.4 %gains.1 = f32[4,40,128]{2,1,0:T(8,128)S(1)} custom-call(bf16[8,72,384]{2,1,0:T(8,128)(2,1)S(1)} %all_to_all.10.got_ref, bf16[8,72,384]{2,1,0:T(8,128)(2,1)S(1)} %collective-permute-done.refs_0_), custom_call_target="tpu_custom_call" | custom-call | flops 3422552064 | bytes 884736 | tf_op jit(solution)/shard_map/gains/pallas_call | solution.py:359
  28.9 0.0 collective-permute-done.1.refs_1_
  28.9 0.0 collective-permute-done.2.refs_2_
  28.9 0.0 collective-permute-done.3.refs_3_
  28.9 7.4 %all_to_all.11.got_ref = f32[4,40,128]{2,1,0:T(8,128)S(1)} all-to-all(f32[4,40,128]{2,1,0:T(8,128)S(1)} %gains.1), channel_id=1, replica_groups={{0,4,8,12},{16,20,24,28},{1,5,9,13},{17,21,25,29},{2,6,10,14},{18,22,26..., dimensions={0} | all-to-all | bytes 163840 | tf_op jit(solution)/shard_map/all_to_all | solution.py:379
  36.3 0.7 %finish.1 = (f32[16,64]{1,0:T(8,128)}, f32[32,64]{1,0:T(8,128)}, f32[64,64]{1,0:T(8,128)}, f32[3,1,2,128]{3,2,1,0:T(2,128)}) custom-call(f32[4,40,128]{2,1,0:T(8,128)S(1)} %all_to_all.11.got_ref, f32[8,128]{1,0:T(8,128)S(1)} %scores.1.refs_0_, f32[8,128]{1,0:T(8,128)S(1)} %collective-permute-done.1.refs_1_, f32[8,128]{1,0:T(8,128)S(1)} %collective-permute-done.2.refs_2_, ...), custom_call_target="tpu_custom_call" | custom-call | tf_op jit(solution)/shard_map/finish/pallas_call | solution.py:384
  (1 shorter events, 0.0 us)
Async XLA Ops:
  22.4 2.1 %collective-permute-start = (bf16[8,72,384]{2,1,0:T(8,128)(2,1)S(1)}, bf16[8,72,384]{2,1,0:T(8,128)(2,1)S(1)}, u32[]{:S(2)}, u32[]{:S(2)}) collective-permute-start(bf16[8,72,384]{2,1,0:T(8,128)(2,1)S(1)} %all_to_all.10.got_ref), channel_id=1, source_target_pairs={{0,1},{1,0},{2,3},{3,2},{4,5},{5,4},{6,7},{7,6},{8,9},{9,8},{10,11... | collective-permute-start | bytes 1327112 | tf_op jit(solution)/shard_map/ppermute | solution.py:317
  22.4 6.4 %collective-permute-start.1 = (f32[8,128]{1,0:T(8,128)S(1)}, f32[8,128]{1,0:T(8,128)S(1)}, u32[]{:S(2)}, u32[]{:S(2)}) collective-permute-start(f32[8,128]{1,0:T(8,128)S(1)} %scores.1.refs_0_), channel_id=1, source_target_pairs={{0,1},{1,0},{2,3},{3,2},{4,5},{5,4},{6,7},{7,6},{8,9},{9,8},{10,11... | collective-permute-start | bytes 12296 | tf_op jit(solution)/shard_map/ppermute | solution.py:317
  23.0 5.9 %collective-permute-start.2 = (f32[8,128]{1,0:T(8,128)S(1)}, f32[8,128]{1,0:T(8,128)S(1)}, u32[]{:S(2)}, u32[]{:S(2)}) collective-permute-start(f32[8,128]{1,0:T(8,128)S(1)} %scores.1.refs_0_), channel_id=1, source_target_pairs={{0,2},{1,3},{2,0},{3,1},{4,6},{5,7},{6,4},{7,5},{8,10},{9,11},{10,... | collective-permute-start | bytes 12296 | tf_op jit(solution)/shard_map/ppermute | solution.py:317
  24.5 4.4 %collective-permute-start.3 = (f32[8,128]{1,0:T(8,128)S(1)}, f32[8,128]{1,0:T(8,128)S(1)}, u32[]{:S(2)}, u32[]{:S(2)}) collective-permute-start(f32[8,128]{1,0:T(8,128)S(1)} %scores.1.refs_0_), channel_id=1, source_target_pairs={{0,3},{1,2},{2,1},{3,0},{4,7},{5,6},{6,5},{7,4},{8,11},{9,10},{10,... | collective-permute-start | bytes 12296 | tf_op jit(solution)/shard_map/ppermute | solution.py:317

commit v5 on v4

--- a/solution.py
+++ b/solution.py
@@ -18,6 +18,15 @@
 bf16 = jnp.bfloat16
 f32 = jnp.float32
 NT = (((1,), (1,)), ((), ()))
+PERMUTED = 8
+
+
+def div(value, by):
+    return value // by if isinstance(value, int) else lax.div(value, jnp.int32(by))
+
+
+def rem(value, by):
+    return value % by if isinstance(value, int) else lax.rem(value, jnp.int32(by))
 
 
 def round_up(value, unit):
@@ -43,8 +52,8 @@
         self.outs_dev = self.outs // OUT_SPLIT
         self.pair = 2 if feat_axis % 2 == 0 else 1
         self.outs_sent = self.outs_dev // self.pair
-        self.code_at = self.outs_sent
-        self.misc_at = self.outs_sent + self.share
+        self.grad_at = self.share
+        self.misc_at = self.share + self.outs_sent
         self.score_rows = 2 * self.levels + 1
         self.spans = self.slots // LANES
         self.misc_rows = 2 + -(-self.score_rows * PIECES // self.spans)
@@ -62,9 +71,12 @@
         self.level_at = [sum(self.needed[:level]) // 2 for level in range(self.levels)]
         self.gain_rows = sum(self.needed) // 2
         self.message = round_up(self.gain_rows, 8)
+        self.ends = [(level, n) for level in reversed(range(self.levels)) for n in range(2**level)]
+        self.permuted = self.half <= PERMUTED
+        self.messages = self.half if self.permuted else 1
 
     def code_row(self, feature):
-        return self.code_at + feature // 2 + (feature % 2) * (self.share // 2)
+        return feature // 2 + (feature % 2) * (self.share // 2)
 
 
 def prep_kernel(plan, *refs):
@@ -76,13 +88,21 @@
     ]
     for copy in copies:
         copy.start()
+    rows = plan.row_dev
+    panel = lax.axis_index("feat")
+    sent = OUT_SPLIT * plan.outs_sent
+    low_at, high_at, own_at = sent, sent + plan.words, sent + plan.feats
+    at = lax.broadcasted_iota(jnp.int32, (sent, plan.outs), 0)
+    wanted = at + (at // plan.outs_sent) * (plan.outs_dev - plan.outs_sent) + lax.rem(panel, plan.pair) * plan.outs_sent
+    turn = jnp.where(wanted == lax.broadcasted_iota(jnp.int32, (sent, plan.outs), 1), 1.0, 0.0).astype(bf16)
+    ahead = jnp.where(
+        lax.broadcasted_iota(jnp.int32, (rows, rows), 0) <= lax.broadcasted_iota(jnp.int32, (rows, rows), 1), 1.0, 0.0
+    ).astype(bf16)
     for copy in copies:
         copy.wait()
     grad_ref, hess_ref, word_ref, child_ref, feature_ref, bin_ref = fetched
-    rows = plan.row_dev
     grads = grad_ref[...]
     hess = hess_ref[...].astype(f32).reshape(1, rows)
-    panel = lax.axis_index("feat")
     words = word_ref[...]
     low = jnp.bitwise_and(words, 63)
     high = jnp.bitwise_and(jnp.right_shift(words, 6), 63)
@@ -91,24 +111,14 @@
     for level in range(1, plan.levels):
         nodes.append(nodes[-1] * 2 + child_ref[level : level + 1, :])
 
-    unit = jnp.where(
-        lax.broadcasted_iota(jnp.int32, (plan.outs, plan.outs), 0)
-        == lax.broadcasted_iota(jnp.int32, (plan.outs, plan.outs), 1),
-        1.0,
-        0.0,
-    ).astype(bf16)
-    low_at, high_at, own_at = plan.outs, plan.outs + plan.words, plan.outs + plan.feats
-    table[0:low_at] = lax.dot_general(unit, grads, NT, preferred_element_type=f32).astype(bf16)
+    table[0:low_at] = lax.dot_general(turn, grads, NT, preferred_element_type=f32).astype(bf16)
     table[low_at:high_at] = low.astype(f32).astype(bf16)
     table[high_at:own_at] = high.astype(f32).astype(bf16)
     at = lax.broadcasted_iota(jnp.int32, (TILE, rows), 0)
     leaf = jnp.bitwise_and(nodes[-1], plan.leaves - 1).astype(f32)
     table[own_at:] = jnp.where(at == 0, hess, jnp.where(at == 1, leaf, 0.0)).astype(bf16)
     side = jnp.where(at == nodes[0], 1.0, 0.0)
-    ahead = jnp.where(
-        lax.broadcasted_iota(jnp.int32, (rows, rows), 0) <= lax.broadcasted_iota(jnp.int32, (rows, rows), 1), 1.0, 0.0
-    )
-    rank = jnp.dot(side.astype(bf16), ahead.astype(bf16), preferred_element_type=f32)
+    rank = jnp.dot(side.astype(bf16), ahead, preferred_element_type=f32)
     slot = jnp.where(side > 0.0, rank - 1.0, -1.0)
     slot_ids = lax.broadcasted_iota(jnp.int32, (plan.slots, rows), 0).astype(f32)
     for half in range(2):
@@ -148,7 +158,6 @@
         pieces.append(sums.astype(bf16).astype(f32))
         sums = sums - pieces[-1]
 
-    parity = lax.rem(panel, plan.pair)
     word_share = plan.share // 2
     blank = jnp.zeros((1, LANES), f32)
     filler = jnp.zeros((plan.sent_rows - plan.misc_at - plan.misc_rows, plan.slots), f32)
@@ -161,13 +170,13 @@
     for device in range(plan.devices):
         half, place = divmod(device, plan.half)
         share, split = divmod(place, OUT_SPLIT)
-        start = pl.multiple_of(split * plan.outs_dev + parity * plan.outs_sent, plan.outs_sent)
+        grads_from = split * plan.outs_sent
         low_from, high_from = low_at + share * word_share, high_at + share * word_share
         send_ref[device] = jnp.concatenate(
             [
-                packed[half, pl.ds(start, plan.outs_sent), :],
                 packed[half, low_from : low_from + word_share, :],
                 packed[half, high_from : high_from + word_share, :],
+                packed[half, grads_from : grads_from + plan.outs_sent, :],
                 packed[half, own_at : own_at + 2, :],
                 lines[device * leaf_count // plan.devices],
             ],
@@ -177,7 +186,7 @@
 
 def main_kernel(plan, chunk, got_ref, *refs):
     others, refs = refs[: plan.pair - 1], refs[plan.pair - 1 :]
-    out_ref, weighted, left_sums = refs
+    out_refs, (weighted, gain_table, left_sums) = refs[: plan.messages], refs[plan.messages :]
     rows = plan.slots
     leaves, outs_dev, step = plan.leaves, plan.outs_dev, plan.step
     hess_at = leaves * outs_dev
@@ -201,7 +210,8 @@
             weighted[hess_at : hess_at + TILE, columns] = jnp.where(leaf_ids == node, hess, 0.0).astype(bf16)
             node_wide = jnp.broadcast_to(node, (plan.outs_sent, rows)).astype(bf16)
             for place, ref in enumerate((got_ref, *others)):
-                grads = ref[source, 0 : plan.outs_sent, :]
+                grads_from = plan.grad_at if place == 0 else 0
+                grads = ref[source, grads_from : grads_from + plan.outs_sent, :]
                 for leaf in range(leaves):
                     at = leaf * outs_dev + place * plan.outs_sent
                     weighted[at : at + plan.outs_sent, columns] = jnp.where(
@@ -230,7 +240,6 @@
     def add_gains(group, sums):
         left = [sums[leaf * outs_dev : (leaf + 1) * outs_dev] for leaf in range(leaves)]
         hess = [sums[hess_at + leaf : hess_at + leaf + 1] for leaf in range(leaves)]
-        ends = [(level, n) for level in reversed(range(plan.levels)) for n in range(2**level)]
         for level in reversed(range(plan.levels - 1)):
             past = len(left) - 2 ** (level + 1)
             for n in range(past, len(left), 2):
@@ -247,16 +256,10 @@
         rights = [t - part for t, part in zip(totals, left, strict=True)]
         on_right = jnp.concatenate([jnp.sum(part * part, axis=0, keepdims=True) for part in rights], axis=0)
         gains = (on_left / hess + on_right / (hess_total - hess) - whole_part) / plan.outs
-        for line_at, (level, n) in enumerate(ends):
-            size = plan.sizes[level]
+        for end in range(len(plan.ends)):
             for tile in range(step // 2):
-                piece = gains[line_at : line_at + 1, tile * LANES : (tile + 1) * LANES]
-                for place in range(size):
-                    first = place * plan.returned[level] % plan.share // 2
-                    line = group * (step // 2) + tile - first
-                    if 0 <= line < plan.needed[level] // 2:
-                        row = plan.level_at[level] + line
-                        out_ref[n * size + place, row : row + 1, :] = piece
+                at = group * (step // 2) + tile
+                gain_table[end, at : at + 1, :] = gains[end : end + 1, tile * LANES : (tile + 1) * LANES]
 
     count = plan.devices // chunk
     add_chunk(0, True)
@@ -264,13 +267,25 @@
         lax.fori_loop(1, count, lambda c, _: (add_chunk(c * chunk, False), 0)[1], 0)
         for group in range(plan.share // step):
             add_gains(group, left_sums[:, group * step * BINS : (group + 1) * step * BINS])
-    if plan.message > plan.gain_rows:
-        filler = jnp.zeros((plan.message - plan.gain_rows, LANES), f32)
-        for device in range(plan.half):
-            out_ref[device, plan.gain_rows : plan.message, :] = filler
-
-
-def score_kernel(plan, got_ref, score_ref):
+    me = rem(lax.axis_index("rows"), plan.half)
+    for slot in range(plan.half):
+        place = jnp.bitwise_xor(me, slot) if plan.permuted else slot
+        out_ref = out_refs[slot] if plan.permuted else out_refs[0].at[slot]
+        for level in range(plan.levels):
+            count = plan.needed[level] // 2
+            end = plan.ends.index((level, 0)) + div(place, plan.sizes[level])
+            first = rem(rem(place, plan.sizes[level]) * plan.returned[level], plan.share) // 2
+            if not isinstance(first, int) and count % 8 == 0:
+                first = pl.multiple_of(first, 8)
+            at = plan.level_at[level]
+            out_ref[at : at + count, :] = gain_table[end, pl.ds(first, count), :]
+        if plan.message > plan.gain_rows:
+            out_ref[plan.gain_rows :, :] = jnp.zeros((plan.message - plan.gain_rows, LANES), f32)
+
+
+def score_kernel(plan, got_ref, score_ref, grads_ref):
+    grads_ref[...] = got_ref[:, plan.grad_at : plan.grad_at + plan.outs_sent, :]
+
     def add(source, total):
         return total + got_ref[source, plan.misc_at + 2 : plan.misc_at + plan.misc_rows, :].astype(f32)
 
@@ -284,21 +299,30 @@
         score_ref[i : i + 1, :] = value
 
 
-def final_kernel(plan, got_ref, *refs):
+def final_kernel(plan, *refs):
+    got_refs, refs = refs[: plan.messages], refs[plan.messages :]
     score_refs, refs = refs[: -plan.levels - 1], refs[-plan.levels - 1 :]
     *gain_refs, child_ref = refs
+    me = rem(lax.axis_index("rows"), plan.half)
     side = plan.block // 2
+    totals = []
+    for other in range(plan.shares):
+        share = jnp.bitwise_xor(div(me, OUT_SPLIT), other)
+        total = 0.0
+        for split in range(OUT_SPLIT):
+            slot = other * OUT_SPLIT + split
+            total = total + (got_refs[slot][...] if plan.permuted else got_refs[0][jnp.bitwise_xor(me, slot)])
+        totals.append((share, total))
     for level, gain_ref in enumerate(gain_refs):
-        position = lax.rem(lax.axis_index("rows"), plan.sizes[level])
-        for t in range(plan.returned[level] // plan.needed[level]):
-            share = (position * plan.returned[level] + t * plan.share) // plan.share
-            rows = slice(plan.level_at[level], plan.level_at[level] + plan.needed[level] // 2)
-            total = got_ref[share * OUT_SPLIT, rows, :]
-            for split in range(1, OUT_SPLIT):
-                total = total + got_ref[share * OUT_SPLIT + split, rows, :]
+        rows = slice(plan.level_at[level], plan.level_at[level] + plan.needed[level] // 2)
+        first = div(rem(me, plan.sizes[level]) * plan.returned[level], plan.share)
+        for turn in range(plan.returned[level] // plan.needed[level]):
+            value = totals[0][1][rows]
+            for share, total in totals[1:]:
+                value = jnp.where(share == first + turn, total[rows], value)
             for start in range(0, plan.needed[level], plan.block):
-                part = total[start // 2 : start // 2 + side]
-                at = t * plan.share + start
+                part = value[start // 2 : start // 2 + side]
+                at = turn * plan.share + start
                 gain_ref[at : at + side, :] = part[:, :BINS]
                 gain_ref[at + side : at + 2 * side, :] = part[:, BINS:]
     sums = score_refs[0][...]
@@ -312,15 +336,16 @@
             child_ref[level, 0, side : side + 1, :] = -sums[line : line + 1, :] / scale
 
 
-def flipped(block, bit):
-    count = lax.axis_size("feat")
-    return lax.ppermute(block, "feat", [(p, p ^ bit) for p in range(count)])
+def flipped(block, bits, axis="feat"):
+    count = lax.axis_size(axis)
+    return lax.ppermute(block, axis, [(p, p ^ bits) for p in range(count)])
 
 
 def on_device(gradients, hessians, bin_words, children, split_feature, split_bin):
     plan = Plan(lax.axis_size("rows"), lax.axis_size("feat"), gradients, bin_words, children)
     params = pltpu.CompilerParams(vmem_limit_bytes=VMEM_BYTES)
 
+    table_rows = OUT_SPLIT * plan.outs_sent + plan.feats + TILE
     inputs = (gradients, hessians, bin_words, children, split_feature, split_bin)
     inputs = tuple(pltpu.with_memory_space_constraint(a, pltpu.HBM) for a in inputs)
     send = pl.pallas_call(
@@ -332,8 +357,8 @@
             *(pltpu.VMEM(a.shape, a.dtype) for a in inputs[:4]),
             *(pltpu.SMEM(a.shape, a.dtype) for a in inputs[4:]),
             pltpu.VMEM((2 * plan.leaves * 8, plan.row_dev), f32),
-            pltpu.VMEM((plan.outs + plan.feats + TILE, plan.row_dev), bf16),
-            pltpu.VMEM((2, plan.outs + plan.feats + TILE, plan.slots), f32),
+            pltpu.VMEM((table_rows, plan.row_dev), bf16),
+            pltpu.VMEM((2, table_rows, plan.slots), f32),
             pltpu.SemaphoreType.DMA((len(inputs),)),
         ],
         compiler_params=params,
@@ -341,28 +366,33 @@
     )(*inputs)
 
     got = lax.all_to_all(send, "rows", 0, 0)
-    arrays = [got] + ([flipped(got, 1)] if plan.pair > 1 else [])
-    scores = pl.pallas_call(
+    scores, grads_part = pl.pallas_call(
         functools.partial(score_kernel, plan),
-        out_shape=jax.ShapeDtypeStruct((8, plan.outs), f32),
+        out_shape=(
+            jax.ShapeDtypeStruct((8, plan.outs), f32),
+            jax.ShapeDtypeStruct((plan.devices, plan.outs_sent, plan.slots), bf16),
+        ),
         in_specs=[whole()],
-        out_specs=whole(),
+        out_specs=(whole(), whole()),
         compiler_params=params,
         name="scores",
     )(got)
+    arrays = [got] + ([flipped(grads_part, 1)] if plan.pair > 1 else [])
     score_parts = [scores] + [flipped(scores, away) for away in range(1, lax.axis_size("feat"))]
 
     chunk = max(1, min(plan.devices, 4096 // plan.slots))
     while plan.devices % chunk:
         chunk -= 1
     sums_rows = plan.leaves * plan.outs_dev + TILE
-    message = pl.pallas_call(
+    block = (plan.message, LANES) if plan.permuted else (plan.half, plan.message, LANES)
+    messages = pl.pallas_call(
         functools.partial(main_kernel, plan, chunk),
-        out_shape=jax.ShapeDtypeStruct((plan.half, plan.message, LANES), f32),
+        out_shape=[jax.ShapeDtypeStruct(block, f32)] * plan.messages,
         in_specs=[whole()] * len(arrays),
-        out_specs=whole(),
+        out_specs=[whole()] * plan.messages,
         scratch_shapes=[
             pltpu.VMEM((sums_rows, chunk * plan.slots), bf16),
+            pltpu.VMEM((len(plan.ends), plan.share // 2, LANES), f32),
             pltpu.VMEM((sums_rows, plan.share * BINS), f32),
         ],
         cost_estimate=pl.CostEstimate(
@@ -374,9 +404,12 @@
         name="gains",
     )(*arrays)
 
-    message, *score_parts = lax.optimization_barrier((message, *score_parts))
-    halves = [list(range(plan.half)), list(range(plan.half, plan.devices))]
-    answer = lax.all_to_all(message, "rows", 0, 0, axis_index_groups=halves)
+    messages, score_parts = lax.optimization_barrier((list(messages), score_parts))
+    if plan.permuted:
+        messages = [flipped(block, slot, "rows") if slot else block for slot, block in enumerate(messages)]
+    else:
+        halves = [list(range(plan.half)), list(range(plan.half, plan.devices))]
+        messages = [lax.all_to_all(messages[0], "rows", 0, 0, axis_index_groups=halves)]
     shapes = [
         jax.ShapeDtypeStruct((count, BINS), f32) for count in plan.returned
     ]
@@ -384,11 +417,11 @@
     return pl.pallas_call(
         functools.partial(final_kernel, plan),
         out_shape=tuple(shapes),
-        in_specs=[whole()] * (1 + len(score_parts)),
+        in_specs=[whole()] * (plan.messages + len(score_parts)),
         out_specs=tuple(whole() for _ in shapes),
         compiler_params=params,
         name="finish",
-    )(answer, *score_parts)
+    )(*messages, *score_parts)
 
 
 def solution(mesh):

time: 37.2 us -> 36.1 us (0.970)
  blocking collectives: 27.4 us -> 20 us
  starting transfers between devices: 2.07 us -> 5.77 us
  waiting for transfers between devices: 0.01 us -> 2.56 us
    all_to_all x1 -> x0, blocking collectives: 7.37 us -> none  [on_device(): answer = lax.all_to_all(message, 'rows', 0, 0, axis_index_groups=halves)]
    ppermute x4 -> x7, starting transfers between devices: 2.07 us -> 5.77 us  [flipped(): return lax.ppermute(block, axis, [(p, p ^ bits) for p in range(count)])]
    ppermute x4 -> x7, waiting for transfers between devices: 0.01 us -> 2.56 us  [flipped(): return lax.ppermute(block, axis, [(p, p ^ bits) for p in range(count)])]
  transfers between devices with their start and end apart: 4 -> 7, of which waited for: 0 -> 3; matrix products, arithmetic and copies ran while one was open for 0% -> 0% of each run, Pallas kernels for 12% -> 12%
where the time goes in v5:
time: 36.1 us; the launch traced here: 35.9 us
  blocking collectives  20 us (55%)
  Pallas kernels  6.82 us (19%)
  starting transfers between devices  5.77 us (16%)
  waiting for transfers between devices  2.56 us (7%)
  between operations  0.69 us (2%)
    all_to_all x1, blocking collectives, on_device(): got = lax.all_to_all(send, 'rows', 0, 0)  20 us
    ppermute x7, starting transfers between devices, flipped(): return lax.ppermute(block, axis, [(p, p ^ bits) for p in range(count)])  5.77 us
    pallas_call x1, Pallas kernels, on_device(): pl.pallas_call(functools.partial(main_kernel, plan, chunk), out_shape=[ja...  4.38 us
    ppermute x7, waiting for transfers between devices, flipped(): return lax.ppermute(block, axis, [(p, p ^ bits) for p in range(count)])  2.56 us
    pallas_call x1, Pallas kernels, on_device(): pl.pallas_call(functools.partial(prep_kernel, plan), out_shape=jax.ShapeD...  1.66 us
    pallas_call x1, Pallas kernels, on_device(): pl.pallas_call(functools.partial(final_kernel, plan), out_shape=tuple(sha...  0.72 us
  transfers between devices with their start and end apart: 7, of which 3 were waited for; matrix products, arithmetic and copies ran while one was open for 0% of the time, Pallas kernels for 12%

profile of v5, /device:TPU:0, one launch (start us, length us, event | category | flops | bytes accessed | tf_op | source)
XLA Modules:
  0.0 35.9 jit_solution(16504884508819463372)
XLA Ops:
  0.6 1.7 %prep.1 = bf16[8,72,384]{2,1,0:T(8,128)(2,1)S(1)} custom-call(bf16[512,128]{1,0:T(8,128)(2,1)} %refs_0_.1, bf16[512]{0:T(512)(128)(2,1)} %refs_1_.1, s32[32,512]{1,0:T(8,128)} %refs_2_.1, s32[3,512]{1,0:T(4,128)} %refs_3_.1, s32[14]{0:T(128)} %refs_4_.1, s32[14]{0:T(128)} %refs_5_.1), custom_call_target="tpu_custom_call" | custom-call | tf_op jit(solution)/shard_map/prep/pallas_call | solution.py:351
  2.3 20.0 %all_to_all.5.got_ref = bf16[8,72,384]{2,1,0:T(8,128)(2,1)S(1)} all-to-all(bf16[8,72,384]{2,1,0:T(8,128)(2,1)S(1)} %prep.1), channel_id=1, replica_groups=mesh['rows'=8,'feat'=4] {'rows'}, dimensions={0} | all-to-all | bytes 884736 | tf_op jit(solution)/shard_map/all_to_all | solution.py:368
  22.3 0.1 scores.1
  22.4 0.1 collective-permute-start
  22.5 1.6 %collective-permute-start.3 = (f32[8,128]{1,0:T(8,128)S(1)}, f32[8,128]{1,0:T(8,128)S(1)}, u32[]{:S(2)}, u32[]{:S(2)}) collective-permute-start(f32[8,128]{1,0:T(8,128)S(1)} %get-tuple-element.28.refs_4_), channel_id=1, source_target_pairs={{0,3},{1,2},{2,1},{3,0},{4,7},{5,6},{6,5},{7,4},{8,11},{9,10},{10,... | collective-permute-start | bytes 12296 | tf_op jit(solution)/shard_map/ppermute | solution.py:341
  24.1 0.5 %collective-permute-start.2 = (f32[8,128]{1,0:T(8,128)S(1)}, f32[8,128]{1,0:T(8,128)S(1)}, u32[]{:S(2)}, u32[]{:S(2)}) collective-permute-start(f32[8,128]{1,0:T(8,128)S(1)} %get-tuple-element.28.refs_4_), channel_id=1, source_target_pairs={{0,2},{1,3},{2,0},{3,1},{4,6},{5,7},{6,4},{7,5},{8,10},{9,11},{10,... | collective-permute-start | bytes 12296 | tf_op jit(solution)/shard_map/ppermute | solution.py:341
  24.6 0.0 collective-permute-start.1
  24.6 0.0 collective-permute-done.refs_0_
  24.6 4.4 %gains.1 = (f32[40,128]{1,0:T(8,128)S(1)}, f32[40,128]{1,0:T(8,128)S(1)}, f32[40,128]{1,0:T(8,128)S(1)}, f32[40,128]{1,0:T(8,128)S(1)}) custom-call(bf16[8,72,384]{2,1,0:T(8,128)(2,1)S(1)} %all_to_all.5.got_ref, bf16[8,32,384]{2,1,0:T(8,128)(2,1)S(1)} %collective-permute-done.refs_0_), custom_call_target="tpu_custom_call" | custom-call | flops 3422552064 | bytes 884736 | tf_op jit(solution)/shard_map/gains/pallas_call | solution.py:388
  29.0 0.0 collective-permute-done.3.refs_7_
  29.0 0.0 collective-permute-done.2.refs_6_
  29.0 0.0 collective-permute-done.1.refs_5_
  29.0 1.3 %collective-permute-start.4 = (f32[40,128]{1,0:T(8,128)S(1)}, f32[40,128]{1,0:T(8,128)S(1)}, u32[]{:S(2)}, u32[]{:S(2)}) collective-permute-start(f32[40,128]{1,0:T(8,128)S(1)} %get-tuple-element.25), channel_id=1, source_target_pairs={{0,4},{4,0},{8,12},{12,8},{16,20},{20,16},{24,28},{28,24},{1,5},{5... | collective-permute-start | bytes 61448 | tf_op jit(solution)/shard_map/ppermute | solution.py:341
  30.4 0.1 collective-permute-start.5
  30.5 2.1 %collective-permute-start.6 = (f32[40,128]{1,0:T(8,128)S(1)}, f32[40,128]{1,0:T(8,128)S(1)}, u32[]{:S(2)}, u32[]{:S(2)}) collective-permute-start(f32[40,128]{1,0:T(8,128)S(1)} %get-tuple-element.27), channel_id=1, source_target_pairs={{0,12},{4,8},{8,4},{12,0},{16,28},{20,24},{24,20},{28,16},{1,13},{... | collective-permute-start | bytes 61448 | tf_op jit(solution)/shard_map/ppermute | solution.py:341
  32.6 0.3 collective-permute-done.4.refs_1_
  32.9 1.3 %collective-permute-done.5.refs_2_ = f32[40,128]{1,0:T(8,128)S(1)} collective-permute-done((f32[40,128]{1,0:T(8,128)S(1)}, f32[40,128]{1,0:T(8,128)S(1)}, u32[]{:S(2)}, u32[]{:S(2)}) %collective-permute-start.5) | collective-permute-done | bytes 20512 | tf_op jit(solution)/shard_map/ppermute | solution.py:341
  34.2 0.9 %collective-permute-done.6.refs_3_ = f32[40,128]{1,0:T(8,128)S(1)} collective-permute-done((f32[40,128]{1,0:T(8,128)S(1)}, f32[40,128]{1,0:T(8,128)S(1)}, u32[]{:S(2)}, u32[]{:S(2)}) %collective-permute-start.6) | collective-permute-done | bytes 20512 | tf_op jit(solution)/shard_map/ppermute | solution.py:341
  35.1 0.7 %finish.1 = (f32[16,64]{1,0:T(8,128)}, f32[32,64]{1,0:T(8,128)}, f32[64,64]{1,0:T(8,128)}, f32[3,1,2,128]{3,2,1,0:T(2,128)}) custom-call(f32[40,128]{1,0:T(8,128)S(1)} %get-tuple-element.24.refs_0_, f32[40,128]{1,0:T(8,128)S(1)} %collective-permute-done.4.refs_1_, f32[40,128]{1,0:T(8,128)S(1)} %collective-permute-done.5.refs_2_, ...), custom_call_target="tpu_custom_call" | custom-call | tf_op jit(solution)/shard_map/finish/pallas_call | solution.py:417
Async XLA Ops:
  22.4 2.2 %collective-permute-start = (bf16[8,32,384]{2,1,0:T(8,128)(2,1)S(1)}, bf16[8,32,384]{2,1,0:T(8,128)(2,1)S(1)}, u32[]{:S(2)}, u32[]{:S(2)}) collective-permute-start(bf16[8,32,384]{2,1,0:T(8,128)(2,1)S(1)} %get-tuple-element.18), channel_id=1, source_target_pairs={{0,1},{1,0},{2,3},{3,2},{4,5},{5,4},{6,7},{7,6},{8,9},{9,8},{10,11... | collective-permute-start | bytes 589832 | tf_op jit(solution)/shard_map/ppermute | solution.py:341
  22.5 6.5 %collective-permute-start.3 = (f32[8,128]{1,0:T(8,128)S(1)}, f32[8,128]{1,0:T(8,128)S(1)}, u32[]{:S(2)}, u32[]{:S(2)}) collective-permute-start(f32[8,128]{1,0:T(8,128)S(1)} %get-tuple-element.28.refs_4_), channel_id=1, source_target_pairs={{0,3},{1,2},{2,1},{3,0},{4,7},{5,6},{6,5},{7,4},{8,11},{9,10},{10,... | collective-permute-start | bytes 12296 | tf_op jit(solution)/shard_map/ppermute | solution.py:341
  24.1 4.9 %collective-permute-start.2 = (f32[8,128]{1,0:T(8,128)S(1)}, f32[8,128]{1,0:T(8,128)S(1)}, u32[]{:S(2)}, u32[]{:S(2)}) collective-permute-start(f32[8,128]{1,0:T(8,128)S(1)} %get-tuple-element.28.refs_4_), channel_id=1, source_target_pairs={{0,2},{1,3},{2,0},{3,1},{4,6},{5,7},{6,4},{7,5},{8,10},{9,11},{10,... | collective-permute-start | bytes 12296 | tf_op jit(solution)/shard_map/ppermute | solution.py:341
  24.6 4.4 %collective-permute-start.1 = (f32[8,128]{1,0:T(8,128)S(1)}, f32[8,128]{1,0:T(8,128)S(1)}, u32[]{:S(2)}, u32[]{:S(2)}) collective-permute-start(f32[8,128]{1,0:T(8,128)S(1)} %get-tuple-element.28.refs_4_), channel_id=1, source_target_pairs={{0,1},{1,0},{2,3},{3,2},{4,5},{5,4},{6,7},{7,6},{8,9},{9,8},{10,11... | collective-permute-start | bytes 12296 | tf_op jit(solution)/shard_map/ppermute | solution.py:341
  29.0 3.8 %collective-permute-start.4 = (f32[40,128]{1,0:T(8,128)S(1)}, f32[40,128]{1,0:T(8,128)S(1)}, u32[]{:S(2)}, u32[]{:S(2)}) collective-permute-start(f32[40,128]{1,0:T(8,128)S(1)} %get-tuple-element.25), channel_id=1, source_target_pairs={{0,4},{4,0},{8,12},{12,8},{16,20},{20,16},{24,28},{28,24},{1,5},{5... | collective-permute-start | bytes 61448 | tf_op jit(solution)/shard_map/ppermute | solution.py:341
  30.4 3.8 %collective-permute-start.5 = (f32[40,128]{1,0:T(8,128)S(1)}, f32[40,128]{1,0:T(8,128)S(1)}, u32[]{:S(2)}, u32[]{:S(2)}) collective-permute-start(f32[40,128]{1,0:T(8,128)S(1)} %get-tuple-element.26), channel_id=1, source_target_pairs={{0,8},{4,12},{8,0},{12,4},{16,24},{20,28},{24,16},{28,20},{1,9},{5... | collective-permute-start | bytes 61448 | tf_op jit(solution)/shard_map/ppermute | solution.py:341
  30.5 4.7 %collective-permute-start.6 = (f32[40,128]{1,0:T(8,128)S(1)}, f32[40,128]{1,0:T(8,128)S(1)}, u32[]{:S(2)}, u32[]{:S(2)}) collective-permute-start(f32[40,128]{1,0:T(8,128)S(1)} %get-tuple-element.27), channel_id=1, source_target_pairs={{0,12},{4,8},{8,4},{12,0},{16,28},{20,24},{24,20},{28,16},{1,13},{... | collective-permute-start | bytes 61448 | tf_op jit(solution)/shard_map/ppermute | solution.py:341

commit v6 on v5

--- a/solution.py
+++ b/solution.py
@@ -35,6 +35,26 @@
 
 def whole(*_):
     return pl.BlockSpec(memory_space=pltpu.VMEM)
+
+
+def aligned(value, unit):
+    return value if isinstance(value, int) or unit % 8 else pl.multiple_of(value, 8)
+
+
+def target(me, slot, count):
+    return rem(me + slot, count)
+
+
+def source_of(me, slot, count):
+    return rem(me + (count - slot), count)
+
+
+def exchanged(blocks, group, count):
+    moved = [blocks[0]]
+    for slot in range(1, group):
+        route = [(p, p - p % group + (p + slot) % group) for p in range(count)]
+        moved.append(lax.ppermute(blocks[slot], "rows", route))
+    return moved
 
 
 class Plan:
@@ -72,16 +92,17 @@
         self.gain_rows = sum(self.needed) // 2
         self.message = round_up(self.gain_rows, 8)
         self.ends = [(level, n) for level in reversed(range(self.levels)) for n in range(2**level)]
-        self.permuted = self.half <= PERMUTED
+        self.permuted = self.devices <= PERMUTED
         self.messages = self.half if self.permuted else 1
+        self.parcels = self.devices if self.permuted else 1
 
     def code_row(self, feature):
         return feature // 2 + (feature % 2) * (self.share // 2)
 
 
 def prep_kernel(plan, *refs):
-    inputs, send_ref, refs = refs[:6], refs[6], refs[7:]
-    fetched, (masks, table, packed, sems) = refs[:6], refs[6:]
+    inputs, send_refs, refs = refs[:6], refs[6 : 6 + plan.parcels], refs[6 + plan.parcels :]
+    fetched, (masks, table, packed, lines, sems) = refs[:6], refs[6:]
     copies = [
         pltpu.make_async_copy(source, target, sems.at[i])
         for i, (source, target) in enumerate(zip(inputs, fetched, strict=True))
@@ -161,30 +182,35 @@
     word_share = plan.share // 2
     blank = jnp.zeros((1, LANES), f32)
     filler = jnp.zeros((plan.sent_rows - plan.misc_at - plan.misc_rows, plan.slots), f32)
-    lines = []
     for leaf in range(leaf_count):
         parts = [piece[leaf * 8 + i : leaf * 8 + i + 1] for i in range(plan.score_rows) for piece in pieces]
         parts += [blank] * (-len(parts) % plan.spans)
         parts = [jnp.concatenate(parts[i : i + plan.spans], axis=1) for i in range(0, len(parts), plan.spans)]
-        lines.append(jnp.concatenate(parts + ([filler] if filler.shape[0] else []), axis=0))
-    for device in range(plan.devices):
-        half, place = divmod(device, plan.half)
-        share, split = divmod(place, OUT_SPLIT)
-        grads_from = split * plan.outs_sent
-        low_from, high_from = low_at + share * word_share, high_at + share * word_share
-        send_ref[device] = jnp.concatenate(
+        lines[leaf] = jnp.concatenate(parts + ([filler] if filler.shape[0] else []), axis=0)
+    for slot in range(plan.devices):
+        device = target(lax.axis_index("rows"), slot, plan.devices) if plan.permuted else slot
+        half, place = div(device, plan.half), rem(device, plan.half)
+        share, split = div(place, OUT_SPLIT), rem(place, OUT_SPLIT)
+        from_low = aligned(low_at + share * word_share, word_share)
+        from_high = aligned(high_at + share * word_share, word_share)
+        message = jnp.concatenate(
             [
-                packed[half, low_from : low_from + word_share, :],
-                packed[half, high_from : high_from + word_share, :],
-                packed[half, grads_from : grads_from + plan.outs_sent, :],
+                packed[half, pl.ds(from_low, word_share), :],
+                packed[half, pl.ds(from_high, word_share), :],
+                packed[half, pl.ds(aligned(split * plan.outs_sent, plan.outs_sent), plan.outs_sent), :],
                 packed[half, own_at : own_at + 2, :],
-                lines[device * leaf_count // plan.devices],
+                lines[div(device, plan.devices // leaf_count)],
             ],
             axis=0,
         ).astype(bf16)
-
-
-def main_kernel(plan, chunk, got_ref, *refs):
+        if plan.permuted:
+            send_refs[slot][...] = message
+        else:
+            send_refs[0][slot] = message
+
+
+def main_kernel(plan, chunk, *refs):
+    got_refs, refs = refs[: plan.parcels], refs[plan.parcels :]
     others, refs = refs[: plan.pair - 1], refs[plan.pair - 1 :]
     out_refs, (weighted, gain_table, left_sums) = refs[: plan.messages], refs[plan.messages :]
     rows = plan.slots
@@ -196,22 +222,25 @@
     zero = jnp.zeros((), bf16)
     one = jnp.ones((), bf16)
 
+    def parcel(source):
+        return got_refs[source] if plan.permuted else got_refs[0].at[source]
+
     def marked(source, feature):
         row = plan.code_row(feature)
-        code = jnp.broadcast_to(got_ref[source, row : row + 1, :], (BINS, rows))
+        code = jnp.broadcast_to(parcel(source)[row : row + 1, :], (BINS, rows))
         return jnp.where(code <= level_bins, one, zero)
 
     def add_chunk(first, fresh):
         for k in range(chunk):
             source = first + k
             columns = slice(k * rows, (k + 1) * rows)
-            misc = got_ref[source, plan.misc_at : plan.misc_at + 2, :].astype(f32)
+            misc = parcel(source)[plan.misc_at : plan.misc_at + 2, :].astype(f32)
             hess, node = misc[0:1], misc[1:2]
             weighted[hess_at : hess_at + TILE, columns] = jnp.where(leaf_ids == node, hess, 0.0).astype(bf16)
             node_wide = jnp.broadcast_to(node, (plan.outs_sent, rows)).astype(bf16)
-            for place, ref in enumerate((got_ref, *others)):
-                grads_from = plan.grad_at if place == 0 else 0
-                grads = ref[source, grads_from : grads_from + plan.outs_sent, :]
+            grads_parts = [parcel(source)[plan.grad_at : plan.grad_at + plan.outs_sent, :]]
+            grads_parts += [ref[source] for ref in others]
+            for place, grads in enumerate(grads_parts):
                 for leaf in range(leaves):
                     at = leaf * outs_dev + place * plan.outs_sent
                     weighted[at : at + plan.outs_sent, columns] = jnp.where(
@@ -269,7 +298,7 @@
             add_gains(group, left_sums[:, group * step * BINS : (group + 1) * step * BINS])
     me = rem(lax.axis_index("rows"), plan.half)
     for slot in range(plan.half):
-        place = jnp.bitwise_xor(me, slot) if plan.permuted else slot
+        place = target(me, slot, plan.half) if plan.permuted else slot
         out_ref = out_refs[slot] if plan.permuted else out_refs[0].at[slot]
         for level in range(plan.levels):
             count = plan.needed[level] // 2
@@ -283,13 +312,18 @@
             out_ref[plan.gain_rows :, :] = jnp.zeros((plan.message - plan.gain_rows, LANES), f32)
 
 
-def score_kernel(plan, got_ref, score_ref, grads_ref):
-    grads_ref[...] = got_ref[:, plan.grad_at : plan.grad_at + plan.outs_sent, :]
-
-    def add(source, total):
-        return total + got_ref[source, plan.misc_at + 2 : plan.misc_at + plan.misc_rows, :].astype(f32)
-
-    total = lax.fori_loop(0, plan.devices, add, jnp.zeros((plan.misc_rows - 2, plan.slots), f32))
+def score_kernel(plan, *refs):
+    got_refs, (score_ref, grads_ref) = refs[: plan.parcels], refs[plan.parcels :]
+    tail = slice(plan.misc_at + 2, plan.misc_at + plan.misc_rows)
+    wanted = slice(plan.grad_at, plan.grad_at + plan.outs_sent)
+    total = jnp.zeros((plan.misc_rows - 2, plan.slots), f32)
+    if plan.permuted:
+        for source, ref in enumerate(got_refs):
+            grads_ref[source] = ref[wanted, :]
+            total = total + ref[tail, :].astype(f32)
+    else:
+        grads_ref[...] = got_refs[0][:, wanted, :]
+        total = lax.fori_loop(0, plan.devices, lambda k, sums: sums + got_refs[0][k, tail, :].astype(f32), total)
     score_ref[...] = jnp.zeros_like(score_ref)
     for i in range(plan.score_rows):
         value = 0.0
@@ -305,21 +339,17 @@
     *gain_refs, child_ref = refs
     me = rem(lax.axis_index("rows"), plan.half)
     side = plan.block // 2
-    totals = []
-    for other in range(plan.shares):
-        share = jnp.bitwise_xor(div(me, OUT_SPLIT), other)
-        total = 0.0
-        for split in range(OUT_SPLIT):
-            slot = other * OUT_SPLIT + split
-            total = total + (got_refs[slot][...] if plan.permuted else got_refs[0][jnp.bitwise_xor(me, slot)])
-        totals.append((share, total))
+    arrived = []
+    for slot in range(plan.half):
+        place = source_of(me, slot, plan.half) if plan.permuted else slot
+        arrived.append((div(place, OUT_SPLIT), got_refs[slot] if plan.permuted else got_refs[0].at[slot]))
     for level, gain_ref in enumerate(gain_refs):
         rows = slice(plan.level_at[level], plan.level_at[level] + plan.needed[level] // 2)
         first = div(rem(me, plan.sizes[level]) * plan.returned[level], plan.share)
         for turn in range(plan.returned[level] // plan.needed[level]):
-            value = totals[0][1][rows]
-            for share, total in totals[1:]:
-                value = jnp.where(share == first + turn, total[rows], value)
+            value = 0.0
+            for share, ref in arrived:
+                value = value + jnp.where(share == first + turn, ref[rows, :], 0.0)
             for start in range(0, plan.needed[level], plan.block):
                 part = value[start // 2 : start // 2 + side]
                 at = turn * plan.share + start
@@ -336,9 +366,9 @@
             child_ref[level, 0, side : side + 1, :] = -sums[line : line + 1, :] / scale
 
 
-def flipped(block, bits, axis="feat"):
-    count = lax.axis_size(axis)
-    return lax.ppermute(block, axis, [(p, p ^ bits) for p in range(count)])
+def flipped(block, bits):
+    count = lax.axis_size("feat")
+    return lax.ppermute(block, "feat", [(p, p ^ bits) for p in range(count)])
 
 
 def on_device(gradients, hessians, bin_words, children, split_feature, split_bin):
@@ -348,36 +378,41 @@
     table_rows = OUT_SPLIT * plan.outs_sent + plan.feats + TILE
     inputs = (gradients, hessians, bin_words, children, split_feature, split_bin)
     inputs = tuple(pltpu.with_memory_space_constraint(a, pltpu.HBM) for a in inputs)
-    send = pl.pallas_call(
+    parcel = (plan.sent_rows, plan.slots) if plan.permuted else (plan.devices, plan.sent_rows, plan.slots)
+    parcels = pl.pallas_call(
         functools.partial(prep_kernel, plan),
-        out_shape=jax.ShapeDtypeStruct((plan.devices, plan.sent_rows, plan.slots), bf16),
+        out_shape=[jax.ShapeDtypeStruct(parcel, bf16)] * plan.parcels,
         in_specs=[pl.BlockSpec(memory_space=pltpu.HBM)] * len(inputs),
-        out_specs=whole(),
+        out_specs=[whole()] * plan.parcels,
         scratch_shapes=[
             *(pltpu.VMEM(a.shape, a.dtype) for a in inputs[:4]),
             *(pltpu.SMEM(a.shape, a.dtype) for a in inputs[4:]),
             pltpu.VMEM((2 * plan.leaves * 8, plan.row_dev), f32),
             pltpu.VMEM((table_rows, plan.row_dev), bf16),
             pltpu.VMEM((2, table_rows, plan.slots), f32),
+            pltpu.VMEM((2 * plan.leaves, plan.sent_rows - plan.misc_at - 2, plan.slots), f32),
             pltpu.SemaphoreType.DMA((len(inputs),)),
         ],
         compiler_params=params,
         name="prep",
     )(*inputs)
 
-    got = lax.all_to_all(send, "rows", 0, 0)
+    if plan.permuted:
+        got = exchanged(parcels, plan.devices, plan.devices)
+    else:
+        got = [lax.all_to_all(parcels[0], "rows", 0, 0)]
     scores, grads_part = pl.pallas_call(
         functools.partial(score_kernel, plan),
         out_shape=(
             jax.ShapeDtypeStruct((8, plan.outs), f32),
             jax.ShapeDtypeStruct((plan.devices, plan.outs_sent, plan.slots), bf16),
         ),
-        in_specs=[whole()],
+        in_specs=[whole()] * plan.parcels,
         out_specs=(whole(), whole()),
         compiler_params=params,
         name="scores",
-    )(got)
-    arrays = [got] + ([flipped(grads_part, 1)] if plan.pair > 1 else [])
+    )(*got)
+    arrays = got + ([flipped(grads_part, 1)] if plan.pair > 1 else [])
     score_parts = [scores] + [flipped(scores, away) for away in range(1, lax.axis_size("feat"))]
 
     chunk = max(1, min(plan.devices, 4096 // plan.slots))
@@ -406,7 +441,7 @@
 
     messages, score_parts = lax.optimization_barrier((list(messages), score_parts))
     if plan.permuted:
-        messages = [flipped(block, slot, "rows") if slot else block for slot, block in enumerate(messages)]
+        messages = exchanged(messages, plan.half, plan.devices)
     else:
         halves = [list(range(plan.half)), list(range(plan.half, plan.devices))]
         messages = [lax.all_to_all(messages[0], "rows", 0, 0, axis_index_groups=halves)]

time: 36.1 us -> 33.3 us (0.922)
  blocking collectives: 20 us -> 0 us
  starting transfers between devices: 5.77 us -> 20 us
  waiting for transfers between devices: 2.56 us -> 5.68 us
    all_to_all x1 -> x0, blocking collectives: 20 us -> none  [on_device(): got = lax.all_to_all(send, 'rows', 0, 0)]
    ppermute x7 -> x14, starting transfers between devices: 5.77 us -> 20 us  [the longest x10 17.7 us: exchanged(): moved.append(lax.ppermute(blocks[slot], 'rows', route))]
    ppermute x7 -> x14, waiting for transfers between devices: 2.56 us -> 5.68 us  [the longest x10 5.67 us: exchanged(): moved.append(lax.ppermute(blocks[slot], 'rows', route))]
  transfers between devices with their start and end apart: 7 -> 14, of which waited for: 3 -> 7; matrix products, arithmetic and copies ran while one was open for 0% -> 0% of each run, Pallas kernels for 12% -> 13%
where the time goes in v6:
time: 33.3 us; the launch traced here: 33.1 us
  starting transfers between devices  20 us (60%)
  Pallas kernels  6.8 us (20%)
  waiting for transfers between devices  5.68 us (17%)
  between operations  0.69 us (2%)
    ppermute x10, starting transfers between devices, exchanged(): moved.append(lax.ppermute(blocks[slot], 'rows', route))  17.7 us
    ppermute x10, waiting for transfers between devices, exchanged(): moved.append(lax.ppermute(blocks[slot], 'rows', route))  5.67 us
    pallas_call x1, Pallas kernels, on_device(): pl.pallas_call(functools.partial(main_kernel, plan, chunk), out_shape=[ja...  4.37 us
    ppermute x4, starting transfers between devices, flipped(): return lax.ppermute(block, 'feat', [(p, p ^ bits) for p in range(count)])  2.28 us
    pallas_call x1, Pallas kernels, on_device(): pl.pallas_call(functools.partial(prep_kernel, plan), out_shape=[jax.Shape...  1.68 us
    pallas_call x1, Pallas kernels, on_device(): pl.pallas_call(functools.partial(final_kernel, plan), out_shape=tuple(sha...  0.73 us
  transfers between devices with their start and end apart: 14, of which 7 were waited for; matrix products, arithmetic and copies ran while one was open for 0% of the time, Pallas kernels for 13%

profile of v6, /device:TPU:0, one launch (start us, length us, event | category | flops | bytes accessed | tf_op | source)
XLA Modules:
  0.0 33.1 jit_solution(16657129148330313590)
XLA Ops:
  0.6 1.7 %prep.1 = (bf16[72,384]{1,0:T(8,128)(2,1)S(1)}, bf16[72,384]{1,0:T(8,128)(2,1)S(1)}, bf16[72,384]{1,0:T(8,128)(2,1)S(1)}, bf16[72,384]{1,0:T(8,128)(2,1)S(1)}, b...) custom-call(bf16[512,128]{1,0:T(8,128)(2,1)} %refs_0_.1, ...), custom_call_target="tpu_custom_call" | custom-call | tf_op jit(solution)/shard_map/prep/pallas_call | solution.py:382
  2.3 3.0 %collective-permute-start = (bf16[72,384]{1,0:T(8,128)(2,1)S(1)}, bf16[72,384]{1,0:T(8,128)(2,1)S(1)}, u32[]{:S(2)}, u32[]{:S(2)}) collective-permute-start(bf16[72,384]{1,0:T(8,128)(2,1)S(1)} %get-tuple-element.27), channel_id=1, source_target_pairs={{0,4},{4,8},{8,12},{12,16},{16,20},{20,24},{24,28},{28,0},{1,5},{5... | collective-permute-start | bytes 165896 | tf_op jit(solution)/shard_map/ppermute | solution.py:56
  5.3 1.6 %collective-permute-start.1 = (bf16[72,384]{1,0:T(8,128)(2,1)S(1)}, bf16[72,384]{1,0:T(8,128)(2,1)S(1)}, u32[]{:S(2)}, u32[]{:S(2)}) collective-permute-start(bf16[72,384]{1,0:T(8,128)(2,1)S(1)} %get-tuple-element.28), channel_id=1, source_target_pairs={{0,8},{4,12},{8,16},{12,20},{16,24},{20,28},{24,0},{28,4},{1,9},{5... | collective-permute-start | bytes 165896 | tf_op jit(solution)/shard_map/ppermute | solution.py:56
  6.9 2.5 %collective-permute-start.2 = (bf16[72,384]{1,0:T(8,128)(2,1)S(1)}, bf16[72,384]{1,0:T(8,128)(2,1)S(1)}, u32[]{:S(2)}, u32[]{:S(2)}) collective-permute-start(bf16[72,384]{1,0:T(8,128)(2,1)S(1)} %get-tuple-element.29), channel_id=1, source_target_pairs={{0,12},{4,16},{8,20},{12,24},{16,28},{20,0},{24,4},{28,8},{1,13},{... | collective-permute-start | bytes 165896 | tf_op jit(solution)/shard_map/ppermute | solution.py:56
  9.4 1.2 %collective-permute-start.3 = (bf16[72,384]{1,0:T(8,128)(2,1)S(1)}, bf16[72,384]{1,0:T(8,128)(2,1)S(1)}, u32[]{:S(2)}, u32[]{:S(2)}) collective-permute-start(bf16[72,384]{1,0:T(8,128)(2,1)S(1)} %get-tuple-element.30), channel_id=1, source_target_pairs={{0,16},{4,20},{8,24},{12,28},{16,0},{20,4},{24,8},{28,12},{1,17},{... | collective-permute-start | bytes 165896 | tf_op jit(solution)/shard_map/ppermute | solution.py:56
  10.7 2.6 %collective-permute-start.4 = (bf16[72,384]{1,0:T(8,128)(2,1)S(1)}, bf16[72,384]{1,0:T(8,128)(2,1)S(1)}, u32[]{:S(2)}, u32[]{:S(2)}) collective-permute-start(bf16[72,384]{1,0:T(8,128)(2,1)S(1)} %get-tuple-element.31), channel_id=1, source_target_pairs={{0,20},{4,24},{8,28},{12,0},{16,4},{20,8},{24,12},{28,16},{1,21},{... | collective-permute-start | bytes 165896 | tf_op jit(solution)/shard_map/ppermute | solution.py:56
  13.3 0.0 collective-permute-done.refs_1_
  13.3 1.4 %collective-permute-start.5 = (bf16[72,384]{1,0:T(8,128)(2,1)S(1)}, bf16[72,384]{1,0:T(8,128)(2,1)S(1)}, u32[]{:S(2)}, u32[]{:S(2)}) collective-permute-start(bf16[72,384]{1,0:T(8,128)(2,1)S(1)} %get-tuple-element.32), channel_id=1, source_target_pairs={{0,24},{4,28},{8,0},{12,4},{16,8},{20,12},{24,16},{28,20},{1,25},{... | collective-permute-start | bytes 165896 | tf_op jit(solution)/shard_map/ppermute | solution.py:56
  14.7 0.0 collective-permute-done.1.refs_2_
  14.7 1.4 %collective-permute-start.6 = (bf16[72,384]{1,0:T(8,128)(2,1)S(1)}, bf16[72,384]{1,0:T(8,128)(2,1)S(1)}, u32[]{:S(2)}, u32[]{:S(2)}) collective-permute-start(bf16[72,384]{1,0:T(8,128)(2,1)S(1)} %get-tuple-element.33), channel_id=1, source_target_pairs={{0,28},{4,0},{8,4},{12,8},{16,12},{20,16},{24,20},{28,24},{1,29},{... | collective-permute-start | bytes 165896 | tf_op jit(solution)/shard_map/ppermute | solution.py:56
  16.1 0.0 collective-permute-done.2.refs_3_
  16.1 0.2 collective-permute-done.3.refs_4_
  16.3 0.7 %collective-permute-done.4.refs_5_ = bf16[72,384]{1,0:T(8,128)(2,1)S(1)} collective-permute-done((bf16[72,384]{1,0:T(8,128)(2,1)S(1)}, bf16[72,384]{1,0:T(8,128)(2,1)S(1)}, u32[]{:S(2)}, u32[]{:S(2)}) %collective-permute-start.4) | collective-permute-done | bytes 55328 | tf_op jit(solution)/shard_map/ppermute | solution.py:56
  17.0 1.0 %collective-permute-done.5.refs_6_ = bf16[72,384]{1,0:T(8,128)(2,1)S(1)} collective-permute-done((bf16[72,384]{1,0:T(8,128)(2,1)S(1)}, bf16[72,384]{1,0:T(8,128)(2,1)S(1)}, u32[]{:S(2)}, u32[]{:S(2)}) %collective-permute-start.5) | collective-permute-done | bytes 55328 | tf_op jit(solution)/shard_map/ppermute | solution.py:56
  18.1 0.8 %collective-permute-done.6.refs_7_ = bf16[72,384]{1,0:T(8,128)(2,1)S(1)} collective-permute-done((bf16[72,384]{1,0:T(8,128)(2,1)S(1)}, bf16[72,384]{1,0:T(8,128)(2,1)S(1)}, u32[]{:S(2)}, u32[]{:S(2)}) %collective-permute-start.6) | collective-permute-done | bytes 55328 | tf_op jit(solution)/shard_map/ppermute | solution.py:56
  18.9 0.1 collective-permute-start.7
  19.0 1.6 %collective-permute-start.10 = (f32[8,128]{1,0:T(8,128)S(1)}, f32[8,128]{1,0:T(8,128)S(1)}, u32[]{:S(2)}, u32[]{:S(2)}) collective-permute-start(f32[8,128]{1,0:T(8,128)S(1)} %get-tuple-element.44.refs_4_), channel_id=1, source_target_pairs={{0,3},{1,2},{2,1},{3,0},{4,7},{5,6},{6,5},{7,4},{8,11},{9,10},{10,... | collective-permute-start | bytes 12296 | tf_op jit(solution)/shard_map/ppermute | solution.py:371
  20.6 0.1 collective-permute-start.8
  20.6 0.5 %collective-permute-start.9 = (f32[8,128]{1,0:T(8,128)S(1)}, f32[8,128]{1,0:T(8,128)S(1)}, u32[]{:S(2)}, u32[]{:S(2)}) collective-permute-start(f32[8,128]{1,0:T(8,128)S(1)} %get-tuple-element.44.refs_4_), channel_id=1, source_target_pairs={{0,2},{1,3},{2,0},{3,1},{4,6},{5,7},{6,4},{7,5},{8,10},{9,11},{10,... | collective-permute-start | bytes 12296 | tf_op jit(solution)/shard_map/ppermute | solution.py:371
  21.2 0.0 collective-permute-done.7.refs_8_
  21.2 4.4 %gains.1 = (f32[40,128]{1,0:T(8,128)S(1)}, f32[40,128]{1,0:T(8,128)S(1)}, f32[40,128]{1,0:T(8,128)S(1)}, f32[40,128]{1,0:T(8,128)S(1)}) custom-call(bf16[72,384]{1,0:T(8,128)(2,1)S(1)} %get-tuple-element.26.refs_0_, bf16[72,384]{1,0:T(8,128)(2,1)S(1)} %collective-permute-done.refs_1_, bf16[72,384]{1,0:T(8,128)(2,1)S(1)} %collective-permute-done.1.refs_2_, ...), custom_call_target="tpu_custom_call" | custom-call | flops 3422552064 | bytes 884736 | tf_op jit(solution)/shard_map/gains/pallas_call | solution.py:423
  25.5 0.0 collective-permute-done.10.refs_7_
  25.5 0.0 collective-permute-done.8.refs_5_
  25.6 0.0 collective-permute-done.9.refs_6_
  25.6 1.6 %collective-permute-start.11 = (f32[40,128]{1,0:T(8,128)S(1)}, f32[40,128]{1,0:T(8,128)S(1)}, u32[]{:S(2)}, u32[]{:S(2)}) collective-permute-start(f32[40,128]{1,0:T(8,128)S(1)} %get-tuple-element.41), channel_id=1, source_target_pairs={{0,4},{4,8},{8,12},{12,0},{16,20},{20,24},{24,28},{28,16},{1,5},{5... | collective-permute-start | bytes 61448 | tf_op jit(solution)/shard_map/ppermute | solution.py:56
  27.2 1.5 %collective-permute-start.12 = (f32[40,128]{1,0:T(8,128)S(1)}, f32[40,128]{1,0:T(8,128)S(1)}, u32[]{:S(2)}, u32[]{:S(2)}) collective-permute-start(f32[40,128]{1,0:T(8,128)S(1)} %get-tuple-element.42), channel_id=1, source_target_pairs={{0,8},{4,12},{8,0},{12,4},{16,24},{20,28},{24,16},{28,20},{1,9},{5... | collective-permute-start | bytes 61448 | tf_op jit(solution)/shard_map/ppermute | solution.py:56
  28.6 0.9 %collective-permute-start.13 = (f32[40,128]{1,0:T(8,128)S(1)}, f32[40,128]{1,0:T(8,128)S(1)}, u32[]{:S(2)}, u32[]{:S(2)}) collective-permute-start(f32[40,128]{1,0:T(8,128)S(1)} %get-tuple-element.43), channel_id=1, source_target_pairs={{0,12},{4,0},{8,4},{12,8},{16,28},{20,16},{24,20},{28,24},{1,13},{... | collective-permute-start | bytes 61448 | tf_op jit(solution)/shard_map/ppermute | solution.py:56
  29.5 0.9 %collective-permute-done.11.refs_1_ = f32[40,128]{1,0:T(8,128)S(1)} collective-permute-done((f32[40,128]{1,0:T(8,128)S(1)}, f32[40,128]{1,0:T(8,128)S(1)}, u32[]{:S(2)}, u32[]{:S(2)}) %collective-permute-start.11) | collective-permute-done | bytes 20512 | tf_op jit(solution)/shard_map/ppermute | solution.py:56
  30.4 0.8 %collective-permute-done.12.refs_2_ = f32[40,128]{1,0:T(8,128)S(1)} collective-permute-done((f32[40,128]{1,0:T(8,128)S(1)}, f32[40,128]{1,0:T(8,128)S(1)}, u32[]{:S(2)}, u32[]{:S(2)}) %collective-permute-start.12) | collective-permute-done | bytes 20512 | tf_op jit(solution)/shard_map/ppermute | solution.py:56
  31.2 1.3 %collective-permute-done.13.refs_3_ = f32[40,128]{1,0:T(8,128)S(1)} collective-permute-done((f32[40,128]{1,0:T(8,128)S(1)}, f32[40,128]{1,0:T(8,128)S(1)}, u32[]{:S(2)}, u32[]{:S(2)}) %collective-permute-start.13) | collective-permute-done | bytes 20512 | tf_op jit(solution)/shard_map/ppermute | solution.py:56
  32.4 0.7 %finish.1 = (f32[16,64]{1,0:T(8,128)}, f32[32,64]{1,0:T(8,128)}, f32[64,64]{1,0:T(8,128)}, f32[3,1,2,128]{3,2,1,0:T(2,128)}) custom-call(f32[40,128]{1,0:T(8,128)S(1)} %get-tuple-element.40.refs_0_, f32[40,128]{1,0:T(8,128)S(1)} %collective-permute-done.11.refs_1_, f32[40,128]{1,0:T(8,128)S(1)} %collective-permute-done.12.refs_2_, ...), custom_call_target="tpu_custom_call" | custom-call | tf_op jit(solution)/shard_map/finish/pallas_call | solution.py:452
  (1 shorter events, 0.0 us)
Async XLA Ops:
  2.3 11.0 %collective-permute-start = (bf16[72,384]{1,0:T(8,128)(2,1)S(1)}, bf16[72,384]{1,0:T(8,128)(2,1)S(1)}, u32[]{:S(2)}, u32[]{:S(2)}) collective-permute-start(bf16[72,384]{1,0:T(8,128)(2,1)S(1)} %get-tuple-element.27), channel_id=1, source_target_pairs={{0,4},{4,8},{8,12},{12,16},{16,20},{20,24},{24,28},{28,0},{1,5},{5... | collective-permute-start | bytes 165896 | tf_op jit(solution)/shard_map/ppermute | solution.py:56
  5.3 9.3 %collective-permute-start.1 = (bf16[72,384]{1,0:T(8,128)(2,1)S(1)}, bf16[72,384]{1,0:T(8,128)(2,1)S(1)}, u32[]{:S(2)}, u32[]{:S(2)}) collective-permute-start(bf16[72,384]{1,0:T(8,128)(2,1)S(1)} %get-tuple-element.28), channel_id=1, source_target_pairs={{0,8},{4,12},{8,16},{12,20},{16,24},{20,28},{24,0},{28,4},{1,9},{5... | collective-permute-start | bytes 165896 | tf_op jit(solution)/shard_map/ppermute | solution.py:56
  6.9 9.2 %collective-permute-start.2 = (bf16[72,384]{1,0:T(8,128)(2,1)S(1)}, bf16[72,384]{1,0:T(8,128)(2,1)S(1)}, u32[]{:S(2)}, u32[]{:S(2)}) collective-permute-start(bf16[72,384]{1,0:T(8,128)(2,1)S(1)} %get-tuple-element.29), channel_id=1, source_target_pairs={{0,12},{4,16},{8,20},{12,24},{16,28},{20,0},{24,4},{28,8},{1,13},{... | collective-permute-start | bytes 165896 | tf_op jit(solution)/shard_map/ppermute | solution.py:56
  9.4 6.9 %collective-permute-start.3 = (bf16[72,384]{1,0:T(8,128)(2,1)S(1)}, bf16[72,384]{1,0:T(8,128)(2,1)S(1)}, u32[]{:S(2)}, u32[]{:S(2)}) collective-permute-start(bf16[72,384]{1,0:T(8,128)(2,1)S(1)} %get-tuple-element.30), channel_id=1, source_target_pairs={{0,16},{4,20},{8,24},{12,28},{16,0},{20,4},{24,8},{28,12},{1,17},{... | collective-permute-start | bytes 165896 | tf_op jit(solution)/shard_map/ppermute | solution.py:56
  10.7 6.3 %collective-permute-start.4 = (bf16[72,384]{1,0:T(8,128)(2,1)S(1)}, bf16[72,384]{1,0:T(8,128)(2,1)S(1)}, u32[]{:S(2)}, u32[]{:S(2)}) collective-permute-start(bf16[72,384]{1,0:T(8,128)(2,1)S(1)} %get-tuple-element.31), channel_id=1, source_target_pairs={{0,20},{4,24},{8,28},{12,0},{16,4},{20,8},{24,12},{28,16},{1,21},{... | collective-permute-start | bytes 165896 | tf_op jit(solution)/shard_map/ppermute | solution.py:56
  13.3 4.7 %collective-permute-start.5 = (bf16[72,384]{1,0:T(8,128)(2,1)S(1)}, bf16[72,384]{1,0:T(8,128)(2,1)S(1)}, u32[]{:S(2)}, u32[]{:S(2)}) collective-permute-start(bf16[72,384]{1,0:T(8,128)(2,1)S(1)} %get-tuple-element.32), channel_id=1, source_target_pairs={{0,24},{4,28},{8,0},{12,4},{16,8},{20,12},{24,16},{28,20},{1,25},{... | collective-permute-start | bytes 165896 | tf_op jit(solution)/shard_map/ppermute | solution.py:56
  14.7 4.2 %collective-permute-start.6 = (bf16[72,384]{1,0:T(8,128)(2,1)S(1)}, bf16[72,384]{1,0:T(8,128)(2,1)S(1)}, u32[]{:S(2)}, u32[]{:S(2)}) collective-permute-start(bf16[72,384]{1,0:T(8,128)(2,1)S(1)} %get-tuple-element.33), channel_id=1, source_target_pairs={{0,28},{4,0},{8,4},{12,8},{16,12},{20,16},{24,20},{28,24},{1,29},{... | collective-permute-start | bytes 165896 | tf_op jit(solution)/shard_map/ppermute | solution.py:56
  18.9 2.3 %collective-permute-start.7 = (bf16[8,32,384]{2,1,0:T(8,128)(2,1)S(1)}, bf16[8,32,384]{2,1,0:T(8,128)(2,1)S(1)}, u32[]{:S(2)}, u32[]{:S(2)}) collective-permute-start(bf16[8,32,384]{2,1,0:T(8,128)(2,1)S(1)} %get-tuple-element.34), channel_id=1, source_target_pairs={{0,1},{1,0},{2,3},{3,2},{4,5},{5,4},{6,7},{7,6},{8,9},{9,8},{10,11... | collective-permute-start | bytes 589832 | tf_op jit(solution)/shard_map/ppermute | solution.py:371
  19.0 6.6 %collective-permute-start.10 = (f32[8,128]{1,0:T(8,128)S(1)}, f32[8,128]{1,0:T(8,128)S(1)}, u32[]{:S(2)}, u32[]{:S(2)}) collective-permute-start(f32[8,128]{1,0:T(8,128)S(1)} %get-tuple-element.44.refs_4_), channel_id=1, source_target_pairs={{0,3},{1,2},{2,1},{3,0},{4,7},{5,6},{6,5},{7,4},{8,11},{9,10},{10,... | collective-permute-start | bytes 12296 | tf_op jit(solution)/shard_map/ppermute | solution.py:371
  20.6 5.0 %collective-permute-start.8 = (f32[8,128]{1,0:T(8,128)S(1)}, f32[8,128]{1,0:T(8,128)S(1)}, u32[]{:S(2)}, u32[]{:S(2)}) collective-permute-start(f32[8,128]{1,0:T(8,128)S(1)} %get-tuple-element.44.refs_4_), channel_id=1, source_target_pairs={{0,1},{1,0},{2,3},{3,2},{4,5},{5,4},{6,7},{7,6},{8,9},{9,8},{10,11... | collective-permute-start | bytes 12296 | tf_op jit(solution)/shard_map/ppermute | solution.py:371
  20.6 4.9 %collective-permute-start.9 = (f32[8,128]{1,0:T(8,128)S(1)}, f32[8,128]{1,0:T(8,128)S(1)}, u32[]{:S(2)}, u32[]{:S(2)}) collective-permute-start(f32[8,128]{1,0:T(8,128)S(1)} %get-tuple-element.44.refs_4_), channel_id=1, source_target_pairs={{0,2},{1,3},{2,0},{3,1},{4,6},{5,7},{6,4},{7,5},{8,10},{9,11},{10,... | collective-permute-start | bytes 12296 | tf_op jit(solution)/shard_map/ppermute | solution.py:371
  25.6 4.8 %collective-permute-start.11 = (f32[40,128]{1,0:T(8,128)S(1)}, f32[40,128]{1,0:T(8,128)S(1)}, u32[]{:S(2)}, u32[]{:S(2)}) collective-permute-start(f32[40,128]{1,0:T(8,128)S(1)} %get-tuple-element.41), channel_id=1, source_target_pairs={{0,4},{4,8},{8,12},{12,0},{16,20},{20,24},{24,28},{28,16},{1,5},{5... | collective-permute-start | bytes 61448 | tf_op jit(solution)/shard_map/ppermute | solution.py:56
  27.2 4.0 %collective-permute-start.12 = (f32[40,128]{1,0:T(8,128)S(1)}, f32[40,128]{1,0:T(8,128)S(1)}, u32[]{:S(2)}, u32[]{:S(2)}) collective-permute-start(f32[40,128]{1,0:T(8,128)S(1)} %get-tuple-element.42), channel_id=1, source_target_pairs={{0,8},{4,12},{8,0},{12,4},{16,24},{20,28},{24,16},{28,20},{1,9},{5... | collective-permute-start | bytes 61448 | tf_op jit(solution)/shard_map/ppermute | solution.py:56
  28.6 3.8 %collective-permute-start.13 = (f32[40,128]{1,0:T(8,128)S(1)}, f32[40,128]{1,0:T(8,128)S(1)}, u32[]{:S(2)}, u32[]{:S(2)}) collective-permute-start(f32[40,128]{1,0:T(8,128)S(1)} %get-tuple-element.43), channel_id=1, source_target_pairs={{0,12},{4,0},{8,4},{12,8},{16,28},{20,16},{24,20},{28,24},{1,13},{... | collective-permute-start | bytes 61448 | tf_op jit(solution)/shard_map/ppermute | solution.py:56

commit v7 on v6

--- a/solution.py
+++ b/solution.py
@@ -54,6 +54,19 @@
     for slot in range(1, group):
         route = [(p, p - p % group + (p + slot) % group) for p in range(count)]
         moved.append(lax.ppermute(blocks[slot], "rows", route))
+    return moved
+
+
+def spread(parcels, plan):
+    feat_axis = lax.axis_size("feat")
+    moved = []
+    for slot, block in enumerate(parcels):
+        route = []
+        for p in range(plan.devices * feat_axis):
+            row, panel = divmod(p, feat_axis)
+            row = (row + 2 * slot + 2 - panel % 2) % plan.devices
+            route.append((p, row * feat_axis + panel))
+        moved.append(lax.ppermute(block, ("rows", "feat"), route))
     return moved
 
 
@@ -70,14 +83,19 @@
         self.shares = self.half // OUT_SPLIT
         self.share = self.feats // self.shares
         self.outs_dev = self.outs // OUT_SPLIT
-        self.pair = 2 if feat_axis % 2 == 0 else 1
-        self.outs_sent = self.outs_dev // self.pair
+        self.permuted = rows_axis <= PERMUTED and feat_axis % 2 == 0
+        self.panels = 2 if self.permuted else 1
+        self.parcels = rows_axis // 2 if self.permuted else 1
+        self.codes = self.panels * self.feats
+        self.splits = 2 ** (self.levels + 1) - 2
+        self.split_rows = round_up(self.splits, TILE)
         self.grad_at = self.share
-        self.misc_at = self.share + self.outs_sent
+        self.misc_at = self.share + self.outs_dev
         self.score_rows = 2 * self.levels + 1
         self.spans = self.slots // LANES
         self.misc_rows = 2 + -(-self.score_rows * PIECES // self.spans)
-        self.sent_rows = round_up(self.misc_at + self.misc_rows, 8)
+        self.base_rows = round_up(self.misc_at + self.misc_rows, 8)
+        self.sent_rows = self.base_rows + (self.panels - 1) * self.share
         self.sizes = [self.devices >> (level + 1) for level in range(self.levels)]
         self.returned = [self.feats // size for size in self.sizes]
         self.needed = [min(self.share, count) for count in self.returned]
@@ -92,126 +110,153 @@
         self.gain_rows = sum(self.needed) // 2
         self.message = round_up(self.gain_rows, 8)
         self.ends = [(level, n) for level in reversed(range(self.levels)) for n in range(2**level)]
-        self.permuted = self.devices <= PERMUTED
         self.messages = self.half if self.permuted else 1
-        self.parcels = self.devices if self.permuted else 1
 
     def code_row(self, feature):
         return feature // 2 + (feature % 2) * (self.share // 2)
 
 
-def prep_kernel(plan, *refs):
-    inputs, send_refs, refs = refs[:6], refs[6 : 6 + plan.parcels], refs[6 + plan.parcels :]
-    fetched, (masks, table, packed, lines, sems) = refs[:6], refs[6:]
+def fetch_kernel(plan, *refs):
+    inputs, refs = refs[:6], refs[6:]
+    (grad_ref, word_ref, row_ref, pick_ref, chosen_ref), (hess_ref, child_ref, feature_ref, bin_ref, sems) = refs[:5], refs[5:]
+    targets = (grad_ref, hess_ref, child_ref, feature_ref, bin_ref, word_ref)
     copies = [
-        pltpu.make_async_copy(source, target, sems.at[i])
-        for i, (source, target) in enumerate(zip(inputs, fetched, strict=True))
+        pltpu.make_async_copy(source, into, sems.at[i])
+        for i, (source, into) in enumerate(zip(inputs, targets, strict=True))
     ]
     for copy in copies:
         copy.start()
     rows = plan.row_dev
-    panel = lax.axis_index("feat")
-    sent = OUT_SPLIT * plan.outs_sent
-    low_at, high_at, own_at = sent, sent + plan.words, sent + plan.feats
-    at = lax.broadcasted_iota(jnp.int32, (sent, plan.outs), 0)
-    wanted = at + (at // plan.outs_sent) * (plan.outs_dev - plan.outs_sent) + lax.rem(panel, plan.pair) * plan.outs_sent
-    turn = jnp.where(wanted == lax.broadcasted_iota(jnp.int32, (sent, plan.outs), 1), 1.0, 0.0).astype(bf16)
     ahead = jnp.where(
         lax.broadcasted_iota(jnp.int32, (rows, rows), 0) <= lax.broadcasted_iota(jnp.int32, (rows, rows), 1), 1.0, 0.0
     ).astype(bf16)
     for copy in copies:
         copy.wait()
-    grad_ref, hess_ref, word_ref, child_ref, feature_ref, bin_ref = fetched
-    grads = grad_ref[...]
-    hess = hess_ref[...].astype(f32).reshape(1, rows)
-    words = word_ref[...]
-    low = jnp.bitwise_and(words, 63)
-    high = jnp.bitwise_and(jnp.right_shift(words, 6), 63)
-    codes = (low.astype(f32), high.astype(f32))
+
     nodes = [child_ref[0:1, :]]
     for level in range(1, plan.levels):
         nodes.append(nodes[-1] * 2 + child_ref[level : level + 1, :])
-
-    table[0:low_at] = lax.dot_general(turn, grads, NT, preferred_element_type=f32).astype(bf16)
-    table[low_at:high_at] = low.astype(f32).astype(bf16)
-    table[high_at:own_at] = high.astype(f32).astype(bf16)
+    row_ref[...] = jnp.zeros_like(row_ref)
+    row_ref[0:1, :] = hess_ref[...].astype(f32).reshape(1, rows)
+    for level, node in enumerate(nodes):
+        row_ref[level + 1 : level + 2, :] = node.astype(f32)
+
     at = lax.broadcasted_iota(jnp.int32, (TILE, rows), 0)
-    leaf = jnp.bitwise_and(nodes[-1], plan.leaves - 1).astype(f32)
-    table[own_at:] = jnp.where(at == 0, hess, jnp.where(at == 1, leaf, 0.0)).astype(bf16)
     side = jnp.where(at == nodes[0], 1.0, 0.0)
     rank = jnp.dot(side.astype(bf16), ahead, preferred_element_type=f32)
     slot = jnp.where(side > 0.0, rank - 1.0, -1.0)
     slot_ids = lax.broadcasted_iota(jnp.int32, (plan.slots, rows), 0).astype(f32)
     for half in range(2):
-        chosen = jnp.where(slot_ids == slot[half : half + 1], 1.0, 0.0).astype(bf16)
-        packed[half] = lax.dot_general(table[...], chosen, NT, preferred_element_type=f32)
-
-    masks[...] = jnp.zeros_like(masks)
-    leaf_count = 2 * plan.leaves
-    for level in range(plan.levels):
-        for node in range(2 ** (level + 1)):
-            slot = 2 ** (level + 1) - 2 + node
-            feature = feature_ref[slot]
-            inner = feature - panel * plan.feats
-            owned = jnp.logical_and(inner >= 0, inner < plan.feats)
-            inner = jnp.clip(inner, 0, plan.feats - 1)
-            word = word_ref[pl.ds(inner // 2, 1), :]
-            code = jnp.bitwise_and(jnp.right_shift(word, 6 * lax.rem(inner, 2)), 63)
-            here = jnp.where(nodes[level] == node, jnp.where(owned, 1.0, 0.0), 0.0)
-            left = jnp.where(code <= bin_ref[slot], here, 0.0)
-            right = here - left
-            under = 2 ** (plan.levels - level - 1)
-            for leaf in range(node * under, (node + 1) * under):
-                masks[leaf * 8 + level : leaf * 8 + level + 1, :] = left
-                at_right = leaf * 8 + plan.levels + level
-                masks[at_right : at_right + 1, :] = right
-    mask = masks[...]
-    sums = jnp.dot(mask.astype(bf16), grads, preferred_element_type=f32)
-    curv = jnp.sum(mask * hess, axis=1, keepdims=True)
-    shape = (leaf_count * 8, plan.outs)
-    line = jnp.bitwise_and(lax.broadcasted_iota(jnp.int32, shape, 0), 7)
-    lane = lax.broadcasted_iota(jnp.int32, shape, 1)
-    spread = jnp.where(lane == line, curv, 0.0).reshape(leaf_count, 8, plan.outs)
-    spread = jnp.broadcast_to(jnp.sum(spread, axis=1, keepdims=True), spread.shape)
-    sums = jnp.where(line == 2 * plan.levels, spread.reshape(shape), sums)
-    pieces = []
-    for _ in range(PIECES):
-        pieces.append(sums.astype(bf16).astype(f32))
-        sums = sums - pieces[-1]
-
-    word_share = plan.share // 2
+        chosen_ref[half] = jnp.where(slot_ids == slot[half : half + 1], 1.0, 0.0).astype(bf16)
+
+    panel = lax.axis_index("feat")
+    lane = lax.broadcasted_iota(jnp.int32, (1, plan.codes), 1)
+    pick_ref[...] = jnp.zeros_like(pick_ref)
+    for slot in range(plan.splits):
+        feature = feature_ref[slot]
+        owner = lax.div(feature, jnp.int32(plan.feats))
+        inner = feature - owner * plan.feats
+        held = jnp.bitwise_xor(owner, panel)
+        place = held * plan.words + inner // 2 + lax.rem(inner, 2) * (plan.panels * plan.words)
+        place = jnp.where(held < plan.panels, place, plan.codes)
+        pick_ref[0, slot : slot + 1, :] = jnp.where(lane == place, 1.0, 0.0)
+        pick_ref[1, slot : slot + 1, :] = jnp.full((1, plan.codes), bin_ref[slot].astype(f32))
+        pick_ref[2, slot : slot + 1, :] = jnp.full((1, plan.codes), jnp.where(held < plan.panels, 1.0, 0.0))
+
+
+def prep_kernel(plan, *refs):
+    (grad_ref, row_ref, pick_ref, chosen_ref), refs = refs[:4], refs[4:]
+    word_refs, send_refs = refs[: plan.panels], refs[plan.panels : plan.panels + plan.parcels]
+    table, packed, lines, marked = refs[plan.panels + plan.parcels :]
+    rows = plan.row_dev
+    low_at, high_at = plan.outs, plan.outs + plan.panels * plan.words
+    own_at = plan.outs + plan.codes
+    grads = grad_ref[...]
+    hess = row_ref[0:1, :]
+    nodes = [row_ref[level + 1 : level + 2, :] for level in range(plan.levels)]
+
+    turn = jnp.where(
+        lax.broadcasted_iota(jnp.int32, (plan.outs, plan.outs), 0)
+        == lax.broadcasted_iota(jnp.int32, (plan.outs, plan.outs), 1),
+        1.0,
+        0.0,
+    ).astype(bf16)
+    table[0:low_at] = lax.dot_general(turn, grads, NT, preferred_element_type=f32).astype(bf16)
+    for which, word_ref in enumerate(word_refs):
+        words = word_ref[...]
+        low = jnp.bitwise_and(words, 63)
+        high = jnp.bitwise_and(jnp.right_shift(words, 6), 63)
+        for first, codes in ((low_at, low), (high_at, high)):
+            at = first + which * plan.words
+            table[at : at + plan.words] = codes.astype(f32).astype(bf16)
+    at = lax.broadcasted_iota(jnp.int32, (TILE, rows), 0)
+    leaf = nodes[-1] - nodes[0] * plan.leaves
+    table[own_at:] = jnp.where(at == 0, hess, jnp.where(at == 1, leaf, 0.0)).astype(bf16)
+    for half in range(2):
+        packed[half] = lax.dot_general(table[...], chosen_ref[half], NT, preferred_element_type=f32)
+
+    ends = [(level, node) for level in range(plan.levels) for node in range(2 ** (level + 1))]
+    code = jnp.dot(pick_ref[0].astype(bf16), table[low_at:own_at], preferred_element_type=f32)
+    marked[...] = jnp.zeros_like(marked)
+    for slot, (level, node) in enumerate(ends):
+        here = jnp.where(nodes[level] == node, pick_ref[2, slot : slot + 1, 0:1], 0.0)
+        left = jnp.where(code[slot : slot + 1] <= pick_ref[1, slot : slot + 1, 0:1], here, 0.0)
+        marked[slot : slot + 1, :] = left
+        marked[plan.split_rows + slot : plan.split_rows + slot + 1, :] = here - left
+    mark = marked[...]
+    sums = jnp.dot(mark.astype(bf16), grads, preferred_element_type=f32)
+    curv = jnp.sum(mark * hess, axis=1, keepdims=True)
+    shape = (2 * plan.split_rows, plan.outs)
+    curv = jnp.broadcast_to(curv, shape)
+    lane = lax.broadcasted_iota(jnp.int32, (1, plan.outs), 1)
     blank = jnp.zeros((1, LANES), f32)
-    filler = jnp.zeros((plan.sent_rows - plan.misc_at - plan.misc_rows, plan.slots), f32)
-    for leaf in range(leaf_count):
-        parts = [piece[leaf * 8 + i : leaf * 8 + i + 1] for i in range(plan.score_rows) for piece in pieces]
+    filler = jnp.zeros((plan.base_rows - plan.misc_at - plan.misc_rows, plan.slots), f32)
+    for leaf in range(2 * plan.leaves):
+        places = [
+            side * plan.split_rows + 2 ** (level + 1) - 2 + (leaf >> (plan.levels - 1 - level))
+            for side in range(2)
+            for level in range(plan.levels)
+        ]
+        spread_curv = jnp.zeros((1, plan.outs), f32)
+        for i, at in enumerate(places):
+            spread_curv = jnp.where(lane == i, curv[at : at + 1], spread_curv)
+        parts = []
+        for value in [*(sums[at : at + 1] for at in places), spread_curv]:
+            for _ in range(PIECES):
+                parts.append(value.astype(bf16).astype(f32))
+                value = value - parts[-1]
         parts += [blank] * (-len(parts) % plan.spans)
         parts = [jnp.concatenate(parts[i : i + plan.spans], axis=1) for i in range(0, len(parts), plan.spans)]
         lines[leaf] = jnp.concatenate(parts + ([filler] if filler.shape[0] else []), axis=0)
-    for slot in range(plan.devices):
-        device = target(lax.axis_index("rows"), slot, plan.devices) if plan.permuted else slot
+
+    word_share = plan.share // 2
+    parity = rem(lax.axis_index("feat"), plan.panels)
+    for slot in range(plan.parcels if plan.permuted else plan.devices):
+        device = slot
+        if plan.permuted:
+            device = rem(lax.axis_index("rows") + 2 * slot + 2 - parity, plan.devices)
         half, place = div(device, plan.half), rem(device, plan.half)
         share, split = div(place, OUT_SPLIT), rem(place, OUT_SPLIT)
-        from_low = aligned(low_at + share * word_share, word_share)
-        from_high = aligned(high_at + share * word_share, word_share)
-        message = jnp.concatenate(
-            [
-                packed[half, pl.ds(from_low, word_share), :],
-                packed[half, pl.ds(from_high, word_share), :],
-                packed[half, pl.ds(aligned(split * plan.outs_sent, plan.outs_sent), plan.outs_sent), :],
-                packed[half, own_at : own_at + 2, :],
-                lines[div(device, plan.devices // leaf_count)],
-            ],
-            axis=0,
-        ).astype(bf16)
+
+        def codes(which):
+            at = [first + which * plan.words + share * word_share for first in (low_at, high_at)]
+            return [packed[half, pl.ds(aligned(first, word_share), word_share), :] for first in at]
+
+        message = [
+            *codes(0),
+            packed[half, pl.ds(aligned(split * plan.outs_dev, plan.outs_dev), plan.outs_dev), :],
+            packed[half, own_at : own_at + 2, :],
+            lines[div(device, plan.devices // (2 * plan.leaves))],
+        ]
         if plan.permuted:
-            send_refs[slot][...] = message
+            send_refs[slot][...] = jnp.concatenate(message + codes(1), axis=0).astype(bf16)
         else:
-            send_refs[0][slot] = message
+            send_refs[0][slot] = jnp.concatenate(message, axis=0).astype(bf16)
 
 
 def main_kernel(plan, chunk, *refs):
     got_refs, refs = refs[: plan.parcels], refs[plan.parcels :]
-    others, refs = refs[: plan.pair - 1], refs[plan.pair - 1 :]
+    others, refs = refs[: plan.panels - 1], refs[plan.panels - 1 :]
     out_refs, (weighted, gain_table, left_sums) = refs[: plan.messages], refs[plan.messages :]
     rows = plan.slots
     leaves, outs_dev, step = plan.leaves, plan.outs_dev, plan.step
@@ -223,7 +268,9 @@
     one = jnp.ones((), bf16)
 
     def parcel(source):
-        return got_refs[source] if plan.permuted else got_refs[0].at[source]
+        if not plan.permuted:
+            return got_refs[0].at[source]
+        return got_refs[source] if source < plan.parcels else others[0].at[source - plan.parcels]
 
     def marked(source, feature):
         row = plan.code_row(feature)
@@ -237,15 +284,12 @@
             misc = parcel(source)[plan.misc_at : plan.misc_at + 2, :].astype(f32)
             hess, node = misc[0:1], misc[1:2]
             weighted[hess_at : hess_at + TILE, columns] = jnp.where(leaf_ids == node, hess, 0.0).astype(bf16)
-            node_wide = jnp.broadcast_to(node, (plan.outs_sent, rows)).astype(bf16)
-            grads_parts = [parcel(source)[plan.grad_at : plan.grad_at + plan.outs_sent, :]]
-            grads_parts += [ref[source] for ref in others]
-            for place, grads in enumerate(grads_parts):
-                for leaf in range(leaves):
-                    at = leaf * outs_dev + place * plan.outs_sent
-                    weighted[at : at + plan.outs_sent, columns] = jnp.where(
-                        node_wide == jnp.asarray(leaf, bf16), grads, zero
-                    )
+            node_wide = jnp.broadcast_to(node, (outs_dev, rows)).astype(bf16)
+            grads = parcel(source)[plan.grad_at : plan.grad_at + outs_dev, :]
+            for leaf in range(leaves):
+                weighted[leaf * outs_dev : (leaf + 1) * outs_dev, columns] = jnp.where(
+                    node_wide == jnp.asarray(leaf, bf16), grads, zero
+                )
         for group in range(plan.share // step):
             features = order[group * step : (group + 1) * step]
             marks = jnp.concatenate(
@@ -313,16 +357,15 @@
 
 
 def score_kernel(plan, *refs):
-    got_refs, (score_ref, grads_ref) = refs[: plan.parcels], refs[plan.parcels :]
+    got_refs, (score_ref, *passed) = refs[: plan.parcels], refs[plan.parcels :]
     tail = slice(plan.misc_at + 2, plan.misc_at + plan.misc_rows)
-    wanted = slice(plan.grad_at, plan.grad_at + plan.outs_sent)
     total = jnp.zeros((plan.misc_rows - 2, plan.slots), f32)
     if plan.permuted:
         for source, ref in enumerate(got_refs):
-            grads_ref[source] = ref[wanted, :]
+            passed[0][source, : plan.share] = ref[plan.base_rows :, :]
+            passed[0][source, plan.share :] = ref[plan.share : plan.base_rows, :]
             total = total + ref[tail, :].astype(f32)
     else:
-        grads_ref[...] = got_refs[0][:, wanted, :]
         total = lax.fori_loop(0, plan.devices, lambda k, sums: sums + got_refs[0][k, tail, :].astype(f32), total)
     score_ref[...] = jnp.zeros_like(score_ref)
     for i in range(plan.score_rows):
@@ -375,44 +418,62 @@
     plan = Plan(lax.axis_size("rows"), lax.axis_size("feat"), gradients, bin_words, children)
     params = pltpu.CompilerParams(vmem_limit_bytes=VMEM_BYTES)
 
-    table_rows = OUT_SPLIT * plan.outs_sent + plan.feats + TILE
-    inputs = (gradients, hessians, bin_words, children, split_feature, split_bin)
-    inputs = tuple(pltpu.with_memory_space_constraint(a, pltpu.HBM) for a in inputs)
+    inputs = (gradients, hessians, children, split_feature, split_bin, bin_words)
+    crossed = [flipped(bin_words, 1)] if plan.permuted else []
+    row_dev, table_rows = plan.row_dev, plan.outs + plan.codes + TILE
+    grads, words, row_values, picks, chosen = pl.pallas_call(
+        functools.partial(fetch_kernel, plan),
+        out_shape=(
+            jax.ShapeDtypeStruct(gradients.shape, bf16),
+            jax.ShapeDtypeStruct(bin_words.shape, jnp.int32),
+            jax.ShapeDtypeStruct((8, row_dev), f32),
+            jax.ShapeDtypeStruct((3, plan.split_rows, plan.codes), f32),
+            jax.ShapeDtypeStruct((2, plan.slots, row_dev), bf16),
+        ),
+        in_specs=[pl.BlockSpec(memory_space=pltpu.HBM)] * len(inputs),
+        out_specs=[whole()] * 5,
+        scratch_shapes=[
+            pltpu.VMEM(hessians.shape, bf16),
+            pltpu.VMEM(children.shape, jnp.int32),
+            pltpu.SMEM(split_feature.shape, jnp.int32),
+            pltpu.SMEM(split_bin.shape, jnp.int32),
+            pltpu.SemaphoreType.DMA((len(inputs),)),
+        ],
+        cost_estimate=pl.CostEstimate(flops=10**9, bytes_accessed=10**6, transcendentals=0),
+        compiler_params=params,
+        name="fetch",
+    )(*(pltpu.with_memory_space_constraint(a, pltpu.HBM) for a in inputs))
     parcel = (plan.sent_rows, plan.slots) if plan.permuted else (plan.devices, plan.sent_rows, plan.slots)
     parcels = pl.pallas_call(
         functools.partial(prep_kernel, plan),
         out_shape=[jax.ShapeDtypeStruct(parcel, bf16)] * plan.parcels,
-        in_specs=[pl.BlockSpec(memory_space=pltpu.HBM)] * len(inputs),
+        in_specs=[whole()] * (4 + plan.panels),
         out_specs=[whole()] * plan.parcels,
         scratch_shapes=[
-            *(pltpu.VMEM(a.shape, a.dtype) for a in inputs[:4]),
-            *(pltpu.SMEM(a.shape, a.dtype) for a in inputs[4:]),
-            pltpu.VMEM((2 * plan.leaves * 8, plan.row_dev), f32),
-            pltpu.VMEM((table_rows, plan.row_dev), bf16),
+            pltpu.VMEM((table_rows, row_dev), bf16),
             pltpu.VMEM((2, table_rows, plan.slots), f32),
-            pltpu.VMEM((2 * plan.leaves, plan.sent_rows - plan.misc_at - 2, plan.slots), f32),
-            pltpu.SemaphoreType.DMA((len(inputs),)),
+            pltpu.VMEM((2 * plan.leaves, plan.base_rows - plan.misc_at - 2, plan.slots), f32),
+            pltpu.VMEM((2 * plan.split_rows, row_dev), f32),
         ],
         compiler_params=params,
         name="prep",
-    )(*inputs)
-
+    )(grads, row_values, picks, chosen, words, *crossed)
+
+    shapes = [jax.ShapeDtypeStruct((8, plan.outs), f32)]
     if plan.permuted:
-        got = exchanged(parcels, plan.devices, plan.devices)
+        got = spread(parcels, plan)
+        shapes.append(jax.ShapeDtypeStruct((plan.parcels, plan.base_rows, plan.slots), bf16))
     else:
         got = [lax.all_to_all(parcels[0], "rows", 0, 0)]
-    scores, grads_part = pl.pallas_call(
+    scores, *passed = pl.pallas_call(
         functools.partial(score_kernel, plan),
-        out_shape=(
-            jax.ShapeDtypeStruct((8, plan.outs), f32),
-            jax.ShapeDtypeStruct((plan.devices, plan.outs_sent, plan.slots), bf16),
-        ),
+        out_shape=shapes,
         in_specs=[whole()] * plan.parcels,
-        out_specs=(whole(), whole()),
+        out_specs=[whole()] * len(shapes),
         compiler_params=params,
         name="scores",
     )(*got)
-    arrays = got + ([flipped(grads_part, 1)] if plan.pair > 1 else [])
+    arrays = got + [flipped(block, 1) for block in passed]
     score_parts = [scores] + [flipped(scores, away) for away in range(1, lax.axis_size("feat"))]
 
     chunk = max(1, min(plan.devices, 4096 // plan.slots))

time: 33.3 us -> 31.7 us (0.952)
  starting transfers between devices: 20 us -> 17.4 us
  waiting for transfers between devices: 5.68 us -> 6.23 us
  Pallas kernels: 6.8 us -> 7.26 us
    ppermute x10 -> x3, starting transfers between devices: 17.7 us -> 5.75 us  [exchanged(): moved.append(lax.ppermute(blocks[slot], 'rows', route))]
    ppermute x0 -> x4, starting transfers between devices: none -> 7.37 us  [spread(): moved.append(lax.ppermute(block, ('rows', 'feat'), route))]
    ppermute x0 -> x4, waiting for transfers between devices: none -> 4.24 us  [spread(): moved.append(lax.ppermute(block, ('rows', 'feat'), route))]
    ppermute x10 -> x3, waiting for transfers between devices: 5.67 us -> 1.98 us  [exchanged(): moved.append(lax.ppermute(blocks[slot], 'rows', route))]
    ppermute x4 -> x5, starting transfers between devices: 2.28 us -> 4.25 us  [flipped(): return lax.ppermute(block, 'feat', [(p, p ^ bits) for p in range(count)])]
    pallas_call x1 -> x2, Pallas kernels: 0.03 us -> 1.33 us  [the longest x1 1.29 us: on_device(): pl.pallas_call(functools.partial(fetch_kernel, plan), out_shape=(jax.Shap...]
    pallas_call x1, Pallas kernels: 1.68 us -> 0.82 us  [on_device(): pl.pallas_call(functools.partial(prep_kernel, plan), out_shape=[jax.Shape...]
  transfers between devices with their start and end apart: 14 -> 12, of which waited for: 7 -> 4; matrix products, arithmetic and copies ran while one was open for 0% -> 0% of each run, Pallas kernels for 13% -> 18%
where the time goes in v7:
time: 31.7 us; the launch traced here: 31.6 us
  starting transfers between devices  17.4 us (55%)
  Pallas kernels  7.26 us (23%)
  waiting for transfers between devices  6.23 us (20%)
  between operations  0.7 us (2%)
    ppermute x4, starting transfers between devices, spread(): moved.append(lax.ppermute(block, ('rows', 'feat'), route))  7.37 us
    ppermute x3, starting transfers between devices, exchanged(): moved.append(lax.ppermute(blocks[slot], 'rows', route))  5.75 us
    pallas_call x1, Pallas kernels, on_device(): pl.pallas_call(functools.partial(main_kernel, plan, chunk), out_shape=[ja...  4.39 us
    ppermute x5, starting transfers between devices, flipped(): return lax.ppermute(block, 'feat', [(p, p ^ bits) for p in range(count)])  4.25 us
    ppermute x4, waiting for transfers between devices, spread(): moved.append(lax.ppermute(block, ('rows', 'feat'), route))  4.24 us
    ppermute x3, waiting for transfers between devices, exchanged(): moved.append(lax.ppermute(blocks[slot], 'rows', route))  1.98 us
    pallas_call x1, Pallas kernels, on_device(): pl.pallas_call(functools.partial(fetch_kernel, plan), out_shape=(jax.Shap...  1.29 us
    pallas_call x1, Pallas kernels, on_device(): pl.pallas_call(functools.partial(prep_kernel, plan), out_shape=[jax.Shape...  0.82 us
  transfers between devices with their start and end apart: 12, of which 4 were waited for; matrix products, arithmetic and copies ran while one was open for 0% of the time, Pallas kernels for 18%

profile of v7, /device:TPU:0, one launch (start us, length us, event | category | flops | bytes accessed | tf_op | source)
XLA Modules:
  0.0 31.6 jit_solution(6547399364467594869)
XLA Ops:
  0.6 0.5 %collective-permute-start = (s32[32,512]{1,0:T(8,128)}, s32[32,512]{1,0:T(8,128)S(1)}, u32[]{:S(2)}, u32[]{:S(2)}) collective-permute-start(s32[32,512]{1,0:T(8,128)} %refs_5_.1), channel_id=1, source_target_pairs={{0,1},{1,0},{2,3},{3,2},{4,5},{5,4},{6,7},{7,6},{8,9},{9,8},{10,11... | collective-permute-start | bytes 196616 | tf_op jit(solution)/shard_map/ppermute | solution.py:414
  1.2 1.3 %fetch.1 = (bf16[512,128]{1,0:T(8,128)(2,1)S(1)}, s32[32,512]{1,0:T(8,128)S(1)}, f32[8,512]{1,0:T(8,128)S(1)}, f32[3,16,128]{2,1,0:T(8,128)S(1)}, bf16[2,384,512]{2,1,0:T(8,128)(2,1)S(1)}) custom-call(bf16[512,128]{1,0:T(8,128)(2,1)} %refs_0_.1, bf16[512]{0:T(512)(128)(2,1)} %refs_1_.1, s32[3,512]{1,0:T(4,128)} %refs_2_.1, s32[14]{0:T(128)} %refs_3_.1, ...), custom_call_target="tpu_custom_call" | custom-call | flops 1000000000 | bytes 1000000 | tf_op jit(solution)/shard_map/fetch/pallas_call | solution.py:424
  2.4 0.0 collective-permute-done.refs_5_
  2.5 0.8 %prep.1 = (bf16[136,384]{1,0:T(8,128)(2,1)S(1)}, bf16[136,384]{1,0:T(8,128)(2,1)S(1)}, bf16[136,384]{1,0:T(8,128)(2,1)S(1)}, bf16[136,384]{1,0:T(8,128)(2,1)S(1)}) custom-call(bf16[512,128]{1,0:T(8,128)(2,1)S(1)} %get-tuple-element.27.refs_0_, f32[8,512]{1,0:T(8,128)S(1)} %get-tuple-element.28.refs_1_, f32[3,16,128]{2,1,0:T(8,128)S(1)} %get-tuple-element.29.refs_2_, ...), custom_call_target="tpu_custom_call" | custom-call | tf_op jit(solution)/shard_map/prep/pallas_call | solution.py:447
  3.3 2.8 %collective-permute-start.1 = (bf16[136,384]{1,0:T(8,128)(2,1)S(1)}, bf16[136,384]{1,0:T(8,128)(2,1)S(1)}, u32[]{:S(2)}, u32[]{:S(2)}) collective-permute-start(bf16[136,384]{1,0:T(8,128)(2,1)S(1)} %get-tuple-element.32), channel_id=1, source_target_pairs={{0,8},{1,5},{2,10},{3,7},{4,12},{5,9},{6,14},{7,11},{8,16},{9,13},... | collective-permute-start | bytes 313352 | tf_op jit(solution)/shard_map/ppermute | solution.py:69
  6.1 2.6 %collective-permute-start.2 = (bf16[136,384]{1,0:T(8,128)(2,1)S(1)}, bf16[136,384]{1,0:T(8,128)(2,1)S(1)}, u32[]{:S(2)}, u32[]{:S(2)}) collective-permute-start(bf16[136,384]{1,0:T(8,128)(2,1)S(1)} %get-tuple-element.33), channel_id=1, source_target_pairs={{0,16},{1,13},{2,18},{3,15},{4,20},{5,17},{6,22},{7,19},{8,24},{9,... | collective-permute-start | bytes 313352 | tf_op jit(solution)/shard_map/ppermute | solution.py:69
  8.7 1.3 %collective-permute-start.3 = (bf16[136,384]{1,0:T(8,128)(2,1)S(1)}, bf16[136,384]{1,0:T(8,128)(2,1)S(1)}, u32[]{:S(2)}, u32[]{:S(2)}) collective-permute-start(bf16[136,384]{1,0:T(8,128)(2,1)S(1)} %get-tuple-element.34), channel_id=1, source_target_pairs={{0,24},{1,21},{2,26},{3,23},{4,28},{5,25},{6,30},{7,27},{8,0},{9,2... | collective-permute-start | bytes 313352 | tf_op jit(solution)/shard_map/ppermute | solution.py:69
  10.0 0.7 %collective-permute-start.4 = (bf16[136,384]{1,0:T(8,128)(2,1)S(1)}, bf16[136,384]{1,0:T(8,128)(2,1)S(1)}, u32[]{:S(2)}, u32[]{:S(2)}) collective-permute-start(bf16[136,384]{1,0:T(8,128)(2,1)S(1)} %get-tuple-element.35), channel_id=1, source_target_pairs={{0,0},{1,29},{2,2},{3,31},{4,4},{5,1},{6,6},{7,3},{8,8},{9,5},{10,... | collective-permute-start | bytes 313352 | tf_op jit(solution)/shard_map/ppermute | solution.py:69
  10.7 0.1 collective-permute-done.1.refs_0_
  10.8 4.1 %collective-permute-done.2.refs_1_ = bf16[136,384]{1,0:T(8,128)(2,1)S(1)} collective-permute-done((bf16[136,384]{1,0:T(8,128)(2,1)S(1)}, bf16[136,384]{1,0:T(8,128)(2,1)S(1)}, u32[]{:S(2)}, u32[]{:S(2)}) %collective-permute-start.2) | collective-permute-done | bytes 104480 | tf_op jit(solution)/shard_map/ppermute | solution.py:69
  14.9 0.0 collective-permute-done.3.refs_2_
  14.9 0.0 collective-permute-done.4.refs_3_
  14.9 1.9 %collective-permute-start.5 = (bf16[4,104,384]{2,1,0:T(8,128)(2,1)S(1)}, bf16[4,104,384]{2,1,0:T(8,128)(2,1)S(1)}, u32[]{:S(2)}, u32[]{:S(2)}) collective-permute-start(bf16[4,104,384]{2,1,0:T(8,128)(2,1)S(1)} %get-tuple-element.36), channel_id=1, source_target_pairs={{0,1},{1,0},{2,3},{3,2},{4,5},{5,4},{6,7},{7,6},{8,9},{9,8},{10,11... | collective-permute-start | bytes 958472 | tf_op jit(solution)/shard_map/ppermute | solution.py:414
  16.8 1.2 %collective-permute-start.8 = (f32[8,128]{1,0:T(8,128)S(1)}, f32[8,128]{1,0:T(8,128)S(1)}, u32[]{:S(2)}, u32[]{:S(2)}) collective-permute-start(f32[8,128]{1,0:T(8,128)S(1)} %get-tuple-element.46.refs_4_), channel_id=1, source_target_pairs={{0,3},{1,2},{2,1},{3,0},{4,7},{5,6},{6,5},{7,4},{8,11},{9,10},{10,... | collective-permute-start | bytes 12296 | tf_op jit(solution)/shard_map/ppermute | solution.py:414
  18.0 0.5 %collective-permute-start.7 = (f32[8,128]{1,0:T(8,128)S(1)}, f32[8,128]{1,0:T(8,128)S(1)}, u32[]{:S(2)}, u32[]{:S(2)}) collective-permute-start(f32[8,128]{1,0:T(8,128)S(1)} %get-tuple-element.46.refs_4_), channel_id=1, source_target_pairs={{0,2},{1,3},{2,0},{3,1},{4,6},{5,7},{6,4},{7,5},{8,10},{9,11},{10,... | collective-permute-start | bytes 12296 | tf_op jit(solution)/shard_map/ppermute | solution.py:414
  18.5 0.2 collective-permute-start.6
  18.7 0.0 collective-permute-done.5.refs_4_
  18.7 4.4 %gains.1 = (f32[40,128]{1,0:T(8,128)S(1)}, f32[40,128]{1,0:T(8,128)S(1)}, f32[40,128]{1,0:T(8,128)S(1)}, f32[40,128]{1,0:T(8,128)S(1)}) custom-call(bf16[136,384]{1,0:T(8,128)(2,1)S(1)} %collective-permute-done.1.refs_0_, bf16[136,384]{1,0:T(8,128)(2,1)S(1)} %collective-permute-done.2.refs_1_, bf16[136,384]{1,0:T(8,128)(2,1)S(1)} %collective-permute-done.3.refs_2_, ...), custom_call_target="tpu_custom_call" | custom-call | flops 3422552064 | bytes 1671168 | tf_op jit(solution)/shard_map/gains/pallas_call | solution.py:484
  23.1 0.0 collective-permute-done.8.refs_7_
  23.1 0.0 collective-permute-done.7.refs_6_
  23.1 0.0 collective-permute-done.6.refs_5_
  23.1 2.1 %collective-permute-start.9 = (f32[40,128]{1,0:T(8,128)S(1)}, f32[40,128]{1,0:T(8,128)S(1)}, u32[]{:S(2)}, u32[]{:S(2)}) collective-permute-start(f32[40,128]{1,0:T(8,128)S(1)} %get-tuple-element.43), channel_id=1, source_target_pairs={{0,4},{4,8},{8,12},{12,0},{16,20},{20,24},{24,28},{28,16},{1,5},{5... | collective-permute-start | bytes 61448 | tf_op jit(solution)/shard_map/ppermute | solution.py:56
  25.2 1.9 %collective-permute-start.10 = (f32[40,128]{1,0:T(8,128)S(1)}, f32[40,128]{1,0:T(8,128)S(1)}, u32[]{:S(2)}, u32[]{:S(2)}) collective-permute-start(f32[40,128]{1,0:T(8,128)S(1)} %get-tuple-element.44), channel_id=1, source_target_pairs={{0,8},{4,12},{8,0},{12,4},{16,24},{20,28},{24,16},{28,20},{1,9},{5... | collective-permute-start | bytes 61448 | tf_op jit(solution)/shard_map/ppermute | solution.py:56
  27.1 1.8 %collective-permute-start.11 = (f32[40,128]{1,0:T(8,128)S(1)}, f32[40,128]{1,0:T(8,128)S(1)}, u32[]{:S(2)}, u32[]{:S(2)}) collective-permute-start(f32[40,128]{1,0:T(8,128)S(1)} %get-tuple-element.45), channel_id=1, source_target_pairs={{0,12},{4,0},{8,4},{12,8},{16,28},{20,16},{24,20},{28,24},{1,13},{... | collective-permute-start | bytes 61448 | tf_op jit(solution)/shard_map/ppermute | solution.py:56
  28.9 0.0 collective-permute-done.9.refs_1_
  28.9 0.1 collective-permute-done.10.refs_2_
  29.0 1.9 %collective-permute-done.11.refs_3_ = f32[40,128]{1,0:T(8,128)S(1)} collective-permute-done((f32[40,128]{1,0:T(8,128)S(1)}, f32[40,128]{1,0:T(8,128)S(1)}, u32[]{:S(2)}, u32[]{:S(2)}) %collective-permute-start.11) | collective-permute-done | bytes 20512 | tf_op jit(solution)/shard_map/ppermute | solution.py:56
  30.8 0.7 %finish.1 = (f32[16,64]{1,0:T(8,128)}, f32[32,64]{1,0:T(8,128)}, f32[64,64]{1,0:T(8,128)}, f32[3,1,2,128]{3,2,1,0:T(2,128)}) custom-call(f32[40,128]{1,0:T(8,128)S(1)} %get-tuple-element.42.refs_0_, f32[40,128]{1,0:T(8,128)S(1)} %collective-permute-done.9.refs_1_, f32[40,128]{1,0:T(8,128)S(1)} %collective-permute-done.10.refs_2_, ...), custom_call_target="tpu_custom_call" | custom-call | tf_op jit(solution)/shard_map/finish/pallas_call | solution.py:513
  (1 shorter events, 0.0 us)
Async XLA Ops:
  0.6 1.8 %collective-permute-start = (s32[32,512]{1,0:T(8,128)}, s32[32,512]{1,0:T(8,128)S(1)}, u32[]{:S(2)}, u32[]{:S(2)}) collective-permute-start(s32[32,512]{1,0:T(8,128)} %refs_5_.1), channel_id=1, source_target_pairs={{0,1},{1,0},{2,3},{3,2},{4,5},{5,4},{6,7},{7,6},{8,9},{9,8},{10,11... | collective-permute-start | bytes 196616 | tf_op jit(solution)/shard_map/ppermute | solution.py:414
  3.3 7.5 %collective-permute-start.1 = (bf16[136,384]{1,0:T(8,128)(2,1)S(1)}, bf16[136,384]{1,0:T(8,128)(2,1)S(1)}, u32[]{:S(2)}, u32[]{:S(2)}) collective-permute-start(bf16[136,384]{1,0:T(8,128)(2,1)S(1)} %get-tuple-element.32), channel_id=1, source_target_pairs={{0,8},{1,5},{2,10},{3,7},{4,12},{5,9},{6,14},{7,11},{8,16},{9,13},... | collective-permute-start | bytes 313352 | tf_op jit(solution)/shard_map/ppermute | solution.py:69
  6.1 8.8 %collective-permute-start.2 = (bf16[136,384]{1,0:T(8,128)(2,1)S(1)}, bf16[136,384]{1,0:T(8,128)(2,1)S(1)}, u32[]{:S(2)}, u32[]{:S(2)}) collective-permute-start(bf16[136,384]{1,0:T(8,128)(2,1)S(1)} %get-tuple-element.33), channel_id=1, source_target_pairs={{0,16},{1,13},{2,18},{3,15},{4,20},{5,17},{6,22},{7,19},{8,24},{9,... | collective-permute-start | bytes 313352 | tf_op jit(solution)/shard_map/ppermute | solution.py:69
  8.7 6.2 %collective-permute-start.3 = (bf16[136,384]{1,0:T(8,128)(2,1)S(1)}, bf16[136,384]{1,0:T(8,128)(2,1)S(1)}, u32[]{:S(2)}, u32[]{:S(2)}) collective-permute-start(bf16[136,384]{1,0:T(8,128)(2,1)S(1)} %get-tuple-element.34), channel_id=1, source_target_pairs={{0,24},{1,21},{2,26},{3,23},{4,28},{5,25},{6,30},{7,27},{8,0},{9,2... | collective-permute-start | bytes 313352 | tf_op jit(solution)/shard_map/ppermute | solution.py:69
  10.0 4.9 %collective-permute-start.4 = (bf16[136,384]{1,0:T(8,128)(2,1)S(1)}, bf16[136,384]{1,0:T(8,128)(2,1)S(1)}, u32[]{:S(2)}, u32[]{:S(2)}) collective-permute-start(bf16[136,384]{1,0:T(8,128)(2,1)S(1)} %get-tuple-element.35), channel_id=1, source_target_pairs={{0,0},{1,29},{2,2},{3,31},{4,4},{5,1},{6,6},{7,3},{8,8},{9,5},{10,... | collective-permute-start | bytes 313352 | tf_op jit(solution)/shard_map/ppermute | solution.py:69
  14.9 3.7 %collective-permute-start.5 = (bf16[4,104,384]{2,1,0:T(8,128)(2,1)S(1)}, bf16[4,104,384]{2,1,0:T(8,128)(2,1)S(1)}, u32[]{:S(2)}, u32[]{:S(2)}) collective-permute-start(bf16[4,104,384]{2,1,0:T(8,128)(2,1)S(1)} %get-tuple-element.36), channel_id=1, source_target_pairs={{0,1},{1,0},{2,3},{3,2},{4,5},{5,4},{6,7},{7,6},{8,9},{9,8},{10,11... | collective-permute-start | bytes 958472 | tf_op jit(solution)/shard_map/ppermute | solution.py:414
  16.8 6.3 %collective-permute-start.8 = (f32[8,128]{1,0:T(8,128)S(1)}, f32[8,128]{1,0:T(8,128)S(1)}, u32[]{:S(2)}, u32[]{:S(2)}) collective-permute-start(f32[8,128]{1,0:T(8,128)S(1)} %get-tuple-element.46.refs_4_), channel_id=1, source_target_pairs={{0,3},{1,2},{2,1},{3,0},{4,7},{5,6},{6,5},{7,4},{8,11},{9,10},{10,... | collective-permute-start | bytes 12296 | tf_op jit(solution)/shard_map/ppermute | solution.py:414
  18.0 5.1 %collective-permute-start.7 = (f32[8,128]{1,0:T(8,128)S(1)}, f32[8,128]{1,0:T(8,128)S(1)}, u32[]{:S(2)}, u32[]{:S(2)}) collective-permute-start(f32[8,128]{1,0:T(8,128)S(1)} %get-tuple-element.46.refs_4_), channel_id=1, source_target_pairs={{0,2},{1,3},{2,0},{3,1},{4,6},{5,7},{6,4},{7,5},{8,10},{9,11},{10,... | collective-permute-start | bytes 12296 | tf_op jit(solution)/shard_map/ppermute | solution.py:414
  18.5 4.6 %collective-permute-start.6 = (f32[8,128]{1,0:T(8,128)S(1)}, f32[8,128]{1,0:T(8,128)S(1)}, u32[]{:S(2)}, u32[]{:S(2)}) collective-permute-start(f32[8,128]{1,0:T(8,128)S(1)} %get-tuple-element.46.refs_4_), channel_id=1, source_target_pairs={{0,1},{1,0},{2,3},{3,2},{4,5},{5,4},{6,7},{7,6},{8,9},{9,8},{10,11... | collective-permute-start | bytes 12296 | tf_op jit(solution)/shard_map/ppermute | solution.py:414
  23.1 5.8 %collective-permute-start.9 = (f32[40,128]{1,0:T(8,128)S(1)}, f32[40,128]{1,0:T(8,128)S(1)}, u32[]{:S(2)}, u32[]{:S(2)}) collective-permute-start(f32[40,128]{1,0:T(8,128)S(1)} %get-tuple-element.43), channel_id=1, source_target_pairs={{0,4},{4,8},{8,12},{12,0},{16,20},{20,24},{24,28},{28,16},{1,5},{5... | collective-permute-start | bytes 61448 | tf_op jit(solution)/shard_map/ppermute | solution.py:56
  25.2 3.8 %collective-permute-start.10 = (f32[40,128]{1,0:T(8,128)S(1)}, f32[40,128]{1,0:T(8,128)S(1)}, u32[]{:S(2)}, u32[]{:S(2)}) collective-permute-start(f32[40,128]{1,0:T(8,128)S(1)} %get-tuple-element.44), channel_id=1, source_target_pairs={{0,8},{4,12},{8,0},{12,4},{16,24},{20,28},{24,16},{28,20},{1,9},{5... | collective-permute-start | bytes 61448 | tf_op jit(solution)/shard_map/ppermute | solution.py:56
  27.1 3.8 %collective-permute-start.11 = (f32[40,128]{1,0:T(8,128)S(1)}, f32[40,128]{1,0:T(8,128)S(1)}, u32[]{:S(2)}, u32[]{:S(2)}) collective-permute-start(f32[40,128]{1,0:T(8,128)S(1)} %get-tuple-element.45), channel_id=1, source_target_pairs={{0,12},{4,0},{8,4},{12,8},{16,28},{20,16},{24,20},{28,24},{1,13},{... | collective-permute-start | bytes 61448 | tf_op jit(solution)/shard_map/ppermute | solution.py:56

commit v8 on v7

--- a/solution.py
+++ b/solution.py
@@ -256,7 +256,8 @@
 
 def main_kernel(plan, chunk, *refs):
     got_refs, refs = refs[: plan.parcels], refs[plan.parcels :]
-    others, refs = refs[: plan.panels - 1], refs[plan.panels - 1 :]
+    if plan.permuted:
+        got_refs, refs = got_refs + tuple(refs[0].at[k] for k in range(plan.parcels)), refs[1:]
     out_refs, (weighted, gain_table, left_sums) = refs[: plan.messages], refs[plan.messages :]
     rows = plan.slots
     leaves, outs_dev, step = plan.leaves, plan.outs_dev, plan.step
@@ -268,9 +269,7 @@
     one = jnp.ones((), bf16)
 
     def parcel(source):
-        if not plan.permuted:
-            return got_refs[0].at[source]
-        return got_refs[source] if source < plan.parcels else others[0].at[source - plan.parcels]
+        return got_refs[source] if plan.permuted else got_refs[0].at[source]
 
     def marked(source, feature):
         row = plan.code_row(feature)
@@ -459,12 +458,13 @@
         name="prep",
     )(grads, row_values, picks, chosen, words, *crossed)
 
+    if plan.permuted:
+        got = spread(parcels, plan)
+    else:
+        got = [lax.all_to_all(parcels[0], "rows", 0, 0)]
     shapes = [jax.ShapeDtypeStruct((8, plan.outs), f32)]
     if plan.permuted:
-        got = spread(parcels, plan)
         shapes.append(jax.ShapeDtypeStruct((plan.parcels, plan.base_rows, plan.slots), bf16))
-    else:
-        got = [lax.all_to_all(parcels[0], "rows", 0, 0)]
     scores, *passed = pl.pallas_call(
         functools.partial(score_kernel, plan),
         out_shape=shapes,
@@ -474,7 +474,7 @@
         name="scores",
     )(*got)
     arrays = got + [flipped(block, 1) for block in passed]
-    score_parts = [scores] + [flipped(scores, away) for away in range(1, lax.axis_size("feat"))]
+    far = [flipped(scores, away) for away in range(plan.panels, lax.axis_size("feat"), plan.panels)]
 
     chunk = max(1, min(plan.devices, 4096 // plan.slots))
     while plan.devices % chunk:
@@ -500,7 +500,9 @@
         name="gains",
     )(*arrays)
 
-    messages, score_parts = lax.optimization_barrier((list(messages), score_parts))
+    messages, far = lax.optimization_barrier((list(messages), far))
+    scores = sum(far, scores)
+    score_parts = [scores] + ([flipped(scores, 1)] if plan.permuted else [])
     if plan.permuted:
         messages = exchanged(messages, plan.half, plan.devices)
     else:

time: 31.7 us -> 31.4 us (level)
  starting transfers between devices: 17.4 us -> 17 us
    ppermute x5 -> x4, waiting for transfers between devices: 0.01 us -> 1.17 us  [flipped(): return lax.ppermute(block, 'feat', [(p, p ^ bits) for p in range(count)])]
    ppermute x3, waiting for transfers between devices: 1.98 us -> 0.82 us  [exchanged(): moved.append(lax.ppermute(blocks[slot], 'rows', route))]
    ppermute x5 -> x4, starting transfers between devices: 4.25 us -> 3.87 us  [flipped(): return lax.ppermute(block, 'feat', [(p, p ^ bits) for p in range(count)])]
  transfers between devices with their start and end apart: 12 -> 11, of which waited for: 4 -> 4; matrix products, arithmetic and copies ran while one was open for 0% -> 0% of each run, Pallas kernels for 18% -> 18%
where the time goes in v8:
time: 31.4 us; the launch traced here: 31.2 us
  starting transfers between devices  17 us (54%)
  Pallas kernels  7.26 us (23%)
  waiting for transfers between devices  6.23 us (20%)
  between operations  0.69 us (2%)
    ppermute x4, starting transfers between devices, spread(): moved.append(lax.ppermute(block, ('rows', 'feat'), route))  7.37 us
    ppermute x3, starting transfers between devices, exchanged(): moved.append(lax.ppermute(blocks[slot], 'rows', route))  5.78 us
    pallas_call x1, Pallas kernels, on_device(): pl.pallas_call(functools.partial(main_kernel, plan, chunk), out_shape=[ja...  4.4 us
    ppermute x4, waiting for transfers between devices, spread(): moved.append(lax.ppermute(block, ('rows', 'feat'), route))  4.24 us
    ppermute x4, starting transfers between devices, flipped(): return lax.ppermute(block, 'feat', [(p, p ^ bits) for p in range(count)])  3.87 us
    pallas_call x1, Pallas kernels, on_device(): pl.pallas_call(functools.partial(fetch_kernel, plan), out_shape=(jax.Shap...  1.29 us
    ppermute x4, waiting for transfers between devices, flipped(): return lax.ppermute(block, 'feat', [(p, p ^ bits) for p in range(count)])  1.17 us
    ppermute x3, waiting for transfers between devices, exchanged(): moved.append(lax.ppermute(blocks[slot], 'rows', route))  0.82 us
  transfers between devices with their start and end apart: 11, of which 4 were waited for; matrix products, arithmetic and copies ran while one was open for 0% of the time, Pallas kernels for 18%

profile of v8, /device:TPU:0, one launch (start us, length us, event | category | flops | bytes accessed | tf_op | source)
XLA Modules:
  0.0 31.2 jit_solution(630935472878391716)
XLA Ops:
  0.6 0.5 %collective-permute-start = (s32[32,512]{1,0:T(8,128)}, s32[32,512]{1,0:T(8,128)S(1)}, u32[]{:S(2)}, u32[]{:S(2)}) collective-permute-start(s32[32,512]{1,0:T(8,128)} %refs_5_.1), channel_id=1, source_target_pairs={{0,1},{1,0},{2,3},{3,2},{4,5},{5,4},{6,7},{7,6},{8,9},{9,8},{10,11... | collective-permute-start | bytes 196616 | tf_op jit(solution)/shard_map/ppermute | solution.py:413
  1.2 1.3 %fetch.1 = (bf16[512,128]{1,0:T(8,128)(2,1)S(1)}, s32[32,512]{1,0:T(8,128)S(1)}, f32[8,512]{1,0:T(8,128)S(1)}, f32[3,16,128]{2,1,0:T(8,128)S(1)}, bf16[2,384,512]{2,1,0:T(8,128)(2,1)S(1)}) custom-call(bf16[512,128]{1,0:T(8,128)(2,1)} %refs_0_.1, bf16[512]{0:T(512)(128)(2,1)} %refs_1_.1, s32[3,512]{1,0:T(4,128)} %refs_2_.1, s32[14]{0:T(128)} %refs_3_.1, ...), custom_call_target="tpu_custom_call" | custom-call | flops 1000000000 | bytes 1000000 | tf_op jit(solution)/shard_map/fetch/pallas_call | solution.py:423
  2.4 0.0 collective-permute-done.refs_5_
  2.5 0.8 %prep.1 = (bf16[136,384]{1,0:T(8,128)(2,1)S(1)}, bf16[136,384]{1,0:T(8,128)(2,1)S(1)}, bf16[136,384]{1,0:T(8,128)(2,1)S(1)}, bf16[136,384]{1,0:T(8,128)(2,1)S(1)}) custom-call(bf16[512,128]{1,0:T(8,128)(2,1)S(1)} %get-tuple-element.24.refs_0_, f32[8,512]{1,0:T(8,128)S(1)} %get-tuple-element.25.refs_1_, f32[3,16,128]{2,1,0:T(8,128)S(1)} %get-tuple-element.26.refs_2_, ...), custom_call_target="tpu_custom_call" | custom-call | tf_op jit(solution)/shard_map/prep/pallas_call | solution.py:446
  3.3 2.8 %collective-permute-start.1 = (bf16[136,384]{1,0:T(8,128)(2,1)S(1)}, bf16[136,384]{1,0:T(8,128)(2,1)S(1)}, u32[]{:S(2)}, u32[]{:S(2)}) collective-permute-start(bf16[136,384]{1,0:T(8,128)(2,1)S(1)} %get-tuple-element.29), channel_id=1, source_target_pairs={{0,8},{1,5},{2,10},{3,7},{4,12},{5,9},{6,14},{7,11},{8,16},{9,13},... | collective-permute-start | bytes 313352 | tf_op jit(solution)/shard_map/ppermute | solution.py:69
  6.1 2.6 %collective-permute-start.2 = (bf16[136,384]{1,0:T(8,128)(2,1)S(1)}, bf16[136,384]{1,0:T(8,128)(2,1)S(1)}, u32[]{:S(2)}, u32[]{:S(2)}) collective-permute-start(bf16[136,384]{1,0:T(8,128)(2,1)S(1)} %get-tuple-element.30), channel_id=1, source_target_pairs={{0,16},{1,13},{2,18},{3,15},{4,20},{5,17},{6,22},{7,19},{8,24},{9,... | collective-permute-start | bytes 313352 | tf_op jit(solution)/shard_map/ppermute | solution.py:69
  8.7 1.3 %collective-permute-start.3 = (bf16[136,384]{1,0:T(8,128)(2,1)S(1)}, bf16[136,384]{1,0:T(8,128)(2,1)S(1)}, u32[]{:S(2)}, u32[]{:S(2)}) collective-permute-start(bf16[136,384]{1,0:T(8,128)(2,1)S(1)} %get-tuple-element.31), channel_id=1, source_target_pairs={{0,24},{1,21},{2,26},{3,23},{4,28},{5,25},{6,30},{7,27},{8,0},{9,2... | collective-permute-start | bytes 313352 | tf_op jit(solution)/shard_map/ppermute | solution.py:69
  10.0 0.7 %collective-permute-start.4 = (bf16[136,384]{1,0:T(8,128)(2,1)S(1)}, bf16[136,384]{1,0:T(8,128)(2,1)S(1)}, u32[]{:S(2)}, u32[]{:S(2)}) collective-permute-start(bf16[136,384]{1,0:T(8,128)(2,1)S(1)} %get-tuple-element.32), channel_id=1, source_target_pairs={{0,0},{1,29},{2,2},{3,31},{4,4},{5,1},{6,6},{7,3},{8,8},{9,5},{10,... | collective-permute-start | bytes 313352 | tf_op jit(solution)/shard_map/ppermute | solution.py:69
  10.7 0.1 collective-permute-done.1.refs_0_
  10.8 4.1 %collective-permute-done.2.refs_1_ = bf16[136,384]{1,0:T(8,128)(2,1)S(1)} collective-permute-done((bf16[136,384]{1,0:T(8,128)(2,1)S(1)}, bf16[136,384]{1,0:T(8,128)(2,1)S(1)}, u32[]{:S(2)}, u32[]{:S(2)}) %collective-permute-start.2) | collective-permute-done | bytes 104480 | tf_op jit(solution)/shard_map/ppermute | solution.py:69
  14.9 0.0 collective-permute-done.3.refs_2_
  14.9 0.0 collective-permute-done.4.refs_3_
  14.9 1.9 %collective-permute-start.5 = (bf16[4,104,384]{2,1,0:T(8,128)(2,1)S(1)}, bf16[4,104,384]{2,1,0:T(8,128)(2,1)S(1)}, u32[]{:S(2)}, u32[]{:S(2)}) collective-permute-start(bf16[4,104,384]{2,1,0:T(8,128)(2,1)S(1)} %get-tuple-element.33), channel_id=1, source_target_pairs={{0,1},{1,0},{2,3},{3,2},{4,5},{5,4},{6,7},{7,6},{8,9},{9,8},{10,11... | collective-permute-start | bytes 958472 | tf_op jit(solution)/shard_map/ppermute | solution.py:413
  16.8 1.5 %collective-permute-start.6 = (f32[8,128]{1,0:T(8,128)S(1)}, f32[8,128]{1,0:T(8,128)S(1)}, u32[]{:S(2)}, u32[]{:S(2)}) collective-permute-start(f32[8,128]{1,0:T(8,128)S(1)} %get-tuple-element.38), channel_id=1, source_target_pairs={{0,2},{1,3},{2,0},{3,1},{4,6},{5,7},{6,4},{7,5},{8,10},{9,11},{10,... | collective-permute-start | bytes 12296 | tf_op jit(solution)/shard_map/ppermute | solution.py:413
  18.3 0.0 collective-permute-done.5.refs_4_
  18.3 4.4 %gains.1 = (f32[40,128]{1,0:T(8,128)S(1)}, f32[40,128]{1,0:T(8,128)S(1)}, f32[40,128]{1,0:T(8,128)S(1)}, f32[40,128]{1,0:T(8,128)S(1)}) custom-call(bf16[136,384]{1,0:T(8,128)(2,1)S(1)} %collective-permute-done.1.refs_0_, bf16[136,384]{1,0:T(8,128)(2,1)S(1)} %collective-permute-done.2.refs_1_, bf16[136,384]{1,0:T(8,128)(2,1)S(1)} %collective-permute-done.3.refs_2_, ...), custom_call_target="tpu_custom_call" | custom-call | flops 3422552064 | bytes 1671168 | tf_op jit(solution)/shard_map/gains/pallas_call | solution.py:484
  22.7 0.0 collective-permute-done.6
  22.7 2.1 %collective-permute-start.7 = (f32[40,128]{1,0:T(8,128)S(1)}, f32[40,128]{1,0:T(8,128)S(1)}, u32[]{:S(2)}, u32[]{:S(2)}) collective-permute-start(f32[40,128]{1,0:T(8,128)S(1)} %get-tuple-element.40), channel_id=1, source_target_pairs={{0,4},{4,8},{8,12},{12,0},{16,20},{20,24},{24,28},{28,16},{1,5},{5... | collective-permute-start | bytes 61448 | tf_op jit(solution)/shard_map/ppermute | solution.py:56
  24.8 1.9 %collective-permute-start.8 = (f32[40,128]{1,0:T(8,128)S(1)}, f32[40,128]{1,0:T(8,128)S(1)}, u32[]{:S(2)}, u32[]{:S(2)}) collective-permute-start(f32[40,128]{1,0:T(8,128)S(1)} %get-tuple-element.41), channel_id=1, source_target_pairs={{0,8},{4,12},{8,0},{12,4},{16,24},{20,28},{24,16},{28,20},{1,9},{5... | collective-permute-start | bytes 61448 | tf_op jit(solution)/shard_map/ppermute | solution.py:56
  26.7 1.8 %collective-permute-start.9 = (f32[40,128]{1,0:T(8,128)S(1)}, f32[40,128]{1,0:T(8,128)S(1)}, u32[]{:S(2)}, u32[]{:S(2)}) collective-permute-start(f32[40,128]{1,0:T(8,128)S(1)} %get-tuple-element.42), channel_id=1, source_target_pairs={{0,12},{4,0},{8,4},{12,8},{16,28},{20,16},{24,20},{28,24},{1,13},{... | collective-permute-start | bytes 61448 | tf_op jit(solution)/shard_map/ppermute | solution.py:56
  28.5 0.0 collective-permute-start.10
  28.5 1.2 %collective-permute-done.10.refs_5_ = f32[8,128]{1,0:T(8,128)S(1)} collective-permute-done((f32[8,128]{1,0:T(8,128)S(1)}, f32[8,128]{1,0:T(8,128)S(1)}, u32[]{:S(2)}, u32[]{:S(2)}) %collective-permute-start.10) | collective-permute-done | bytes 4128 | tf_op jit(solution)/shard_map/ppermute | solution.py:413
  29.7 0.0 collective-permute-done.7.refs_1_
  29.7 0.0 collective-permute-done.8.refs_2_
  29.7 0.8 %collective-permute-done.9.refs_3_ = f32[40,128]{1,0:T(8,128)S(1)} collective-permute-done((f32[40,128]{1,0:T(8,128)S(1)}, f32[40,128]{1,0:T(8,128)S(1)}, u32[]{:S(2)}, u32[]{:S(2)}) %collective-permute-start.9) | collective-permute-done | bytes 20512 | tf_op jit(solution)/shard_map/ppermute | solution.py:56
  30.5 0.7 %finish.1 = (f32[16,64]{1,0:T(8,128)}, f32[32,64]{1,0:T(8,128)}, f32[64,64]{1,0:T(8,128)}, f32[3,1,2,128]{3,2,1,0:T(2,128)}) custom-call(f32[40,128]{1,0:T(8,128)S(1)} %get-tuple-element.39.refs_0_, f32[40,128]{1,0:T(8,128)S(1)} %collective-permute-done.7.refs_1_, f32[40,128]{1,0:T(8,128)S(1)} %collective-permute-done.8.refs_2_, ...), custom_call_target="tpu_custom_call" | custom-call | tf_op jit(solution)/shard_map/finish/pallas_call | solution.py:515
  (2 shorter events, 0.0 us)
Async XLA Ops:
  0.6 1.8 %collective-permute-start = (s32[32,512]{1,0:T(8,128)}, s32[32,512]{1,0:T(8,128)S(1)}, u32[]{:S(2)}, u32[]{:S(2)}) collective-permute-start(s32[32,512]{1,0:T(8,128)} %refs_5_.1), channel_id=1, source_target_pairs={{0,1},{1,0},{2,3},{3,2},{4,5},{5,4},{6,7},{7,6},{8,9},{9,8},{10,11... | collective-permute-start | bytes 196616 | tf_op jit(solution)/shard_map/ppermute | solution.py:413
  3.3 7.5 %collective-permute-start.1 = (bf16[136,384]{1,0:T(8,128)(2,1)S(1)}, bf16[136,384]{1,0:T(8,128)(2,1)S(1)}, u32[]{:S(2)}, u32[]{:S(2)}) collective-permute-start(bf16[136,384]{1,0:T(8,128)(2,1)S(1)} %get-tuple-element.29), channel_id=1, source_target_pairs={{0,8},{1,5},{2,10},{3,7},{4,12},{5,9},{6,14},{7,11},{8,16},{9,13},... | collective-permute-start | bytes 313352 | tf_op jit(solution)/shard_map/ppermute | solution.py:69
  6.1 8.8 %collective-permute-start.2 = (bf16[136,384]{1,0:T(8,128)(2,1)S(1)}, bf16[136,384]{1,0:T(8,128)(2,1)S(1)}, u32[]{:S(2)}, u32[]{:S(2)}) collective-permute-start(bf16[136,384]{1,0:T(8,128)(2,1)S(1)} %get-tuple-element.30), channel_id=1, source_target_pairs={{0,16},{1,13},{2,18},{3,15},{4,20},{5,17},{6,22},{7,19},{8,24},{9,... | collective-permute-start | bytes 313352 | tf_op jit(solution)/shard_map/ppermute | solution.py:69
  8.7 6.2 %collective-permute-start.3 = (bf16[136,384]{1,0:T(8,128)(2,1)S(1)}, bf16[136,384]{1,0:T(8,128)(2,1)S(1)}, u32[]{:S(2)}, u32[]{:S(2)}) collective-permute-start(bf16[136,384]{1,0:T(8,128)(2,1)S(1)} %get-tuple-element.31), channel_id=1, source_target_pairs={{0,24},{1,21},{2,26},{3,23},{4,28},{5,25},{6,30},{7,27},{8,0},{9,2... | collective-permute-start | bytes 313352 | tf_op jit(solution)/shard_map/ppermute | solution.py:69
  10.0 4.9 %collective-permute-start.4 = (bf16[136,384]{1,0:T(8,128)(2,1)S(1)}, bf16[136,384]{1,0:T(8,128)(2,1)S(1)}, u32[]{:S(2)}, u32[]{:S(2)}) collective-permute-start(bf16[136,384]{1,0:T(8,128)(2,1)S(1)} %get-tuple-element.32), channel_id=1, source_target_pairs={{0,0},{1,29},{2,2},{3,31},{4,4},{5,1},{6,6},{7,3},{8,8},{9,5},{10,... | collective-permute-start | bytes 313352 | tf_op jit(solution)/shard_map/ppermute | solution.py:69
  14.9 3.4 %collective-permute-start.5 = (bf16[4,104,384]{2,1,0:T(8,128)(2,1)S(1)}, bf16[4,104,384]{2,1,0:T(8,128)(2,1)S(1)}, u32[]{:S(2)}, u32[]{:S(2)}) collective-permute-start(bf16[4,104,384]{2,1,0:T(8,128)(2,1)S(1)} %get-tuple-element.33), channel_id=1, source_target_pairs={{0,1},{1,0},{2,3},{3,2},{4,5},{5,4},{6,7},{7,6},{8,9},{9,8},{10,11... | collective-permute-start | bytes 958472 | tf_op jit(solution)/shard_map/ppermute | solution.py:413
  16.8 5.9 %collective-permute-start.6 = (f32[8,128]{1,0:T(8,128)S(1)}, f32[8,128]{1,0:T(8,128)S(1)}, u32[]{:S(2)}, u32[]{:S(2)}) collective-permute-start(f32[8,128]{1,0:T(8,128)S(1)} %get-tuple-element.38), channel_id=1, source_target_pairs={{0,2},{1,3},{2,0},{3,1},{4,6},{5,7},{6,4},{7,5},{8,10},{9,11},{10,... | collective-permute-start | bytes 12296 | tf_op jit(solution)/shard_map/ppermute | solution.py:413
  22.7 7.0 %collective-permute-start.7 = (f32[40,128]{1,0:T(8,128)S(1)}, f32[40,128]{1,0:T(8,128)S(1)}, u32[]{:S(2)}, u32[]{:S(2)}) collective-permute-start(f32[40,128]{1,0:T(8,128)S(1)} %get-tuple-element.40), channel_id=1, source_target_pairs={{0,4},{4,8},{8,12},{12,0},{16,20},{20,24},{24,28},{28,16},{1,5},{5... | collective-permute-start | bytes 61448 | tf_op jit(solution)/shard_map/ppermute | solution.py:56
  24.8 4.9 %collective-permute-start.8 = (f32[40,128]{1,0:T(8,128)S(1)}, f32[40,128]{1,0:T(8,128)S(1)}, u32[]{:S(2)}, u32[]{:S(2)}) collective-permute-start(f32[40,128]{1,0:T(8,128)S(1)} %get-tuple-element.41), channel_id=1, source_target_pairs={{0,8},{4,12},{8,0},{12,4},{16,24},{20,28},{24,16},{28,20},{1,9},{5... | collective-permute-start | bytes 61448 | tf_op jit(solution)/shard_map/ppermute | solution.py:56
  26.7 3.8 %collective-permute-start.9 = (f32[40,128]{1,0:T(8,128)S(1)}, f32[40,128]{1,0:T(8,128)S(1)}, u32[]{:S(2)}, u32[]{:S(2)}) collective-permute-start(f32[40,128]{1,0:T(8,128)S(1)} %get-tuple-element.42), channel_id=1, source_target_pairs={{0,12},{4,0},{8,4},{12,8},{16,28},{20,16},{24,20},{28,24},{1,13},{... | collective-permute-start | bytes 61448 | tf_op jit(solution)/shard_map/ppermute | solution.py:56
  28.5 1.2 %collective-permute-start.10 = (f32[8,128]{1,0:T(8,128)S(1)}, f32[8,128]{1,0:T(8,128)S(1)}, u32[]{:S(2)}, u32[]{:S(2)}) collective-permute-start(f32[8,128]{1,0:T(8,128)S(1)} %add.3.refs_4_), channel_id=1, source_target_pairs={{0,1},{1,0},{2,3},{3,2},{4,5},{5,4},{6,7},{7,6},{8,9},{9,8},{10,11... | collective-permute-start | bytes 12296 | tf_op jit(solution)/shard_map/ppermute | solution.py:413

commit v9 on v8

--- a/solution.py
+++ b/solution.py
@@ -64,7 +64,7 @@
         route = []
         for p in range(plan.devices * feat_axis):
             row, panel = divmod(p, feat_axis)
-            row = (row + 2 * slot + 2 - panel % 2) % plan.devices
+            row = (row + plan.offsets[panel % 2][slot]) % plan.devices
             route.append((p, row * feat_axis + panel))
         moved.append(lax.ppermute(block, ("rows", "feat"), route))
     return moved
@@ -86,6 +86,9 @@
         self.permuted = rows_axis <= PERMUTED and feat_axis % 2 == 0
         self.panels = 2 if self.permuted else 1
         self.parcels = rows_axis // 2 if self.permuted else 1
+        self.offsets = [
+            sorted(range(first, rows_axis, 2), key=lambda k: (abs(k - rows_axis // 2), k)) for first in range(2)
+        ]
         self.codes = self.panels * self.feats
         self.splits = 2 ** (self.levels + 1) - 2
         self.split_rows = round_up(self.splits, TILE)
@@ -234,7 +237,8 @@
     for slot in range(plan.parcels if plan.permuted else plan.devices):
         device = slot
         if plan.permuted:
-            device = rem(lax.axis_index("rows") + 2 * slot + 2 - parity, plan.devices)
+            offset = jnp.where(parity == 0, plan.offsets[0][slot], plan.offsets[1][slot])
+            device = rem(lax.axis_index("rows") + offset, plan.devices)
         half, place = div(device, plan.half), rem(device, plan.half)
         share, split = div(place, OUT_SPLIT), rem(place, OUT_SPLIT)
 

time: 31.4 us -> 30.5 us (0.971)
  waiting for transfers between devices: 6.23 us -> 5.51 us
    ppermute x4, waiting for transfers between devices: 4.24 us -> 3.03 us  [spread(): moved.append(lax.ppermute(block, ('rows', 'feat'), route))]
    ppermute x3, starting transfers between devices: 5.78 us -> 4.62 us  [exchanged(): moved.append(lax.ppermute(blocks[slot], 'rows', route))]
    ppermute x4, starting transfers between devices: 7.37 us -> 8.27 us  [spread(): moved.append(lax.ppermute(block, ('rows', 'feat'), route))]
    ppermute x3, waiting for transfers between devices: 0.82 us -> 1.31 us  [exchanged(): moved.append(lax.ppermute(blocks[slot], 'rows', route))]
  transfers between devices with their start and end apart: 11 -> 11, of which waited for: 4 -> 3; matrix products, arithmetic and copies ran while one was open for 0% -> 0% of each run, Pallas kernels for 18% -> 19%
where the time goes in v9:
time: 30.5 us; the launch traced here: 30.3 us
  starting transfers between devices  16.9 us (55%)
  Pallas kernels  7.24 us (24%)
  waiting for transfers between devices  5.51 us (18%)
  between operations  0.69 us (2%)
    ppermute x4, starting transfers between devices, spread(): moved.append(lax.ppermute(block, ('rows', 'feat'), route))  8.27 us
    ppermute x3, starting transfers between devices, exchanged(): moved.append(lax.ppermute(blocks[slot], 'rows', route))  4.62 us
    pallas_call x1, Pallas kernels, on_device(): pl.pallas_call(functools.partial(main_kernel, plan, chunk), out_shape=[ja...  4.36 us
    ppermute x4, starting transfers between devices, flipped(): return lax.ppermute(block, 'feat', [(p, p ^ bits) for p in range(count)])  3.97 us
    ppermute x4, waiting for transfers between devices, spread(): moved.append(lax.ppermute(block, ('rows', 'feat'), route))  3.03 us
    ppermute x3, waiting for transfers between devices, exchanged(): moved.append(lax.ppermute(blocks[slot], 'rows', route))  1.31 us
    pallas_call x1, Pallas kernels, on_device(): pl.pallas_call(functools.partial(fetch_kernel, plan), out_shape=(jax.Shap...  1.29 us
    ppermute x4, waiting for transfers between devices, flipped(): return lax.ppermute(block, 'feat', [(p, p ^ bits) for p in range(count)])  1.17 us
  transfers between devices with their start and end apart: 11, of which 3 were waited for; matrix products, arithmetic and copies ran while one was open for 0% of the time, Pallas kernels for 19%

profile of v9, /device:TPU:0, one launch (start us, length us, event | category | flops | bytes accessed | tf_op | source)
XLA Modules:
  0.0 30.3 jit_solution(6870473361898679574)
XLA Ops:
  0.6 0.5 %collective-permute-start = (s32[32,512]{1,0:T(8,128)}, s32[32,512]{1,0:T(8,128)S(1)}, u32[]{:S(2)}, u32[]{:S(2)}) collective-permute-start(s32[32,512]{1,0:T(8,128)} %refs_5_.1), channel_id=1, source_target_pairs={{0,1},{1,0},{2,3},{3,2},{4,5},{5,4},{6,7},{7,6},{8,9},{9,8},{10,11... | collective-permute-start | bytes 196616 | tf_op jit(solution)/shard_map/ppermute | solution.py:417
  1.2 1.3 %fetch.1 = (bf16[512,128]{1,0:T(8,128)(2,1)S(1)}, s32[32,512]{1,0:T(8,128)S(1)}, f32[8,512]{1,0:T(8,128)S(1)}, f32[3,16,128]{2,1,0:T(8,128)S(1)}, bf16[2,384,512]{2,1,0:T(8,128)(2,1)S(1)}) custom-call(bf16[512,128]{1,0:T(8,128)(2,1)} %refs_0_.1, bf16[512]{0:T(512)(128)(2,1)} %refs_1_.1, s32[3,512]{1,0:T(4,128)} %refs_2_.1, s32[14]{0:T(128)} %refs_3_.1, ...), custom_call_target="tpu_custom_call" | custom-call | flops 1000000000 | bytes 1000000 | tf_op jit(solution)/shard_map/fetch/pallas_call | solution.py:427
  2.4 0.0 collective-permute-done.refs_5_
  2.5 0.8 %prep.1 = (bf16[136,384]{1,0:T(8,128)(2,1)S(1)}, bf16[136,384]{1,0:T(8,128)(2,1)S(1)}, bf16[136,384]{1,0:T(8,128)(2,1)S(1)}, bf16[136,384]{1,0:T(8,128)(2,1)S(1)}) custom-call(bf16[512,128]{1,0:T(8,128)(2,1)S(1)} %get-tuple-element.24.refs_0_, f32[8,512]{1,0:T(8,128)S(1)} %get-tuple-element.25.refs_1_, f32[3,16,128]{2,1,0:T(8,128)S(1)} %get-tuple-element.26.refs_2_, ...), custom_call_target="tpu_custom_call" | custom-call | tf_op jit(solution)/shard_map/prep/pallas_call | solution.py:450
  3.3 3.8 %collective-permute-start.1 = (bf16[136,384]{1,0:T(8,128)(2,1)S(1)}, bf16[136,384]{1,0:T(8,128)(2,1)S(1)}, u32[]{:S(2)}, u32[]{:S(2)}) collective-permute-start(bf16[136,384]{1,0:T(8,128)(2,1)S(1)} %get-tuple-element.29), channel_id=1, source_target_pairs={{0,16},{1,13},{2,18},{3,15},{4,20},{5,17},{6,22},{7,19},{8,24},{9,... | collective-permute-start | bytes 313352 | tf_op jit(solution)/shard_map/ppermute | solution.py:69
  7.1 1.6 %collective-permute-start.2 = (bf16[136,384]{1,0:T(8,128)(2,1)S(1)}, bf16[136,384]{1,0:T(8,128)(2,1)S(1)}, u32[]{:S(2)}, u32[]{:S(2)}) collective-permute-start(bf16[136,384]{1,0:T(8,128)(2,1)S(1)} %get-tuple-element.30), channel_id=1, source_target_pairs={{0,8},{1,21},{2,10},{3,23},{4,12},{5,25},{6,14},{7,27},{8,16},{9,2... | collective-permute-start | bytes 313352 | tf_op jit(solution)/shard_map/ppermute | solution.py:69
  8.6 2.2 %collective-permute-start.3 = (bf16[136,384]{1,0:T(8,128)(2,1)S(1)}, bf16[136,384]{1,0:T(8,128)(2,1)S(1)}, u32[]{:S(2)}, u32[]{:S(2)}) collective-permute-start(bf16[136,384]{1,0:T(8,128)(2,1)S(1)} %get-tuple-element.31), channel_id=1, source_target_pairs={{0,24},{1,5},{2,26},{3,7},{4,28},{5,9},{6,30},{7,11},{8,0},{9,13},... | collective-permute-start | bytes 313352 | tf_op jit(solution)/shard_map/ppermute | solution.py:69
  10.9 0.7 %collective-permute-start.4 = (bf16[136,384]{1,0:T(8,128)(2,1)S(1)}, bf16[136,384]{1,0:T(8,128)(2,1)S(1)}, u32[]{:S(2)}, u32[]{:S(2)}) collective-permute-start(bf16[136,384]{1,0:T(8,128)(2,1)S(1)} %get-tuple-element.32), channel_id=1, source_target_pairs={{0,0},{1,29},{2,2},{3,31},{4,4},{5,1},{6,6},{7,3},{8,8},{9,5},{10,... | collective-permute-start | bytes 313352 | tf_op jit(solution)/shard_map/ppermute | solution.py:69
  11.6 0.0 collective-permute-done.1.refs_0_
  11.6 3.0 %collective-permute-done.2.refs_1_ = bf16[136,384]{1,0:T(8,128)(2,1)S(1)} collective-permute-done((bf16[136,384]{1,0:T(8,128)(2,1)S(1)}, bf16[136,384]{1,0:T(8,128)(2,1)S(1)}, u32[]{:S(2)}, u32[]{:S(2)}) %collective-permute-start.2) | collective-permute-done | bytes 104480 | tf_op jit(solution)/shard_map/ppermute | solution.py:69
  14.6 0.0 collective-permute-done.3.refs_2_
  14.6 0.0 collective-permute-done.4.refs_3_
  14.6 2.0 %collective-permute-start.5 = (bf16[4,104,384]{2,1,0:T(8,128)(2,1)S(1)}, bf16[4,104,384]{2,1,0:T(8,128)(2,1)S(1)}, u32[]{:S(2)}, u32[]{:S(2)}) collective-permute-start(bf16[4,104,384]{2,1,0:T(8,128)(2,1)S(1)} %get-tuple-element.33), channel_id=1, source_target_pairs={{0,1},{1,0},{2,3},{3,2},{4,5},{5,4},{6,7},{7,6},{8,9},{9,8},{10,11... | collective-permute-start | bytes 958472 | tf_op jit(solution)/shard_map/ppermute | solution.py:417
  16.6 1.5 %collective-permute-start.6 = (f32[8,128]{1,0:T(8,128)S(1)}, f32[8,128]{1,0:T(8,128)S(1)}, u32[]{:S(2)}, u32[]{:S(2)}) collective-permute-start(f32[8,128]{1,0:T(8,128)S(1)} %get-tuple-element.38), channel_id=1, source_target_pairs={{0,2},{1,3},{2,0},{3,1},{4,6},{5,7},{6,4},{7,5},{8,10},{9,11},{10,... | collective-permute-start | bytes 12296 | tf_op jit(solution)/shard_map/ppermute | solution.py:417
  18.1 0.0 collective-permute-done.5.refs_4_
  18.1 4.4 %gains.1 = (f32[40,128]{1,0:T(8,128)S(1)}, f32[40,128]{1,0:T(8,128)S(1)}, f32[40,128]{1,0:T(8,128)S(1)}, f32[40,128]{1,0:T(8,128)S(1)}) custom-call(bf16[136,384]{1,0:T(8,128)(2,1)S(1)} %collective-permute-done.1.refs_0_, bf16[136,384]{1,0:T(8,128)(2,1)S(1)} %collective-permute-done.2.refs_1_, bf16[136,384]{1,0:T(8,128)(2,1)S(1)} %collective-permute-done.3.refs_2_, ...), custom_call_target="tpu_custom_call" | custom-call | flops 3422552064 | bytes 1671168 | tf_op jit(solution)/shard_map/gains/pallas_call | solution.py:488
  22.5 0.0 collective-permute-done.6
  22.5 1.8 %collective-permute-start.7 = (f32[40,128]{1,0:T(8,128)S(1)}, f32[40,128]{1,0:T(8,128)S(1)}, u32[]{:S(2)}, u32[]{:S(2)}) collective-permute-start(f32[40,128]{1,0:T(8,128)S(1)} %get-tuple-element.40), channel_id=1, source_target_pairs={{0,4},{4,8},{8,12},{12,0},{16,20},{20,24},{24,28},{28,16},{1,5},{5... | collective-permute-start | bytes 61448 | tf_op jit(solution)/shard_map/ppermute | solution.py:56
  24.3 1.5 %collective-permute-start.8 = (f32[40,128]{1,0:T(8,128)S(1)}, f32[40,128]{1,0:T(8,128)S(1)}, u32[]{:S(2)}, u32[]{:S(2)}) collective-permute-start(f32[40,128]{1,0:T(8,128)S(1)} %get-tuple-element.41), channel_id=1, source_target_pairs={{0,8},{4,12},{8,0},{12,4},{16,24},{20,28},{24,16},{28,20},{1,9},{5... | collective-permute-start | bytes 61448 | tf_op jit(solution)/shard_map/ppermute | solution.py:56
  25.8 1.3 %collective-permute-start.9 = (f32[40,128]{1,0:T(8,128)S(1)}, f32[40,128]{1,0:T(8,128)S(1)}, u32[]{:S(2)}, u32[]{:S(2)}) collective-permute-start(f32[40,128]{1,0:T(8,128)S(1)} %get-tuple-element.42), channel_id=1, source_target_pairs={{0,12},{4,0},{8,4},{12,8},{16,28},{20,16},{24,20},{28,24},{1,13},{... | collective-permute-start | bytes 61448 | tf_op jit(solution)/shard_map/ppermute | solution.py:56
  27.1 0.0 collective-permute-start.10
  27.1 1.2 %collective-permute-done.10.refs_5_ = f32[8,128]{1,0:T(8,128)S(1)} collective-permute-done((f32[8,128]{1,0:T(8,128)S(1)}, f32[8,128]{1,0:T(8,128)S(1)}, u32[]{:S(2)}, u32[]{:S(2)}) %collective-permute-start.10) | collective-permute-done | bytes 4128 | tf_op jit(solution)/shard_map/ppermute | solution.py:417
  28.3 0.0 collective-permute-done.7.refs_1_
  28.3 0.0 collective-permute-done.8.refs_2_
  28.3 1.3 %collective-permute-done.9.refs_3_ = f32[40,128]{1,0:T(8,128)S(1)} collective-permute-done((f32[40,128]{1,0:T(8,128)S(1)}, f32[40,128]{1,0:T(8,128)S(1)}, u32[]{:S(2)}, u32[]{:S(2)}) %collective-permute-start.9) | collective-permute-done | bytes 20512 | tf_op jit(solution)/shard_map/ppermute | solution.py:56
  29.6 0.7 %finish.1 = (f32[16,64]{1,0:T(8,128)}, f32[32,64]{1,0:T(8,128)}, f32[64,64]{1,0:T(8,128)}, f32[3,1,2,128]{3,2,1,0:T(2,128)}) custom-call(f32[40,128]{1,0:T(8,128)S(1)} %get-tuple-element.39.refs_0_, f32[40,128]{1,0:T(8,128)S(1)} %collective-permute-done.7.refs_1_, f32[40,128]{1,0:T(8,128)S(1)} %collective-permute-done.8.refs_2_, ...), custom_call_target="tpu_custom_call" | custom-call | tf_op jit(solution)/shard_map/finish/pallas_call | solution.py:519
  (2 shorter events, 0.0 us)
Async XLA Ops:
  0.6 1.8 %collective-permute-start = (s32[32,512]{1,0:T(8,128)}, s32[32,512]{1,0:T(8,128)S(1)}, u32[]{:S(2)}, u32[]{:S(2)}) collective-permute-start(s32[32,512]{1,0:T(8,128)} %refs_5_.1), channel_id=1, source_target_pairs={{0,1},{1,0},{2,3},{3,2},{4,5},{5,4},{6,7},{7,6},{8,9},{9,8},{10,11... | collective-permute-start | bytes 196616 | tf_op jit(solution)/shard_map/ppermute | solution.py:417
  3.3 8.3 %collective-permute-start.1 = (bf16[136,384]{1,0:T(8,128)(2,1)S(1)}, bf16[136,384]{1,0:T(8,128)(2,1)S(1)}, u32[]{:S(2)}, u32[]{:S(2)}) collective-permute-start(bf16[136,384]{1,0:T(8,128)(2,1)S(1)} %get-tuple-element.29), channel_id=1, source_target_pairs={{0,16},{1,13},{2,18},{3,15},{4,20},{5,17},{6,22},{7,19},{8,24},{9,... | collective-permute-start | bytes 313352 | tf_op jit(solution)/shard_map/ppermute | solution.py:69
  7.1 7.5 %collective-permute-start.2 = (bf16[136,384]{1,0:T(8,128)(2,1)S(1)}, bf16[136,384]{1,0:T(8,128)(2,1)S(1)}, u32[]{:S(2)}, u32[]{:S(2)}) collective-permute-start(bf16[136,384]{1,0:T(8,128)(2,1)S(1)} %get-tuple-element.30), channel_id=1, source_target_pairs={{0,8},{1,21},{2,10},{3,23},{4,12},{5,25},{6,14},{7,27},{8,16},{9,2... | collective-permute-start | bytes 313352 | tf_op jit(solution)/shard_map/ppermute | solution.py:69
  8.6 5.9 %collective-permute-start.3 = (bf16[136,384]{1,0:T(8,128)(2,1)S(1)}, bf16[136,384]{1,0:T(8,128)(2,1)S(1)}, u32[]{:S(2)}, u32[]{:S(2)}) collective-permute-start(bf16[136,384]{1,0:T(8,128)(2,1)S(1)} %get-tuple-element.31), channel_id=1, source_target_pairs={{0,24},{1,5},{2,26},{3,7},{4,28},{5,9},{6,30},{7,11},{8,0},{9,13},... | collective-permute-start | bytes 313352 | tf_op jit(solution)/shard_map/ppermute | solution.py:69
  10.9 3.7 %collective-permute-start.4 = (bf16[136,384]{1,0:T(8,128)(2,1)S(1)}, bf16[136,384]{1,0:T(8,128)(2,1)S(1)}, u32[]{:S(2)}, u32[]{:S(2)}) collective-permute-start(bf16[136,384]{1,0:T(8,128)(2,1)S(1)} %get-tuple-element.32), channel_id=1, source_target_pairs={{0,0},{1,29},{2,2},{3,31},{4,4},{5,1},{6,6},{7,3},{8,8},{9,5},{10,... | collective-permute-start | bytes 313352 | tf_op jit(solution)/shard_map/ppermute | solution.py:69
  14.6 3.5 %collective-permute-start.5 = (bf16[4,104,384]{2,1,0:T(8,128)(2,1)S(1)}, bf16[4,104,384]{2,1,0:T(8,128)(2,1)S(1)}, u32[]{:S(2)}, u32[]{:S(2)}) collective-permute-start(bf16[4,104,384]{2,1,0:T(8,128)(2,1)S(1)} %get-tuple-element.33), channel_id=1, source_target_pairs={{0,1},{1,0},{2,3},{3,2},{4,5},{5,4},{6,7},{7,6},{8,9},{9,8},{10,11... | collective-permute-start | bytes 958472 | tf_op jit(solution)/shard_map/ppermute | solution.py:417
  16.6 5.9 %collective-permute-start.6 = (f32[8,128]{1,0:T(8,128)S(1)}, f32[8,128]{1,0:T(8,128)S(1)}, u32[]{:S(2)}, u32[]{:S(2)}) collective-permute-start(f32[8,128]{1,0:T(8,128)S(1)} %get-tuple-element.38), channel_id=1, source_target_pairs={{0,2},{1,3},{2,0},{3,1},{4,6},{5,7},{6,4},{7,5},{8,10},{9,11},{10,... | collective-permute-start | bytes 12296 | tf_op jit(solution)/shard_map/ppermute | solution.py:417
  22.5 5.8 %collective-permute-start.7 = (f32[40,128]{1,0:T(8,128)S(1)}, f32[40,128]{1,0:T(8,128)S(1)}, u32[]{:S(2)}, u32[]{:S(2)}) collective-permute-start(f32[40,128]{1,0:T(8,128)S(1)} %get-tuple-element.40), channel_id=1, source_target_pairs={{0,4},{4,8},{8,12},{12,0},{16,20},{20,24},{24,28},{28,16},{1,5},{5... | collective-permute-start | bytes 61448 | tf_op jit(solution)/shard_map/ppermute | solution.py:56
  24.3 4.0 %collective-permute-start.8 = (f32[40,128]{1,0:T(8,128)S(1)}, f32[40,128]{1,0:T(8,128)S(1)}, u32[]{:S(2)}, u32[]{:S(2)}) collective-permute-start(f32[40,128]{1,0:T(8,128)S(1)} %get-tuple-element.41), channel_id=1, source_target_pairs={{0,8},{4,12},{8,0},{12,4},{16,24},{20,28},{24,16},{28,20},{1,9},{5... | collective-permute-start | bytes 61448 | tf_op jit(solution)/shard_map/ppermute | solution.py:56
  25.8 3.8 %collective-permute-start.9 = (f32[40,128]{1,0:T(8,128)S(1)}, f32[40,128]{1,0:T(8,128)S(1)}, u32[]{:S(2)}, u32[]{:S(2)}) collective-permute-start(f32[40,128]{1,0:T(8,128)S(1)} %get-tuple-element.42), channel_id=1, source_target_pairs={{0,12},{4,0},{8,4},{12,8},{16,28},{20,16},{24,20},{28,24},{1,13},{... | collective-permute-start | bytes 61448 | tf_op jit(solution)/shard_map/ppermute | solution.py:56
  27.1 1.2 %collective-permute-start.10 = (f32[8,128]{1,0:T(8,128)S(1)}, f32[8,128]{1,0:T(8,128)S(1)}, u32[]{:S(2)}, u32[]{:S(2)}) collective-permute-start(f32[8,128]{1,0:T(8,128)S(1)} %add.3.refs_4_), channel_id=1, source_target_pairs={{0,1},{1,0},{2,3},{3,2},{4,5},{5,4},{6,7},{7,6},{8,9},{9,8},{10,11... | collective-permute-start | bytes 12296 | tf_op jit(solution)/shard_map/ppermute | solution.py:417

commit v10 on v9

--- a/solution.py
+++ b/solution.py
@@ -119,9 +119,15 @@
         return feature // 2 + (feature % 2) * (self.share // 2)
 
 
+def split_words(words):
+    codes = (jnp.bitwise_and(words, 63), jnp.bitwise_and(jnp.right_shift(words, 6), 63))
+    return jnp.concatenate(codes, axis=0).astype(f32).astype(bf16)
+
+
 def fetch_kernel(plan, *refs):
     inputs, refs = refs[:6], refs[6:]
-    (grad_ref, word_ref, row_ref, pick_ref, chosen_ref), (hess_ref, child_ref, feature_ref, bin_ref, sems) = refs[:5], refs[5:]
+    (grad_ref, word_ref, row_ref, pick_ref, chosen_ref, packed_ref), refs = refs[:6], refs[6:]
+    hess_ref, child_ref, feature_ref, bin_ref, table, sems = refs
     targets = (grad_ref, hess_ref, child_ref, feature_ref, bin_ref, word_ref)
     copies = [
         pltpu.make_async_copy(source, into, sems.at[i])
@@ -152,6 +158,20 @@
     for half in range(2):
         chosen_ref[half] = jnp.where(slot_ids == slot[half : half + 1], 1.0, 0.0).astype(bf16)
 
+    turn = jnp.where(
+        lax.broadcasted_iota(jnp.int32, (plan.outs, plan.outs), 0)
+        == lax.broadcasted_iota(jnp.int32, (plan.outs, plan.outs), 1),
+        1.0,
+        0.0,
+    ).astype(bf16)
+    own_at = plan.outs + plan.feats
+    table[: plan.outs] = lax.dot_general(turn, grad_ref[...], NT, preferred_element_type=f32).astype(bf16)
+    table[plan.outs : own_at] = split_words(word_ref[...])
+    leaf = jnp.bitwise_and(nodes[-1], plan.leaves - 1).astype(f32)
+    table[own_at:] = jnp.where(at == 0, row_ref[0:1, :], jnp.where(at == 1, leaf, 0.0)).astype(bf16)
+    for half in range(2):
+        packed_ref[half] = lax.dot_general(table[...], chosen_ref[half], NT, preferred_element_type=f32)
+
     panel = lax.axis_index("feat")
     lane = lax.broadcasted_iota(jnp.int32, (1, plan.codes), 1)
     pick_ref[...] = jnp.zeros_like(pick_ref)
@@ -160,7 +180,7 @@
         owner = lax.div(feature, jnp.int32(plan.feats))
         inner = feature - owner * plan.feats
         held = jnp.bitwise_xor(owner, panel)
-        place = held * plan.words + inner // 2 + lax.rem(inner, 2) * (plan.panels * plan.words)
+        place = held * plan.feats + inner // 2 + lax.rem(inner, 2) * plan.words
         place = jnp.where(held < plan.panels, place, plan.codes)
         pick_ref[0, slot : slot + 1, :] = jnp.where(lane == place, 1.0, 0.0)
         pick_ref[1, slot : slot + 1, :] = jnp.full((1, plan.codes), bin_ref[slot].astype(f32))
@@ -168,38 +188,22 @@
 
 
 def prep_kernel(plan, *refs):
-    (grad_ref, row_ref, pick_ref, chosen_ref), refs = refs[:4], refs[4:]
+    (grad_ref, row_ref, pick_ref, chosen_ref, own_ref), refs = refs[:5], refs[5:]
     word_refs, send_refs = refs[: plan.panels], refs[plan.panels : plan.panels + plan.parcels]
     table, packed, lines, marked = refs[plan.panels + plan.parcels :]
-    rows = plan.row_dev
-    low_at, high_at = plan.outs, plan.outs + plan.panels * plan.words
-    own_at = plan.outs + plan.codes
+    own_at = plan.outs + plan.feats
     grads = grad_ref[...]
     hess = row_ref[0:1, :]
     nodes = [row_ref[level + 1 : level + 2, :] for level in range(plan.levels)]
 
-    turn = jnp.where(
-        lax.broadcasted_iota(jnp.int32, (plan.outs, plan.outs), 0)
-        == lax.broadcasted_iota(jnp.int32, (plan.outs, plan.outs), 1),
-        1.0,
-        0.0,
-    ).astype(bf16)
-    table[0:low_at] = lax.dot_general(turn, grads, NT, preferred_element_type=f32).astype(bf16)
     for which, word_ref in enumerate(word_refs):
-        words = word_ref[...]
-        low = jnp.bitwise_and(words, 63)
-        high = jnp.bitwise_and(jnp.right_shift(words, 6), 63)
-        for first, codes in ((low_at, low), (high_at, high)):
-            at = first + which * plan.words
-            table[at : at + plan.words] = codes.astype(f32).astype(bf16)
-    at = lax.broadcasted_iota(jnp.int32, (TILE, rows), 0)
-    leaf = nodes[-1] - nodes[0] * plan.leaves
-    table[own_at:] = jnp.where(at == 0, hess, jnp.where(at == 1, leaf, 0.0)).astype(bf16)
-    for half in range(2):
-        packed[half] = lax.dot_general(table[...], chosen_ref[half], NT, preferred_element_type=f32)
+        table[which * plan.feats : (which + 1) * plan.feats] = split_words(word_ref[...])
+    if plan.panels > 1:
+        for half in range(2):
+            packed[half] = lax.dot_general(table[plan.feats :], chosen_ref[half], NT, preferred_element_type=f32)
 
     ends = [(level, node) for level in range(plan.levels) for node in range(2 ** (level + 1))]
-    code = jnp.dot(pick_ref[0].astype(bf16), table[low_at:own_at], preferred_element_type=f32)
+    code = jnp.dot(pick_ref[0].astype(bf16), table[...], preferred_element_type=f32)
     marked[...] = jnp.zeros_like(marked)
     for slot, (level, node) in enumerate(ends):
         here = jnp.where(nodes[level] == node, pick_ref[2, slot : slot + 1, 0:1], 0.0)
@@ -242,18 +246,18 @@
         half, place = div(device, plan.half), rem(device, plan.half)
         share, split = div(place, OUT_SPLIT), rem(place, OUT_SPLIT)
 
-        def codes(which):
-            at = [first + which * plan.words + share * word_share for first in (low_at, high_at)]
-            return [packed[half, pl.ds(aligned(first, word_share), word_share), :] for first in at]
+        def codes(ref, first):
+            at = [first + odd * plan.words + share * word_share for odd in range(2)]
+            return [ref[half, pl.ds(aligned(k, word_share), word_share), :] for k in at]
 
         message = [
-            *codes(0),
-            packed[half, pl.ds(aligned(split * plan.outs_dev, plan.outs_dev), plan.outs_dev), :],
-            packed[half, own_at : own_at + 2, :],
+            *codes(own_ref, plan.outs),
+            own_ref[half, pl.ds(aligned(split * plan.outs_dev, plan.outs_dev), plan.outs_dev), :],
+            own_ref[half, own_at : own_at + 2, :],
             lines[div(device, plan.devices // (2 * plan.leaves))],
         ]
         if plan.permuted:
-            send_refs[slot][...] = jnp.concatenate(message + codes(1), axis=0).astype(bf16)
+            send_refs[slot][...] = jnp.concatenate(message + codes(packed, 0), axis=0).astype(bf16)
         else:
             send_refs[0][slot] = jnp.concatenate(message, axis=0).astype(bf16)
 
@@ -423,8 +427,8 @@
 
     inputs = (gradients, hessians, children, split_feature, split_bin, bin_words)
     crossed = [flipped(bin_words, 1)] if plan.permuted else []
-    row_dev, table_rows = plan.row_dev, plan.outs + plan.codes + TILE
-    grads, words, row_values, picks, chosen = pl.pallas_call(
+    row_dev, table_rows = plan.row_dev, plan.outs + plan.feats + TILE
+    grads, words, row_values, picks, chosen, own_part = pl.pallas_call(
         functools.partial(fetch_kernel, plan),
         out_shape=(
             jax.ShapeDtypeStruct(gradients.shape, bf16),
@@ -432,14 +436,16 @@
             jax.ShapeDtypeStruct((8, row_dev), f32),
             jax.ShapeDtypeStruct((3, plan.split_rows, plan.codes), f32),
             jax.ShapeDtypeStruct((2, plan.slots, row_dev), bf16),
+            jax.ShapeDtypeStruct((2, table_rows, plan.slots), f32),
         ),
         in_specs=[pl.BlockSpec(memory_space=pltpu.HBM)] * len(inputs),
-        out_specs=[whole()] * 5,
+        out_specs=[whole()] * 6,
         scratch_shapes=[
             pltpu.VMEM(hessians.shape, bf16),
             pltpu.VMEM(children.shape, jnp.int32),
             pltpu.SMEM(split_feature.shape, jnp.int32),
             pltpu.SMEM(split_bin.shape, jnp.int32),
+            pltpu.VMEM((table_rows, row_dev), bf16),
             pltpu.SemaphoreType.DMA((len(inputs),)),
         ],
         cost_estimate=pl.CostEstimate(flops=10**9, bytes_accessed=10**6, transcendentals=0),
@@ -450,17 +456,17 @@
     parcels = pl.pallas_call(
         functools.partial(prep_kernel, plan),
         out_shape=[jax.ShapeDtypeStruct(parcel, bf16)] * plan.parcels,
-        in_specs=[whole()] * (4 + plan.panels),
+        in_specs=[whole()] * (5 + plan.panels),
         out_specs=[whole()] * plan.parcels,
         scratch_shapes=[
-            pltpu.VMEM((table_rows, row_dev), bf16),
-            pltpu.VMEM((2, table_rows, plan.slots), f32),
+            pltpu.VMEM((plan.codes, row_dev), bf16),
+            pltpu.VMEM((2, plan.feats, plan.slots), f32),
             pltpu.VMEM((2 * plan.leaves, plan.base_rows - plan.misc_at - 2, plan.slots), f32),
             pltpu.VMEM((2 * plan.split_rows, row_dev), f32),
         ],
         compiler_params=params,
         name="prep",
-    )(grads, row_values, picks, chosen, words, *crossed)
+    )(grads, row_values, picks, chosen, own_part, words, *crossed)
 
     if plan.permuted:
         got = spread(parcels, plan)

time: 30.5 us -> 30.4 us (level)
  transfers between devices with their start and end apart: 11 -> 11, of which waited for: 3 -> 4; matrix products, arithmetic and copies ran while one was open for 0% -> 0% of each run, Pallas kernels for 19% -> 20%
where the time goes in v10:
time: 30.4 us; the launch traced here: 30.2 us
  starting transfers between devices  16.8 us (55%)
  Pallas kernels  7.31 us (24%)
  waiting for transfers between devices  5.42 us (18%)
  between operations  0.69 us (2%)
    ppermute x4, starting transfers between devices, spread(): moved.append(lax.ppermute(block, ('rows', 'feat'), route))  8.13 us
    ppermute x3, starting transfers between devices, exchanged(): moved.append(lax.ppermute(blocks[slot], 'rows', route))  4.52 us
    pallas_call x1, Pallas kernels, on_device(): pl.pallas_call(functools.partial(main_kernel, plan, chunk), out_shape=[ja...  4.4 us
    ppermute x4, starting transfers between devices, flipped(): return lax.ppermute(block, 'feat', [(p, p ^ bits) for p in range(count)])  4.14 us
    ppermute x4, waiting for transfers between devices, spread(): moved.append(lax.ppermute(block, ('rows', 'feat'), route))  3.07 us
    pallas_call x1, Pallas kernels, on_device(): pl.pallas_call(functools.partial(fetch_kernel, plan), out_shape=(jax.Shap...  1.57 us
    ppermute x3, waiting for transfers between devices, exchanged(): moved.append(lax.ppermute(blocks[slot], 'rows', route))  1.18 us
    ppermute x4, waiting for transfers between devices, flipped(): return lax.ppermute(block, 'feat', [(p, p ^ bits) for p in range(count)])  1.17 us
  transfers between devices with their start and end apart: 11, of which 4 were waited for; matrix products, arithmetic and copies ran while one was open for 0% of the time, Pallas kernels for 20%

profile of v10, /device:TPU:0, one launch (start us, length us, event | category | flops | bytes accessed | tf_op | source)
XLA Modules:
  0.0 30.2 jit_solution(2642044859403247362)
XLA Ops:
  0.6 0.5 %collective-permute-start = (s32[32,512]{1,0:T(8,128)}, s32[32,512]{1,0:T(8,128)S(1)}, u32[]{:S(2)}, u32[]{:S(2)}) collective-permute-start(s32[32,512]{1,0:T(8,128)} %refs_5_.1), channel_id=1, source_target_pairs={{0,1},{1,0},{2,3},{3,2},{4,5},{5,4},{6,7},{7,6},{8,9},{9,8},{10,11... | collective-permute-start | bytes 196616 | tf_op jit(solution)/shard_map/ppermute | solution.py:421
  1.2 1.6 %fetch.1 = (bf16[512,128]{1,0:T(8,128)(2,1)S(1)}, s32[32,512]{1,0:T(8,128)S(1)}, f32[8,512]{1,0:T(8,128)S(1)}, f32[3,16,128]{2,1,0:T(8,128)S(1)}, bf16[2,384,512...) custom-call(bf16[512,128]{1,0:T(8,128)(2,1)} %refs_0_.1, bf16[512]{0:T(512)(128)(2,1)} %refs_1_.1, s32[3,512]{1,0:T(4,128)} %refs_2_.1, ...), custom_call_target="tpu_custom_call" | custom-call | flops 1000000000 | bytes 1000000 | tf_op jit(solution)/shard_map/fetch/pallas_call | solution.py:431
  2.7 0.0 collective-permute-done.refs_6_
  2.7 0.6 %prep.1 = (bf16[136,384]{1,0:T(8,128)(2,1)S(1)}, bf16[136,384]{1,0:T(8,128)(2,1)S(1)}, bf16[136,384]{1,0:T(8,128)(2,1)S(1)}, bf16[136,384]{1,0:T(8,128)(2,1)S(1)}) custom-call(bf16[512,128]{1,0:T(8,128)(2,1)S(1)} %get-tuple-element.25.refs_0_, f32[8,512]{1,0:T(8,128)S(1)} %get-tuple-element.26.refs_1_, f32[3,16,128]{2,1,0:T(8,128)S(1)} %get-tuple-element.27.refs_2_, ...), custom_call_target="tpu_custom_call" | custom-call | tf_op jit(solution)/shard_map/prep/pallas_call | solution.py:456
  3.3 3.7 %collective-permute-start.1 = (bf16[136,384]{1,0:T(8,128)(2,1)S(1)}, bf16[136,384]{1,0:T(8,128)(2,1)S(1)}, u32[]{:S(2)}, u32[]{:S(2)}) collective-permute-start(bf16[136,384]{1,0:T(8,128)(2,1)S(1)} %get-tuple-element.31), channel_id=1, source_target_pairs={{0,16},{1,13},{2,18},{3,15},{4,20},{5,17},{6,22},{7,19},{8,24},{9,... | collective-permute-start | bytes 313352 | tf_op jit(solution)/shard_map/ppermute | solution.py:69
  7.0 1.6 %collective-permute-start.2 = (bf16[136,384]{1,0:T(8,128)(2,1)S(1)}, bf16[136,384]{1,0:T(8,128)(2,1)S(1)}, u32[]{:S(2)}, u32[]{:S(2)}) collective-permute-start(bf16[136,384]{1,0:T(8,128)(2,1)S(1)} %get-tuple-element.32), channel_id=1, source_target_pairs={{0,8},{1,21},{2,10},{3,23},{4,12},{5,25},{6,14},{7,27},{8,16},{9,2... | collective-permute-start | bytes 313352 | tf_op jit(solution)/shard_map/ppermute | solution.py:69
  8.6 2.2 %collective-permute-start.3 = (bf16[136,384]{1,0:T(8,128)(2,1)S(1)}, bf16[136,384]{1,0:T(8,128)(2,1)S(1)}, u32[]{:S(2)}, u32[]{:S(2)}) collective-permute-start(bf16[136,384]{1,0:T(8,128)(2,1)S(1)} %get-tuple-element.33), channel_id=1, source_target_pairs={{0,24},{1,5},{2,26},{3,7},{4,28},{5,9},{6,30},{7,11},{8,0},{9,13},... | collective-permute-start | bytes 313352 | tf_op jit(solution)/shard_map/ppermute | solution.py:69
  10.8 0.7 %collective-permute-start.4 = (bf16[136,384]{1,0:T(8,128)(2,1)S(1)}, bf16[136,384]{1,0:T(8,128)(2,1)S(1)}, u32[]{:S(2)}, u32[]{:S(2)}) collective-permute-start(bf16[136,384]{1,0:T(8,128)(2,1)S(1)} %get-tuple-element.34), channel_id=1, source_target_pairs={{0,0},{1,29},{2,2},{3,31},{4,4},{5,1},{6,6},{7,3},{8,8},{9,5},{10,... | collective-permute-start | bytes 313352 | tf_op jit(solution)/shard_map/ppermute | solution.py:69
  11.5 0.0 collective-permute-done.1.refs_0_
  11.5 2.8 %collective-permute-done.2.refs_1_ = bf16[136,384]{1,0:T(8,128)(2,1)S(1)} collective-permute-done((bf16[136,384]{1,0:T(8,128)(2,1)S(1)}, bf16[136,384]{1,0:T(8,128)(2,1)S(1)}, u32[]{:S(2)}, u32[]{:S(2)}) %collective-permute-start.2) | collective-permute-done | bytes 104480 | tf_op jit(solution)/shard_map/ppermute | solution.py:69
  14.3 0.2 collective-permute-done.3.refs_2_
  14.5 0.0 collective-permute-done.4.refs_3_
  14.6 2.1 %collective-permute-start.5 = (bf16[4,104,384]{2,1,0:T(8,128)(2,1)S(1)}, bf16[4,104,384]{2,1,0:T(8,128)(2,1)S(1)}, u32[]{:S(2)}, u32[]{:S(2)}) collective-permute-start(bf16[4,104,384]{2,1,0:T(8,128)(2,1)S(1)} %get-tuple-element.35), channel_id=1, source_target_pairs={{0,1},{1,0},{2,3},{3,2},{4,5},{5,4},{6,7},{7,6},{8,9},{9,8},{10,11... | collective-permute-start | bytes 958472 | tf_op jit(solution)/shard_map/ppermute | solution.py:421
  16.7 1.5 %collective-permute-start.6 = (f32[8,128]{1,0:T(8,128)S(1)}, f32[8,128]{1,0:T(8,128)S(1)}, u32[]{:S(2)}, u32[]{:S(2)}) collective-permute-start(f32[8,128]{1,0:T(8,128)S(1)} %get-tuple-element.40), channel_id=1, source_target_pairs={{0,2},{1,3},{2,0},{3,1},{4,6},{5,7},{6,4},{7,5},{8,10},{9,11},{10,... | collective-permute-start | bytes 12296 | tf_op jit(solution)/shard_map/ppermute | solution.py:421
  18.2 0.0 collective-permute-done.5.refs_4_
  18.2 4.4 %gains.1 = (f32[40,128]{1,0:T(8,128)S(1)}, f32[40,128]{1,0:T(8,128)S(1)}, f32[40,128]{1,0:T(8,128)S(1)}, f32[40,128]{1,0:T(8,128)S(1)}) custom-call(bf16[136,384]{1,0:T(8,128)(2,1)S(1)} %collective-permute-done.1.refs_0_, bf16[136,384]{1,0:T(8,128)(2,1)S(1)} %collective-permute-done.2.refs_1_, bf16[136,384]{1,0:T(8,128)(2,1)S(1)} %collective-permute-done.3.refs_2_, ...), custom_call_target="tpu_custom_call" | custom-call | flops 3422552064 | bytes 1671168 | tf_op jit(solution)/shard_map/gains/pallas_call | solution.py:494
  22.6 0.0 collective-permute-done.6
  22.6 1.6 %collective-permute-start.7 = (f32[40,128]{1,0:T(8,128)S(1)}, f32[40,128]{1,0:T(8,128)S(1)}, u32[]{:S(2)}, u32[]{:S(2)}) collective-permute-start(f32[40,128]{1,0:T(8,128)S(1)} %get-tuple-element.42), channel_id=1, source_target_pairs={{0,4},{4,8},{8,12},{12,0},{16,20},{20,24},{24,28},{28,16},{1,5},{5... | collective-permute-start | bytes 61448 | tf_op jit(solution)/shard_map/ppermute | solution.py:56
  24.2 1.5 %collective-permute-start.8 = (f32[40,128]{1,0:T(8,128)S(1)}, f32[40,128]{1,0:T(8,128)S(1)}, u32[]{:S(2)}, u32[]{:S(2)}) collective-permute-start(f32[40,128]{1,0:T(8,128)S(1)} %get-tuple-element.43), channel_id=1, source_target_pairs={{0,8},{4,12},{8,0},{12,4},{16,24},{20,28},{24,16},{28,20},{1,9},{5... | collective-permute-start | bytes 61448 | tf_op jit(solution)/shard_map/ppermute | solution.py:56
  25.7 1.4 %collective-permute-start.9 = (f32[40,128]{1,0:T(8,128)S(1)}, f32[40,128]{1,0:T(8,128)S(1)}, u32[]{:S(2)}, u32[]{:S(2)}) collective-permute-start(f32[40,128]{1,0:T(8,128)S(1)} %get-tuple-element.44), channel_id=1, source_target_pairs={{0,12},{4,0},{8,4},{12,8},{16,28},{20,16},{24,20},{28,24},{1,13},{... | collective-permute-start | bytes 61448 | tf_op jit(solution)/shard_map/ppermute | solution.py:56
  27.1 0.0 collective-permute-start.10
  27.2 1.2 %collective-permute-done.10.refs_5_ = f32[8,128]{1,0:T(8,128)S(1)} collective-permute-done((f32[8,128]{1,0:T(8,128)S(1)}, f32[8,128]{1,0:T(8,128)S(1)}, u32[]{:S(2)}, u32[]{:S(2)}) %collective-permute-start.10) | collective-permute-done | bytes 4128 | tf_op jit(solution)/shard_map/ppermute | solution.py:421
  28.3 0.0 collective-permute-done.7.refs_1_
  28.3 0.0 collective-permute-done.8.refs_2_
  28.3 1.2 %collective-permute-done.9.refs_3_ = f32[40,128]{1,0:T(8,128)S(1)} collective-permute-done((f32[40,128]{1,0:T(8,128)S(1)}, f32[40,128]{1,0:T(8,128)S(1)}, u32[]{:S(2)}, u32[]{:S(2)}) %collective-permute-start.9) | collective-permute-done | bytes 20512 | tf_op jit(solution)/shard_map/ppermute | solution.py:56
  29.5 0.7 %finish.1 = (f32[16,64]{1,0:T(8,128)}, f32[32,64]{1,0:T(8,128)}, f32[64,64]{1,0:T(8,128)}, f32[3,1,2,128]{3,2,1,0:T(2,128)}) custom-call(f32[40,128]{1,0:T(8,128)S(1)} %get-tuple-element.41.refs_0_, f32[40,128]{1,0:T(8,128)S(1)} %collective-permute-done.7.refs_1_, f32[40,128]{1,0:T(8,128)S(1)} %collective-permute-done.8.refs_2_, ...), custom_call_target="tpu_custom_call" | custom-call | tf_op jit(solution)/shard_map/finish/pallas_call | solution.py:525
  (2 shorter events, 0.0 us)
Async XLA Ops:
  0.6 2.1 %collective-permute-start = (s32[32,512]{1,0:T(8,128)}, s32[32,512]{1,0:T(8,128)S(1)}, u32[]{:S(2)}, u32[]{:S(2)}) collective-permute-start(s32[32,512]{1,0:T(8,128)} %refs_5_.1), channel_id=1, source_target_pairs={{0,1},{1,0},{2,3},{3,2},{4,5},{5,4},{6,7},{7,6},{8,9},{9,8},{10,11... | collective-permute-start | bytes 196616 | tf_op jit(solution)/shard_map/ppermute | solution.py:421
  3.3 8.1 %collective-permute-start.1 = (bf16[136,384]{1,0:T(8,128)(2,1)S(1)}, bf16[136,384]{1,0:T(8,128)(2,1)S(1)}, u32[]{:S(2)}, u32[]{:S(2)}) collective-permute-start(bf16[136,384]{1,0:T(8,128)(2,1)S(1)} %get-tuple-element.31), channel_id=1, source_target_pairs={{0,16},{1,13},{2,18},{3,15},{4,20},{5,17},{6,22},{7,19},{8,24},{9,... | collective-permute-start | bytes 313352 | tf_op jit(solution)/shard_map/ppermute | solution.py:69
  7.0 7.3 %collective-permute-start.2 = (bf16[136,384]{1,0:T(8,128)(2,1)S(1)}, bf16[136,384]{1,0:T(8,128)(2,1)S(1)}, u32[]{:S(2)}, u32[]{:S(2)}) collective-permute-start(bf16[136,384]{1,0:T(8,128)(2,1)S(1)} %get-tuple-element.32), channel_id=1, source_target_pairs={{0,8},{1,21},{2,10},{3,23},{4,12},{5,25},{6,14},{7,27},{8,16},{9,2... | collective-permute-start | bytes 313352 | tf_op jit(solution)/shard_map/ppermute | solution.py:69
  8.6 6.0 %collective-permute-start.3 = (bf16[136,384]{1,0:T(8,128)(2,1)S(1)}, bf16[136,384]{1,0:T(8,128)(2,1)S(1)}, u32[]{:S(2)}, u32[]{:S(2)}) collective-permute-start(bf16[136,384]{1,0:T(8,128)(2,1)S(1)} %get-tuple-element.33), channel_id=1, source_target_pairs={{0,24},{1,5},{2,26},{3,7},{4,28},{5,9},{6,30},{7,11},{8,0},{9,13},... | collective-permute-start | bytes 313352 | tf_op jit(solution)/shard_map/ppermute | solution.py:69
  10.8 3.7 %collective-permute-start.4 = (bf16[136,384]{1,0:T(8,128)(2,1)S(1)}, bf16[136,384]{1,0:T(8,128)(2,1)S(1)}, u32[]{:S(2)}, u32[]{:S(2)}) collective-permute-start(bf16[136,384]{1,0:T(8,128)(2,1)S(1)} %get-tuple-element.34), channel_id=1, source_target_pairs={{0,0},{1,29},{2,2},{3,31},{4,4},{5,1},{6,6},{7,3},{8,8},{9,5},{10,... | collective-permute-start | bytes 313352 | tf_op jit(solution)/shard_map/ppermute | solution.py:69
  14.6 3.6 %collective-permute-start.5 = (bf16[4,104,384]{2,1,0:T(8,128)(2,1)S(1)}, bf16[4,104,384]{2,1,0:T(8,128)(2,1)S(1)}, u32[]{:S(2)}, u32[]{:S(2)}) collective-permute-start(bf16[4,104,384]{2,1,0:T(8,128)(2,1)S(1)} %get-tuple-element.35), channel_id=1, source_target_pairs={{0,1},{1,0},{2,3},{3,2},{4,5},{5,4},{6,7},{7,6},{8,9},{9,8},{10,11... | collective-permute-start | bytes 958472 | tf_op jit(solution)/shard_map/ppermute | solution.py:421
  16.7 5.9 %collective-permute-start.6 = (f32[8,128]{1,0:T(8,128)S(1)}, f32[8,128]{1,0:T(8,128)S(1)}, u32[]{:S(2)}, u32[]{:S(2)}) collective-permute-start(f32[8,128]{1,0:T(8,128)S(1)} %get-tuple-element.40), channel_id=1, source_target_pairs={{0,2},{1,3},{2,0},{3,1},{4,6},{5,7},{6,4},{7,5},{8,10},{9,11},{10,... | collective-permute-start | bytes 12296 | tf_op jit(solution)/shard_map/ppermute | solution.py:421
  22.6 5.7 %collective-permute-start.7 = (f32[40,128]{1,0:T(8,128)S(1)}, f32[40,128]{1,0:T(8,128)S(1)}, u32[]{:S(2)}, u32[]{:S(2)}) collective-permute-start(f32[40,128]{1,0:T(8,128)S(1)} %get-tuple-element.42), channel_id=1, source_target_pairs={{0,4},{4,8},{8,12},{12,0},{16,20},{20,24},{24,28},{28,16},{1,5},{5... | collective-permute-start | bytes 61448 | tf_op jit(solution)/shard_map/ppermute | solution.py:56
  24.2 4.1 %collective-permute-start.8 = (f32[40,128]{1,0:T(8,128)S(1)}, f32[40,128]{1,0:T(8,128)S(1)}, u32[]{:S(2)}, u32[]{:S(2)}) collective-permute-start(f32[40,128]{1,0:T(8,128)S(1)} %get-tuple-element.43), channel_id=1, source_target_pairs={{0,8},{4,12},{8,0},{12,4},{16,24},{20,28},{24,16},{28,20},{1,9},{5... | collective-permute-start | bytes 61448 | tf_op jit(solution)/shard_map/ppermute | solution.py:56
  25.7 3.8 %collective-permute-start.9 = (f32[40,128]{1,0:T(8,128)S(1)}, f32[40,128]{1,0:T(8,128)S(1)}, u32[]{:S(2)}, u32[]{:S(2)}) collective-permute-start(f32[40,128]{1,0:T(8,128)S(1)} %get-tuple-element.44), channel_id=1, source_target_pairs={{0,12},{4,0},{8,4},{12,8},{16,28},{20,16},{24,20},{28,24},{1,13},{... | collective-permute-start | bytes 61448 | tf_op jit(solution)/shard_map/ppermute | solution.py:56
  27.1 1.2 %collective-permute-start.10 = (f32[8,128]{1,0:T(8,128)S(1)}, f32[8,128]{1,0:T(8,128)S(1)}, u32[]{:S(2)}, u32[]{:S(2)}) collective-permute-start(f32[8,128]{1,0:T(8,128)S(1)} %add.3.refs_4_), channel_id=1, source_target_pairs={{0,1},{1,0},{2,3},{3,2},{4,5},{5,4},{6,7},{7,6},{8,9},{9,8},{10,11... | collective-permute-start | bytes 12296 | tf_op jit(solution)/shard_map/ppermute | solution.py:421

commit v11 on v9

--- a/solution.py
+++ b/solution.py
@@ -103,7 +103,7 @@
         self.returned = [self.feats // size for size in self.sizes]
         self.needed = [min(self.share, count) for count in self.returned]
         self.block = min(self.needed)
-        self.step = min(8, self.share)
+        self.step = min(16, self.share)
         self.tiles = [
             (start + k, start + k + self.block // 2)
             for start in range(0, self.share, self.block)

time: 30.5 us -> 30.5 us (level)
  no operation moved by 1% of the time
where the time goes in v11:
time: 30.5 us; the launch traced here: 30.3 us
  starting transfers between devices  16.9 us (55%)
  Pallas kernels  7.25 us (24%)
  waiting for transfers between devices  5.49 us (18%)
  between operations  0.69 us (2%)
    ppermute x4, starting transfers between devices, spread(): moved.append(lax.ppermute(block, ('rows', 'feat'), route))  8.27 us
    ppermute x3, starting transfers between devices, exchanged(): moved.append(lax.ppermute(blocks[slot], 'rows', route))  4.63 us
    pallas_call x1, Pallas kernels, on_device(): pl.pallas_call(functools.partial(main_kernel, plan, chunk), out_shape=[ja...  4.38 us
    ppermute x4, starting transfers between devices, flipped(): return lax.ppermute(block, 'feat', [(p, p ^ bits) for p in range(count)])  3.97 us
    ppermute x4, waiting for transfers between devices, spread(): moved.append(lax.ppermute(block, ('rows', 'feat'), route))  3.03 us
    pallas_call x1, Pallas kernels, on_device(): pl.pallas_call(functools.partial(fetch_kernel, plan), out_shape=(jax.Shap...  1.29 us
    ppermute x3, waiting for transfers between devices, exchanged(): moved.append(lax.ppermute(blocks[slot], 'rows', route))  1.29 us
    ppermute x4, waiting for transfers between devices, flipped(): return lax.ppermute(block, 'feat', [(p, p ^ bits) for p in range(count)])  1.17 us
  transfers between devices with their start and end apart: 11, of which 3 were waited for; matrix products, arithmetic and copies ran while one was open for 0% of the time, Pallas kernels for 19%

profile of v11, /device:TPU:0, one launch (start us, length us, event | category | flops | bytes accessed | tf_op | source)
XLA Modules:
  0.0 30.3 jit_solution(9504793774576389842)
XLA Ops:
  0.6 0.5 %collective-permute-start = (s32[32,512]{1,0:T(8,128)}, s32[32,512]{1,0:T(8,128)S(1)}, u32[]{:S(2)}, u32[]{:S(2)}) collective-permute-start(s32[32,512]{1,0:T(8,128)} %refs_5_.1), channel_id=1, source_target_pairs={{0,1},{1,0},{2,3},{3,2},{4,5},{5,4},{6,7},{7,6},{8,9},{9,8},{10,11... | collective-permute-start | bytes 196616 | tf_op jit(solution)/shard_map/ppermute | solution.py:417
  1.2 1.3 %fetch.1 = (bf16[512,128]{1,0:T(8,128)(2,1)S(1)}, s32[32,512]{1,0:T(8,128)S(1)}, f32[8,512]{1,0:T(8,128)S(1)}, f32[3,16,128]{2,1,0:T(8,128)S(1)}, bf16[2,384,512]{2,1,0:T(8,128)(2,1)S(1)}) custom-call(bf16[512,128]{1,0:T(8,128)(2,1)} %refs_0_.1, bf16[512]{0:T(512)(128)(2,1)} %refs_1_.1, s32[3,512]{1,0:T(4,128)} %refs_2_.1, s32[14]{0:T(128)} %refs_3_.1, ...), custom_call_target="tpu_custom_call" | custom-call | flops 1000000000 | bytes 1000000 | tf_op jit(solution)/shard_map/fetch/pallas_call | solution.py:427
  2.4 0.0 collective-permute-done.refs_5_
  2.5 0.8 %prep.1 = (bf16[136,384]{1,0:T(8,128)(2,1)S(1)}, bf16[136,384]{1,0:T(8,128)(2,1)S(1)}, bf16[136,384]{1,0:T(8,128)(2,1)S(1)}, bf16[136,384]{1,0:T(8,128)(2,1)S(1)}) custom-call(bf16[512,128]{1,0:T(8,128)(2,1)S(1)} %get-tuple-element.24.refs_0_, f32[8,512]{1,0:T(8,128)S(1)} %get-tuple-element.25.refs_1_, f32[3,16,128]{2,1,0:T(8,128)S(1)} %get-tuple-element.26.refs_2_, ...), custom_call_target="tpu_custom_call" | custom-call | tf_op jit(solution)/shard_map/prep/pallas_call | solution.py:450
  3.3 3.8 %collective-permute-start.1 = (bf16[136,384]{1,0:T(8,128)(2,1)S(1)}, bf16[136,384]{1,0:T(8,128)(2,1)S(1)}, u32[]{:S(2)}, u32[]{:S(2)}) collective-permute-start(bf16[136,384]{1,0:T(8,128)(2,1)S(1)} %get-tuple-element.29), channel_id=1, source_target_pairs={{0,16},{1,13},{2,18},{3,15},{4,20},{5,17},{6,22},{7,19},{8,24},{9,... | collective-permute-start | bytes 313352 | tf_op jit(solution)/shard_map/ppermute | solution.py:69
  7.1 1.6 %collective-permute-start.2 = (bf16[136,384]{1,0:T(8,128)(2,1)S(1)}, bf16[136,384]{1,0:T(8,128)(2,1)S(1)}, u32[]{:S(2)}, u32[]{:S(2)}) collective-permute-start(bf16[136,384]{1,0:T(8,128)(2,1)S(1)} %get-tuple-element.30), channel_id=1, source_target_pairs={{0,8},{1,21},{2,10},{3,23},{4,12},{5,25},{6,14},{7,27},{8,16},{9,2... | collective-permute-start | bytes 313352 | tf_op jit(solution)/shard_map/ppermute | solution.py:69
  8.6 2.2 %collective-permute-start.3 = (bf16[136,384]{1,0:T(8,128)(2,1)S(1)}, bf16[136,384]{1,0:T(8,128)(2,1)S(1)}, u32[]{:S(2)}, u32[]{:S(2)}) collective-permute-start(bf16[136,384]{1,0:T(8,128)(2,1)S(1)} %get-tuple-element.31), channel_id=1, source_target_pairs={{0,24},{1,5},{2,26},{3,7},{4,28},{5,9},{6,30},{7,11},{8,0},{9,13},... | collective-permute-start | bytes 313352 | tf_op jit(solution)/shard_map/ppermute | solution.py:69
  10.9 0.7 %collective-permute-start.4 = (bf16[136,384]{1,0:T(8,128)(2,1)S(1)}, bf16[136,384]{1,0:T(8,128)(2,1)S(1)}, u32[]{:S(2)}, u32[]{:S(2)}) collective-permute-start(bf16[136,384]{1,0:T(8,128)(2,1)S(1)} %get-tuple-element.32), channel_id=1, source_target_pairs={{0,0},{1,29},{2,2},{3,31},{4,4},{5,1},{6,6},{7,3},{8,8},{9,5},{10,... | collective-permute-start | bytes 313352 | tf_op jit(solution)/shard_map/ppermute | solution.py:69
  11.6 0.0 collective-permute-done.1.refs_0_
  11.6 3.0 %collective-permute-done.2.refs_1_ = bf16[136,384]{1,0:T(8,128)(2,1)S(1)} collective-permute-done((bf16[136,384]{1,0:T(8,128)(2,1)S(1)}, bf16[136,384]{1,0:T(8,128)(2,1)S(1)}, u32[]{:S(2)}, u32[]{:S(2)}) %collective-permute-start.2) | collective-permute-done | bytes 104480 | tf_op jit(solution)/shard_map/ppermute | solution.py:69
  14.6 0.0 collective-permute-done.3.refs_2_
  14.6 0.0 collective-permute-done.4.refs_3_
  14.6 2.0 %collective-permute-start.5 = (bf16[4,104,384]{2,1,0:T(8,128)(2,1)S(1)}, bf16[4,104,384]{2,1,0:T(8,128)(2,1)S(1)}, u32[]{:S(2)}, u32[]{:S(2)}) collective-permute-start(bf16[4,104,384]{2,1,0:T(8,128)(2,1)S(1)} %get-tuple-element.33), channel_id=1, source_target_pairs={{0,1},{1,0},{2,3},{3,2},{4,5},{5,4},{6,7},{7,6},{8,9},{9,8},{10,11... | collective-permute-start | bytes 958472 | tf_op jit(solution)/shard_map/ppermute | solution.py:417
  16.6 1.5 %collective-permute-start.6 = (f32[8,128]{1,0:T(8,128)S(1)}, f32[8,128]{1,0:T(8,128)S(1)}, u32[]{:S(2)}, u32[]{:S(2)}) collective-permute-start(f32[8,128]{1,0:T(8,128)S(1)} %get-tuple-element.38), channel_id=1, source_target_pairs={{0,2},{1,3},{2,0},{3,1},{4,6},{5,7},{6,4},{7,5},{8,10},{9,11},{10,... | collective-permute-start | bytes 12296 | tf_op jit(solution)/shard_map/ppermute | solution.py:417
  18.1 0.0 collective-permute-done.5.refs_4_
  18.1 4.4 %gains.1 = (f32[40,128]{1,0:T(8,128)S(1)}, f32[40,128]{1,0:T(8,128)S(1)}, f32[40,128]{1,0:T(8,128)S(1)}, f32[40,128]{1,0:T(8,128)S(1)}) custom-call(bf16[136,384]{1,0:T(8,128)(2,1)S(1)} %collective-permute-done.1.refs_0_, bf16[136,384]{1,0:T(8,128)(2,1)S(1)} %collective-permute-done.2.refs_1_, bf16[136,384]{1,0:T(8,128)(2,1)S(1)} %collective-permute-done.3.refs_2_, ...), custom_call_target="tpu_custom_call" | custom-call | flops 3422552064 | bytes 1671168 | tf_op jit(solution)/shard_map/gains/pallas_call | solution.py:488
  22.5 0.0 collective-permute-done.6
  22.5 1.8 %collective-permute-start.7 = (f32[40,128]{1,0:T(8,128)S(1)}, f32[40,128]{1,0:T(8,128)S(1)}, u32[]{:S(2)}, u32[]{:S(2)}) collective-permute-start(f32[40,128]{1,0:T(8,128)S(1)} %get-tuple-element.40), channel_id=1, source_target_pairs={{0,4},{4,8},{8,12},{12,0},{16,20},{20,24},{24,28},{28,16},{1,5},{5... | collective-permute-start | bytes 61448 | tf_op jit(solution)/shard_map/ppermute | solution.py:56
  24.3 1.5 %collective-permute-start.8 = (f32[40,128]{1,0:T(8,128)S(1)}, f32[40,128]{1,0:T(8,128)S(1)}, u32[]{:S(2)}, u32[]{:S(2)}) collective-permute-start(f32[40,128]{1,0:T(8,128)S(1)} %get-tuple-element.41), channel_id=1, source_target_pairs={{0,8},{4,12},{8,0},{12,4},{16,24},{20,28},{24,16},{28,20},{1,9},{5... | collective-permute-start | bytes 61448 | tf_op jit(solution)/shard_map/ppermute | solution.py:56
  25.8 1.3 %collective-permute-start.9 = (f32[40,128]{1,0:T(8,128)S(1)}, f32[40,128]{1,0:T(8,128)S(1)}, u32[]{:S(2)}, u32[]{:S(2)}) collective-permute-start(f32[40,128]{1,0:T(8,128)S(1)} %get-tuple-element.42), channel_id=1, source_target_pairs={{0,12},{4,0},{8,4},{12,8},{16,28},{20,16},{24,20},{28,24},{1,13},{... | collective-permute-start | bytes 61448 | tf_op jit(solution)/shard_map/ppermute | solution.py:56
  27.1 0.0 collective-permute-start.10
  27.1 1.2 %collective-permute-done.10.refs_5_ = f32[8,128]{1,0:T(8,128)S(1)} collective-permute-done((f32[8,128]{1,0:T(8,128)S(1)}, f32[8,128]{1,0:T(8,128)S(1)}, u32[]{:S(2)}, u32[]{:S(2)}) %collective-permute-start.10) | collective-permute-done | bytes 4128 | tf_op jit(solution)/shard_map/ppermute | solution.py:417
  28.3 0.0 collective-permute-done.7.refs_1_
  28.3 0.0 collective-permute-done.8.refs_2_
  28.3 1.3 %collective-permute-done.9.refs_3_ = f32[40,128]{1,0:T(8,128)S(1)} collective-permute-done((f32[40,128]{1,0:T(8,128)S(1)}, f32[40,128]{1,0:T(8,128)S(1)}, u32[]{:S(2)}, u32[]{:S(2)}) %collective-permute-start.9) | collective-permute-done | bytes 20512 | tf_op jit(solution)/shard_map/ppermute | solution.py:56
  29.6 0.7 %finish.1 = (f32[16,64]{1,0:T(8,128)}, f32[32,64]{1,0:T(8,128)}, f32[64,64]{1,0:T(8,128)}, f32[3,1,2,128]{3,2,1,0:T(2,128)}) custom-call(f32[40,128]{1,0:T(8,128)S(1)} %get-tuple-element.39.refs_0_, f32[40,128]{1,0:T(8,128)S(1)} %collective-permute-done.7.refs_1_, f32[40,128]{1,0:T(8,128)S(1)} %collective-permute-done.8.refs_2_, ...), custom_call_target="tpu_custom_call" | custom-call | tf_op jit(solution)/shard_map/finish/pallas_call | solution.py:519
  (2 shorter events, 0.0 us)
Async XLA Ops:
  0.6 1.8 %collective-permute-start = (s32[32,512]{1,0:T(8,128)}, s32[32,512]{1,0:T(8,128)S(1)}, u32[]{:S(2)}, u32[]{:S(2)}) collective-permute-start(s32[32,512]{1,0:T(8,128)} %refs_5_.1), channel_id=1, source_target_pairs={{0,1},{1,0},{2,3},{3,2},{4,5},{5,4},{6,7},{7,6},{8,9},{9,8},{10,11... | collective-permute-start | bytes 196616 | tf_op jit(solution)/shard_map/ppermute | solution.py:417
  3.3 8.3 %collective-permute-start.1 = (bf16[136,384]{1,0:T(8,128)(2,1)S(1)}, bf16[136,384]{1,0:T(8,128)(2,1)S(1)}, u32[]{:S(2)}, u32[]{:S(2)}) collective-permute-start(bf16[136,384]{1,0:T(8,128)(2,1)S(1)} %get-tuple-element.29), channel_id=1, source_target_pairs={{0,16},{1,13},{2,18},{3,15},{4,20},{5,17},{6,22},{7,19},{8,24},{9,... | collective-permute-start | bytes 313352 | tf_op jit(solution)/shard_map/ppermute | solution.py:69
  7.1 7.5 %collective-permute-start.2 = (bf16[136,384]{1,0:T(8,128)(2,1)S(1)}, bf16[136,384]{1,0:T(8,128)(2,1)S(1)}, u32[]{:S(2)}, u32[]{:S(2)}) collective-permute-start(bf16[136,384]{1,0:T(8,128)(2,1)S(1)} %get-tuple-element.30), channel_id=1, source_target_pairs={{0,8},{1,21},{2,10},{3,23},{4,12},{5,25},{6,14},{7,27},{8,16},{9,2... | collective-permute-start | bytes 313352 | tf_op jit(solution)/shard_map/ppermute | solution.py:69
  8.6 5.9 %collective-permute-start.3 = (bf16[136,384]{1,0:T(8,128)(2,1)S(1)}, bf16[136,384]{1,0:T(8,128)(2,1)S(1)}, u32[]{:S(2)}, u32[]{:S(2)}) collective-permute-start(bf16[136,384]{1,0:T(8,128)(2,1)S(1)} %get-tuple-element.31), channel_id=1, source_target_pairs={{0,24},{1,5},{2,26},{3,7},{4,28},{5,9},{6,30},{7,11},{8,0},{9,13},... | collective-permute-start | bytes 313352 | tf_op jit(solution)/shard_map/ppermute | solution.py:69
  10.9 3.7 %collective-permute-start.4 = (bf16[136,384]{1,0:T(8,128)(2,1)S(1)}, bf16[136,384]{1,0:T(8,128)(2,1)S(1)}, u32[]{:S(2)}, u32[]{:S(2)}) collective-permute-start(bf16[136,384]{1,0:T(8,128)(2,1)S(1)} %get-tuple-element.32), channel_id=1, source_target_pairs={{0,0},{1,29},{2,2},{3,31},{4,4},{5,1},{6,6},{7,3},{8,8},{9,5},{10,... | collective-permute-start | bytes 313352 | tf_op jit(solution)/shard_map/ppermute | solution.py:69
  14.6 3.5 %collective-permute-start.5 = (bf16[4,104,384]{2,1,0:T(8,128)(2,1)S(1)}, bf16[4,104,384]{2,1,0:T(8,128)(2,1)S(1)}, u32[]{:S(2)}, u32[]{:S(2)}) collective-permute-start(bf16[4,104,384]{2,1,0:T(8,128)(2,1)S(1)} %get-tuple-element.33), channel_id=1, source_target_pairs={{0,1},{1,0},{2,3},{3,2},{4,5},{5,4},{6,7},{7,6},{8,9},{9,8},{10,11... | collective-permute-start | bytes 958472 | tf_op jit(solution)/shard_map/ppermute | solution.py:417
  16.6 5.9 %collective-permute-start.6 = (f32[8,128]{1,0:T(8,128)S(1)}, f32[8,128]{1,0:T(8,128)S(1)}, u32[]{:S(2)}, u32[]{:S(2)}) collective-permute-start(f32[8,128]{1,0:T(8,128)S(1)} %get-tuple-element.38), channel_id=1, source_target_pairs={{0,2},{1,3},{2,0},{3,1},{4,6},{5,7},{6,4},{7,5},{8,10},{9,11},{10,... | collective-permute-start | bytes 12296 | tf_op jit(solution)/shard_map/ppermute | solution.py:417
  22.5 5.8 %collective-permute-start.7 = (f32[40,128]{1,0:T(8,128)S(1)}, f32[40,128]{1,0:T(8,128)S(1)}, u32[]{:S(2)}, u32[]{:S(2)}) collective-permute-start(f32[40,128]{1,0:T(8,128)S(1)} %get-tuple-element.40), channel_id=1, source_target_pairs={{0,4},{4,8},{8,12},{12,0},{16,20},{20,24},{24,28},{28,16},{1,5},{5... | collective-permute-start | bytes 61448 | tf_op jit(solution)/shard_map/ppermute | solution.py:56
  24.3 4.0 %collective-permute-start.8 = (f32[40,128]{1,0:T(8,128)S(1)}, f32[40,128]{1,0:T(8,128)S(1)}, u32[]{:S(2)}, u32[]{:S(2)}) collective-permute-start(f32[40,128]{1,0:T(8,128)S(1)} %get-tuple-element.41), channel_id=1, source_target_pairs={{0,8},{4,12},{8,0},{12,4},{16,24},{20,28},{24,16},{28,20},{1,9},{5... | collective-permute-start | bytes 61448 | tf_op jit(solution)/shard_map/ppermute | solution.py:56
  25.8 3.8 %collective-permute-start.9 = (f32[40,128]{1,0:T(8,128)S(1)}, f32[40,128]{1,0:T(8,128)S(1)}, u32[]{:S(2)}, u32[]{:S(2)}) collective-permute-start(f32[40,128]{1,0:T(8,128)S(1)} %get-tuple-element.42), channel_id=1, source_target_pairs={{0,12},{4,0},{8,4},{12,8},{16,28},{20,16},{24,20},{28,24},{1,13},{... | collective-permute-start | bytes 61448 | tf_op jit(solution)/shard_map/ppermute | solution.py:56
  27.1 1.2 %collective-permute-start.10 = (f32[8,128]{1,0:T(8,128)S(1)}, f32[8,128]{1,0:T(8,128)S(1)}, u32[]{:S(2)}, u32[]{:S(2)}) collective-permute-start(f32[8,128]{1,0:T(8,128)S(1)} %add.3.refs_4_), channel_id=1, source_target_pairs={{0,1},{1,0},{2,3},{3,2},{4,5},{5,4},{6,7},{7,6},{8,9},{9,8},{10,11... | collective-permute-start | bytes 12296 | tf_op jit(solution)/shard_map/ppermute | solution.py:417

commit v12 on v10

--- a/solution.py
+++ b/solution.py
@@ -103,7 +103,7 @@
         self.returned = [self.feats // size for size in self.sizes]
         self.needed = [min(self.share, count) for count in self.returned]
         self.block = min(self.needed)
-        self.step = min(8, self.share)
+        self.step = min(16, self.share)
         self.tiles = [
             (start + k, start + k + self.block // 2)
             for start in range(0, self.share, self.block)

time: 30.4 us -> 30.4 us (level)
  no operation moved by 1% of the time
where the time goes in v12:
time: 30.4 us; the launch traced here: 30.2 us
  starting transfers between devices  16.8 us (55%)
  Pallas kernels  7.3 us (24%)
  waiting for transfers between devices  5.41 us (18%)
  between operations  0.69 us (2%)
    ppermute x4, starting transfers between devices, spread(): moved.append(lax.ppermute(block, ('rows', 'feat'), route))  8.13 us
    ppermute x3, starting transfers between devices, exchanged(): moved.append(lax.ppermute(blocks[slot], 'rows', route))  4.55 us
    pallas_call x1, Pallas kernels, on_device(): pl.pallas_call(functools.partial(main_kernel, plan, chunk), out_shape=[ja...  4.38 us
    ppermute x4, starting transfers between devices, flipped(): return lax.ppermute(block, 'feat', [(p, p ^ bits) for p in range(count)])  4.14 us
    ppermute x4, waiting for transfers between devices, spread(): moved.append(lax.ppermute(block, ('rows', 'feat'), route))  3.07 us
    pallas_call x1, Pallas kernels, on_device(): pl.pallas_call(functools.partial(fetch_kernel, plan), out_shape=(jax.Shap...  1.57 us
    ppermute x3, waiting for transfers between devices, exchanged(): moved.append(lax.ppermute(blocks[slot], 'rows', route))  1.17 us
    ppermute x4, waiting for transfers between devices, flipped(): return lax.ppermute(block, 'feat', [(p, p ^ bits) for p in range(count)])  1.17 us
  transfers between devices with their start and end apart: 11, of which 4 were waited for; matrix products, arithmetic and copies ran while one was open for 0% of the time, Pallas kernels for 20%

profile of v12, /device:TPU:0, one launch (start us, length us, event | category | flops | bytes accessed | tf_op | source)
XLA Modules:
  0.0 30.2 jit_solution(3069924989657856322)
XLA Ops:
  0.6 0.5 %collective-permute-start = (s32[32,512]{1,0:T(8,128)}, s32[32,512]{1,0:T(8,128)S(1)}, u32[]{:S(2)}, u32[]{:S(2)}) collective-permute-start(s32[32,512]{1,0:T(8,128)} %refs_5_.1), channel_id=1, source_target_pairs={{0,1},{1,0},{2,3},{3,2},{4,5},{5,4},{6,7},{7,6},{8,9},{9,8},{10,11... | collective-permute-start | bytes 196616 | tf_op jit(solution)/shard_map/ppermute | solution.py:421
  1.2 1.6 %fetch.1 = (bf16[512,128]{1,0:T(8,128)(2,1)S(1)}, s32[32,512]{1,0:T(8,128)S(1)}, f32[8,512]{1,0:T(8,128)S(1)}, f32[3,16,128]{2,1,0:T(8,128)S(1)}, bf16[2,384,512...) custom-call(bf16[512,128]{1,0:T(8,128)(2,1)} %refs_0_.1, bf16[512]{0:T(512)(128)(2,1)} %refs_1_.1, s32[3,512]{1,0:T(4,128)} %refs_2_.1, ...), custom_call_target="tpu_custom_call" | custom-call | flops 1000000000 | bytes 1000000 | tf_op jit(solution)/shard_map/fetch/pallas_call | solution.py:431
  2.7 0.0 collective-permute-done.refs_6_
  2.7 0.6 %prep.1 = (bf16[136,384]{1,0:T(8,128)(2,1)S(1)}, bf16[136,384]{1,0:T(8,128)(2,1)S(1)}, bf16[136,384]{1,0:T(8,128)(2,1)S(1)}, bf16[136,384]{1,0:T(8,128)(2,1)S(1)}) custom-call(bf16[512,128]{1,0:T(8,128)(2,1)S(1)} %get-tuple-element.25.refs_0_, f32[8,512]{1,0:T(8,128)S(1)} %get-tuple-element.26.refs_1_, f32[3,16,128]{2,1,0:T(8,128)S(1)} %get-tuple-element.27.refs_2_, ...), custom_call_target="tpu_custom_call" | custom-call | tf_op jit(solution)/shard_map/prep/pallas_call | solution.py:456
  3.3 3.7 %collective-permute-start.1 = (bf16[136,384]{1,0:T(8,128)(2,1)S(1)}, bf16[136,384]{1,0:T(8,128)(2,1)S(1)}, u32[]{:S(2)}, u32[]{:S(2)}) collective-permute-start(bf16[136,384]{1,0:T(8,128)(2,1)S(1)} %get-tuple-element.31), channel_id=1, source_target_pairs={{0,16},{1,13},{2,18},{3,15},{4,20},{5,17},{6,22},{7,19},{8,24},{9,... | collective-permute-start | bytes 313352 | tf_op jit(solution)/shard_map/ppermute | solution.py:69
  7.0 1.6 %collective-permute-start.2 = (bf16[136,384]{1,0:T(8,128)(2,1)S(1)}, bf16[136,384]{1,0:T(8,128)(2,1)S(1)}, u32[]{:S(2)}, u32[]{:S(2)}) collective-permute-start(bf16[136,384]{1,0:T(8,128)(2,1)S(1)} %get-tuple-element.32), channel_id=1, source_target_pairs={{0,8},{1,21},{2,10},{3,23},{4,12},{5,25},{6,14},{7,27},{8,16},{9,2... | collective-permute-start | bytes 313352 | tf_op jit(solution)/shard_map/ppermute | solution.py:69
  8.6 2.2 %collective-permute-start.3 = (bf16[136,384]{1,0:T(8,128)(2,1)S(1)}, bf16[136,384]{1,0:T(8,128)(2,1)S(1)}, u32[]{:S(2)}, u32[]{:S(2)}) collective-permute-start(bf16[136,384]{1,0:T(8,128)(2,1)S(1)} %get-tuple-element.33), channel_id=1, source_target_pairs={{0,24},{1,5},{2,26},{3,7},{4,28},{5,9},{6,30},{7,11},{8,0},{9,13},... | collective-permute-start | bytes 313352 | tf_op jit(solution)/shard_map/ppermute | solution.py:69
  10.8 0.7 %collective-permute-start.4 = (bf16[136,384]{1,0:T(8,128)(2,1)S(1)}, bf16[136,384]{1,0:T(8,128)(2,1)S(1)}, u32[]{:S(2)}, u32[]{:S(2)}) collective-permute-start(bf16[136,384]{1,0:T(8,128)(2,1)S(1)} %get-tuple-element.34), channel_id=1, source_target_pairs={{0,0},{1,29},{2,2},{3,31},{4,4},{5,1},{6,6},{7,3},{8,8},{9,5},{10,... | collective-permute-start | bytes 313352 | tf_op jit(solution)/shard_map/ppermute | solution.py:69
  11.5 0.0 collective-permute-done.1.refs_0_
  11.5 2.8 %collective-permute-done.2.refs_1_ = bf16[136,384]{1,0:T(8,128)(2,1)S(1)} collective-permute-done((bf16[136,384]{1,0:T(8,128)(2,1)S(1)}, bf16[136,384]{1,0:T(8,128)(2,1)S(1)}, u32[]{:S(2)}, u32[]{:S(2)}) %collective-permute-start.2) | collective-permute-done | bytes 104480 | tf_op jit(solution)/shard_map/ppermute | solution.py:69
  14.3 0.2 collective-permute-done.3.refs_2_
  14.5 0.0 collective-permute-done.4.refs_3_
  14.6 2.1 %collective-permute-start.5 = (bf16[4,104,384]{2,1,0:T(8,128)(2,1)S(1)}, bf16[4,104,384]{2,1,0:T(8,128)(2,1)S(1)}, u32[]{:S(2)}, u32[]{:S(2)}) collective-permute-start(bf16[4,104,384]{2,1,0:T(8,128)(2,1)S(1)} %get-tuple-element.35), channel_id=1, source_target_pairs={{0,1},{1,0},{2,3},{3,2},{4,5},{5,4},{6,7},{7,6},{8,9},{9,8},{10,11... | collective-permute-start | bytes 958472 | tf_op jit(solution)/shard_map/ppermute | solution.py:421
  16.7 1.5 %collective-permute-start.6 = (f32[8,128]{1,0:T(8,128)S(1)}, f32[8,128]{1,0:T(8,128)S(1)}, u32[]{:S(2)}, u32[]{:S(2)}) collective-permute-start(f32[8,128]{1,0:T(8,128)S(1)} %get-tuple-element.40), channel_id=1, source_target_pairs={{0,2},{1,3},{2,0},{3,1},{4,6},{5,7},{6,4},{7,5},{8,10},{9,11},{10,... | collective-permute-start | bytes 12296 | tf_op jit(solution)/shard_map/ppermute | solution.py:421
  18.2 0.0 collective-permute-done.5.refs_4_
  18.2 4.4 %gains.1 = (f32[40,128]{1,0:T(8,128)S(1)}, f32[40,128]{1,0:T(8,128)S(1)}, f32[40,128]{1,0:T(8,128)S(1)}, f32[40,128]{1,0:T(8,128)S(1)}) custom-call(bf16[136,384]{1,0:T(8,128)(2,1)S(1)} %collective-permute-done.1.refs_0_, bf16[136,384]{1,0:T(8,128)(2,1)S(1)} %collective-permute-done.2.refs_1_, bf16[136,384]{1,0:T(8,128)(2,1)S(1)} %collective-permute-done.3.refs_2_, ...), custom_call_target="tpu_custom_call" | custom-call | flops 3422552064 | bytes 1671168 | tf_op jit(solution)/shard_map/gains/pallas_call | solution.py:494
  22.6 0.0 collective-permute-done.6
  22.6 1.6 %collective-permute-start.7 = (f32[40,128]{1,0:T(8,128)S(1)}, f32[40,128]{1,0:T(8,128)S(1)}, u32[]{:S(2)}, u32[]{:S(2)}) collective-permute-start(f32[40,128]{1,0:T(8,128)S(1)} %get-tuple-element.42), channel_id=1, source_target_pairs={{0,4},{4,8},{8,12},{12,0},{16,20},{20,24},{24,28},{28,16},{1,5},{5... | collective-permute-start | bytes 61448 | tf_op jit(solution)/shard_map/ppermute | solution.py:56
  24.3 1.5 %collective-permute-start.8 = (f32[40,128]{1,0:T(8,128)S(1)}, f32[40,128]{1,0:T(8,128)S(1)}, u32[]{:S(2)}, u32[]{:S(2)}) collective-permute-start(f32[40,128]{1,0:T(8,128)S(1)} %get-tuple-element.43), channel_id=1, source_target_pairs={{0,8},{4,12},{8,0},{12,4},{16,24},{20,28},{24,16},{28,20},{1,9},{5... | collective-permute-start | bytes 61448 | tf_op jit(solution)/shard_map/ppermute | solution.py:56
  25.7 1.4 %collective-permute-start.9 = (f32[40,128]{1,0:T(8,128)S(1)}, f32[40,128]{1,0:T(8,128)S(1)}, u32[]{:S(2)}, u32[]{:S(2)}) collective-permute-start(f32[40,128]{1,0:T(8,128)S(1)} %get-tuple-element.44), channel_id=1, source_target_pairs={{0,12},{4,0},{8,4},{12,8},{16,28},{20,16},{24,20},{28,24},{1,13},{... | collective-permute-start | bytes 61448 | tf_op jit(solution)/shard_map/ppermute | solution.py:56
  27.2 0.0 collective-permute-start.10
  27.2 1.2 %collective-permute-done.10.refs_5_ = f32[8,128]{1,0:T(8,128)S(1)} collective-permute-done((f32[8,128]{1,0:T(8,128)S(1)}, f32[8,128]{1,0:T(8,128)S(1)}, u32[]{:S(2)}, u32[]{:S(2)}) %collective-permute-start.10) | collective-permute-done | bytes 4128 | tf_op jit(solution)/shard_map/ppermute | solution.py:421
  28.3 0.0 collective-permute-done.7.refs_1_
  28.3 0.0 collective-permute-done.8.refs_2_
  28.3 1.2 %collective-permute-done.9.refs_3_ = f32[40,128]{1,0:T(8,128)S(1)} collective-permute-done((f32[40,128]{1,0:T(8,128)S(1)}, f32[40,128]{1,0:T(8,128)S(1)}, u32[]{:S(2)}, u32[]{:S(2)}) %collective-permute-start.9) | collective-permute-done | bytes 20512 | tf_op jit(solution)/shard_map/ppermute | solution.py:56
  29.5 0.7 %finish.1 = (f32[16,64]{1,0:T(8,128)}, f32[32,64]{1,0:T(8,128)}, f32[64,64]{1,0:T(8,128)}, f32[3,1,2,128]{3,2,1,0:T(2,128)}) custom-call(f32[40,128]{1,0:T(8,128)S(1)} %get-tuple-element.41.refs_0_, f32[40,128]{1,0:T(8,128)S(1)} %collective-permute-done.7.refs_1_, f32[40,128]{1,0:T(8,128)S(1)} %collective-permute-done.8.refs_2_, ...), custom_call_target="tpu_custom_call" | custom-call | tf_op jit(solution)/shard_map/finish/pallas_call | solution.py:525
  (2 shorter events, 0.0 us)
Async XLA Ops:
  0.6 2.1 %collective-permute-start = (s32[32,512]{1,0:T(8,128)}, s32[32,512]{1,0:T(8,128)S(1)}, u32[]{:S(2)}, u32[]{:S(2)}) collective-permute-start(s32[32,512]{1,0:T(8,128)} %refs_5_.1), channel_id=1, source_target_pairs={{0,1},{1,0},{2,3},{3,2},{4,5},{5,4},{6,7},{7,6},{8,9},{9,8},{10,11... | collective-permute-start | bytes 196616 | tf_op jit(solution)/shard_map/ppermute | solution.py:421
  3.3 8.1 %collective-permute-start.1 = (bf16[136,384]{1,0:T(8,128)(2,1)S(1)}, bf16[136,384]{1,0:T(8,128)(2,1)S(1)}, u32[]{:S(2)}, u32[]{:S(2)}) collective-permute-start(bf16[136,384]{1,0:T(8,128)(2,1)S(1)} %get-tuple-element.31), channel_id=1, source_target_pairs={{0,16},{1,13},{2,18},{3,15},{4,20},{5,17},{6,22},{7,19},{8,24},{9,... | collective-permute-start | bytes 313352 | tf_op jit(solution)/shard_map/ppermute | solution.py:69
  7.0 7.3 %collective-permute-start.2 = (bf16[136,384]{1,0:T(8,128)(2,1)S(1)}, bf16[136,384]{1,0:T(8,128)(2,1)S(1)}, u32[]{:S(2)}, u32[]{:S(2)}) collective-permute-start(bf16[136,384]{1,0:T(8,128)(2,1)S(1)} %get-tuple-element.32), channel_id=1, source_target_pairs={{0,8},{1,21},{2,10},{3,23},{4,12},{5,25},{6,14},{7,27},{8,16},{9,2... | collective-permute-start | bytes 313352 | tf_op jit(solution)/shard_map/ppermute | solution.py:69
  8.6 6.0 %collective-permute-start.3 = (bf16[136,384]{1,0:T(8,128)(2,1)S(1)}, bf16[136,384]{1,0:T(8,128)(2,1)S(1)}, u32[]{:S(2)}, u32[]{:S(2)}) collective-permute-start(bf16[136,384]{1,0:T(8,128)(2,1)S(1)} %get-tuple-element.33), channel_id=1, source_target_pairs={{0,24},{1,5},{2,26},{3,7},{4,28},{5,9},{6,30},{7,11},{8,0},{9,13},... | collective-permute-start | bytes 313352 | tf_op jit(solution)/shard_map/ppermute | solution.py:69
  10.8 3.7 %collective-permute-start.4 = (bf16[136,384]{1,0:T(8,128)(2,1)S(1)}, bf16[136,384]{1,0:T(8,128)(2,1)S(1)}, u32[]{:S(2)}, u32[]{:S(2)}) collective-permute-start(bf16[136,384]{1,0:T(8,128)(2,1)S(1)} %get-tuple-element.34), channel_id=1, source_target_pairs={{0,0},{1,29},{2,2},{3,31},{4,4},{5,1},{6,6},{7,3},{8,8},{9,5},{10,... | collective-permute-start | bytes 313352 | tf_op jit(solution)/shard_map/ppermute | solution.py:69
  14.6 3.6 %collective-permute-start.5 = (bf16[4,104,384]{2,1,0:T(8,128)(2,1)S(1)}, bf16[4,104,384]{2,1,0:T(8,128)(2,1)S(1)}, u32[]{:S(2)}, u32[]{:S(2)}) collective-permute-start(bf16[4,104,384]{2,1,0:T(8,128)(2,1)S(1)} %get-tuple-element.35), channel_id=1, source_target_pairs={{0,1},{1,0},{2,3},{3,2},{4,5},{5,4},{6,7},{7,6},{8,9},{9,8},{10,11... | collective-permute-start | bytes 958472 | tf_op jit(solution)/shard_map/ppermute | solution.py:421
  16.7 5.9 %collective-permute-start.6 = (f32[8,128]{1,0:T(8,128)S(1)}, f32[8,128]{1,0:T(8,128)S(1)}, u32[]{:S(2)}, u32[]{:S(2)}) collective-permute-start(f32[8,128]{1,0:T(8,128)S(1)} %get-tuple-element.40), channel_id=1, source_target_pairs={{0,2},{1,3},{2,0},{3,1},{4,6},{5,7},{6,4},{7,5},{8,10},{9,11},{10,... | collective-permute-start | bytes 12296 | tf_op jit(solution)/shard_map/ppermute | solution.py:421
  22.6 5.7 %collective-permute-start.7 = (f32[40,128]{1,0:T(8,128)S(1)}, f32[40,128]{1,0:T(8,128)S(1)}, u32[]{:S(2)}, u32[]{:S(2)}) collective-permute-start(f32[40,128]{1,0:T(8,128)S(1)} %get-tuple-element.42), channel_id=1, source_target_pairs={{0,4},{4,8},{8,12},{12,0},{16,20},{20,24},{24,28},{28,16},{1,5},{5... | collective-permute-start | bytes 61448 | tf_op jit(solution)/shard_map/ppermute | solution.py:56
  24.3 4.1 %collective-permute-start.8 = (f32[40,128]{1,0:T(8,128)S(1)}, f32[40,128]{1,0:T(8,128)S(1)}, u32[]{:S(2)}, u32[]{:S(2)}) collective-permute-start(f32[40,128]{1,0:T(8,128)S(1)} %get-tuple-element.43), channel_id=1, source_target_pairs={{0,8},{4,12},{8,0},{12,4},{16,24},{20,28},{24,16},{28,20},{1,9},{5... | collective-permute-start | bytes 61448 | tf_op jit(solution)/shard_map/ppermute | solution.py:56
  25.7 3.8 %collective-permute-start.9 = (f32[40,128]{1,0:T(8,128)S(1)}, f32[40,128]{1,0:T(8,128)S(1)}, u32[]{:S(2)}, u32[]{:S(2)}) collective-permute-start(f32[40,128]{1,0:T(8,128)S(1)} %get-tuple-element.44), channel_id=1, source_target_pairs={{0,12},{4,0},{8,4},{12,8},{16,28},{20,16},{24,20},{28,24},{1,13},{... | collective-permute-start | bytes 61448 | tf_op jit(solution)/shard_map/ppermute | solution.py:56
  27.2 1.2 %collective-permute-start.10 = (f32[8,128]{1,0:T(8,128)S(1)}, f32[8,128]{1,0:T(8,128)S(1)}, u32[]{:S(2)}, u32[]{:S(2)}) collective-permute-start(f32[8,128]{1,0:T(8,128)S(1)} %add.3.refs_4_), channel_id=1, source_target_pairs={{0,1},{1,0},{2,3},{3,2},{4,5},{5,4},{6,7},{7,6},{8,9},{9,8},{10,11... | collective-permute-start | bytes 12296 | tf_op jit(solution)/shard_map/ppermute | solution.py:421
